TPU v7x, 128 devices: a whole 4x4x4 slice. The times are simulated.
128 devices in a mesh: tensor: 2 (over y_lo), dp: 4 (over y_hi, core), seq: 16 (over z, x).
Axes of the slice: x: 4, y: 4 (y_hi: 2, y_lo: 2; y = y_hi * 2 + y_lo), z: 4, core: 2. Of those that a mesh axis runs over, the one named last changes fastest.
Arguments:
- inputs: bfloat16 [4, 2048, 1024], P('dp', 'seq'), may hold values from -6 to 6
- cotangent: bfloat16 [4, 2048, 1024], P('dp', 'seq'), may hold values from -6 to 6
- norm_mix: bfloat16 [1024], replicated, may hold values from 0.5 to 1.5
- w_query: bfloat16 [1024, 1024], P(None, 'tensor'), may hold values from -0.1875 to 0.1875
- w_key: bfloat16 [1024, 1024], P(None, 'tensor'), may hold values from -0.1875 to 0.1875
- w_value: bfloat16 [1024, 2048], P(None, 'tensor'), may hold values from -0.1875 to 0.1875
- w_outgate: bfloat16 [1024, 2048], P(None, 'tensor'), may hold values from -0.1875 to 0.1875
- w_beta: bfloat16 [1024, 8], P(None, 'tensor'), may hold values from -0.1875 to 0.1875
- w_decay: bfloat16 [1024, 8], P(None, 'tensor'), may hold values from -0.1875 to 0.1875
- decay_log: bfloat16 [8], P('tensor'), may hold values from 0 to 1
- decay_bias: bfloat16 [8], P('tensor'), may hold values from -8 to -4
- conv_query: bfloat16 [1024, 4], P('tensor'), may hold values from -3 to 3
- conv_key: bfloat16 [1024, 4], P('tensor'), may hold values from -3 to 3
- conv_value: bfloat16 [2048, 4], P('tensor'), may hold values from -3 to 3
- out_gain: bfloat16 [256], replicated, may hold values from 0.5 to 1.5
- w_out: bfloat16 [2048, 1024], P('tensor'), may hold values from -0.125 to 0.125
- norm_ffn: bfloat16 [1024], replicated, may hold values from 0.5 to 1.5
- w_gate: bfloat16 [1024, 2816], P(None, 'tensor'), may hold values from -0.1875 to 0.1875
- w_up: bfloat16 [1024, 2816], P(None, 'tensor'), may hold values from -0.1875 to 0.1875
- w_down: bfloat16 [2816, 1024], P('tensor'), may hold values from -0.109375 to 0.109375
Outputs:
- output: bfloat16 [4, 2048, 1024], P('dp', 'seq')
- grad_inputs: bfloat16 [4, 2048, 1024], P('dp', 'seq')
- grad_norm_mix: bfloat16 [1024], P('seq')
- grad_w_query: bfloat16 [1024, 1024], P('seq', 'tensor')
- grad_w_key: bfloat16 [1024, 1024], P('seq', 'tensor')
- grad_w_value: bfloat16 [1024, 2048], P('seq', 'tensor')
- grad_w_outgate: bfloat16 [1024, 2048], P('seq', 'tensor')
- grad_w_beta: bfloat16 [1024, 8], P('seq', 'tensor')
- grad_w_decay: bfloat16 [1024, 8], P('seq', 'tensor')
- grad_decay_log: bfloat16 [8], P('tensor')
- grad_decay_bias: bfloat16 [8], P('tensor')
- grad_conv_query: bfloat16 [1024, 4], P(('tensor', 'seq'))
- grad_conv_key: bfloat16 [1024, 4], P(('tensor', 'seq'))
- grad_conv_value: bfloat16 [2048, 4], P(('tensor', 'seq'))
- grad_out_gain: bfloat16 [256], P('seq')
- grad_w_out: bfloat16 [2048, 1024], P(('tensor', 'seq'))
- grad_norm_ffn: bfloat16 [1024], P('seq')
- grad_w_gate: bfloat16 [1024, 2816], P('seq', 'tensor')
- grad_w_up: bfloat16 [1024, 2816], P('seq', 'tensor')
- grad_w_down: bfloat16 [2816, 1024], P(('tensor', 'seq'))
All inputs are finite; a program needn't handle non-finite values.
Results may differ from a plain program's by a relative error of at most 0.025.
Values may be sent and summed in bfloat16 or wider, within the bound.
No kernel may reach another device: no remote copies, remote signals or barrier semaphores. Data moves between devices by JAX's collectives and lax.ppermute only.
A program may use at most 128 MiB of HBM per device.

v0:
```python
import jax
import jax.numpy as jnp
from jax import lax
from jax.sharding import PartitionSpec as P

GROUP = 64


highest = lax.Precision.HIGHEST
epsilon = 1e-05
smallest = 1e-06


def from_behind(value, axis, steps):
    count = lax.axis_size(axis)
    initial, last = (max(0, -steps), min(count, count - steps))
    return lax.ppermute(value, axis, [(source, source + steps) for source in range(initial, last)])


def product_high(left_op, right_op, form):
    return jnp.einsum(form, left_op, right_op, precision=highest)


def norm_rows(values, scales):
    return values * lax.rsqrt(jnp.mean(values * values, axis=-1, keepdims=True) + epsilon) * scales


def unit_heads(values):
    return values * lax.rsqrt(jnp.sum(values * values, axis=-1, keepdims=True) + smallest)


def conv_rows(extended, filters):
    tap_count = filters.shape[1]
    length = extended.shape[1] - tap_count + 1
    summed = extended[:, 0:length] * filters[:, 0]
    for offset in range(1, tap_count):
        summed = summed + extended[:, offset : offset + length] * filters[:, offset]
    return jax.nn.silu(summed)


def gated_norm(mixed_out, scales, gate_pre):
    normed = mixed_out * lax.rsqrt(
        jnp.mean(mixed_out * mixed_out, axis=-1, keepdims=True) + epsilon
    )
    gated_out = normed * scales * jax.nn.silu(gate_pre)
    return gated_out.reshape(gated_out.shape[0], -1)


def gate_values(beta_logit, decay_pre, decay_log, decay_bias):
    return (
        jax.nn.sigmoid(beta_logit),
        -jnp.exp(decay_log) * jax.nn.softplus(decay_pre + decay_bias),
    )


def swiglu(gate_ffn, up_ffn):
    return jax.nn.silu(gate_ffn) * up_ffn


def to_blocks(values, block_len):
    seq_count, length, heads_here = values.shape[:3]
    trailing = values.shape[3:]
    shaped = values.reshape((seq_count, length // block_len, block_len, heads_here) + trailing)
    axes_order = (1, 0, 3, 2) + tuple(range(4, 4 + len(trailing)))
    return shaped.transpose(axes_order).reshape(
        (length // block_len, seq_count * heads_here, block_len) + trailing
    )


def from_blocks(values, seq_count, heads_here):
    blocks = values.shape[0]
    block_len = values.shape[2]
    trailing = values.shape[3:]
    shaped = values.reshape((blocks, seq_count, heads_here, block_len) + trailing)
    axes_order = (1, 0, 3, 2) + tuple(range(4, 4 + len(trailing)))
    return shaped.transpose(axes_order).reshape(
        (seq_count, blocks * block_len, heads_here) + trailing
    )


def delta_run(queries, keys_in, values, beta_rows, decays, start_state):
    block_len = queries.shape[2]
    places = jnp.arange(block_len)
    inclusive = (places[:, None] >= places[None, :]).astype(jnp.float32)
    strictly = (places[:, None] > places[None, :]).astype(jnp.float32)
    identity = jnp.eye(block_len, dtype=jnp.float32)

    def advance(carried, block_in):
        query_blk, key_blk, value_blk, beta_blk, decay_blk = block_in
        cumulative = jnp.cumsum(decay_blk, axis=-1)
        fading = jnp.exp((cumulative[:, :, None] - cumulative[:, None, :]) * inclusive) * inclusive
        lower_part = (
            strictly
            * fading
            * beta_blk[:, None, :]
            * product_high(key_blk, key_blk, "pcd,ped->pce")
        )
        growth = jnp.exp(cumulative)
        target = value_blk - growth[..., None] * product_high(key_blk, carried, "pcd,pdw->pcw")
        solved = jax.scipy.linalg.solve_triangular(
            identity + lower_part, target, lower=True, unit_diagonal=True
        )
        weighted = beta_blk[..., None] * solved
        scores = product_high(query_blk, key_blk, "pcd,ped->pce") * fading
        output_blk = growth[..., None] * product_high(
            query_blk, carried, "pcd,pdw->pcw"
        ) + product_high(scores, weighted, "pce,pew->pcw")
        last_sum = cumulative[:, -1]
        remains = jnp.exp(last_sum[:, None] - cumulative)
        updated = jnp.exp(last_sum)[:, None, None] * carried + product_high(
            key_blk * remains[..., None], weighted, "pcd,pcw->pdw"
        )
        return (updated, output_blk)

    end_state, outputs = lax.scan(
        advance, start_state, (queries, keys_in, values, beta_rows, decays)
    )
    return (outputs, end_state)


def pass_states(transforms, offsets, direction):

    def turn(turn_index, carried):
        moved_state = product_high(transforms, carried, "pij,pjw->piw") + offsets
        return from_behind(moved_state, "seq", direction)

    return lax.fori_loop(0, lax.axis_size("seq") - 1, turn, jnp.zeros_like(offsets))


def carry_states(transforms, offsets, backward):
    return pass_states(transforms, offsets, -1 if backward else 1)


def per_device(
    inputs,
    cotangent,
    norm_mix,
    w_query,
    w_key,
    w_value,
    w_outgate,
    w_beta,
    w_decay,
    decay_log,
    decay_bias,
    conv_query,
    conv_key,
    conv_value,
    out_gain,
    w_out,
    norm_ffn,
    w_gate,
    w_up,
    w_down,
):
    seq_count, length, model_width = inputs.shape
    row_count = seq_count * length
    heads_here = decay_log.shape[0]
    query_cols = w_query.shape[1]
    key_width = query_cols // heads_here
    value_width = w_value.shape[1] // heads_here
    rim_len = conv_query.shape[1] - 1
    residual = inputs.reshape(row_count, model_width).astype(jnp.float32)
    normed, norm_mix_back = jax.vjp(norm_rows, residual, norm_mix.astype(jnp.float32))
    normed_low = normed.astype(jnp.bfloat16)

    def project(weight):
        return jnp.dot(normed_low, weight, preferred_element_type=jnp.float32)

    mixed_pre = jnp.concatenate(
        [project(w_query), project(w_key), project(w_value)], axis=1
    ).astype(jnp.bfloat16)
    mixed_pre = mixed_pre.reshape(seq_count, length, -1)
    rim_rows = from_behind(mixed_pre[:, length - rim_len :], "seq", 1)
    extended = jnp.concatenate([rim_rows, mixed_pre], axis=1).astype(jnp.float32)
    filters = jnp.concatenate([conv_query, conv_key, conv_value], axis=0).astype(jnp.float32)

    def front(extended_rows, filter_taps):
        activated = conv_rows(extended_rows, filter_taps)
        query_part = activated[..., :query_cols].reshape(seq_count, length, heads_here, key_width)
        key_part = activated[..., query_cols : 2 * query_cols].reshape(
            seq_count, length, heads_here, key_width
        )
        value_part = activated[..., 2 * query_cols :].reshape(
            seq_count, length, heads_here, value_width
        )
        return (unit_heads(query_part) * key_width ** (-0.5), unit_heads(key_part), value_part)

    fronted, front_back = jax.vjp(front, extended, filters)
    lowered = [
        lax.optimization_barrier(low_piece.astype(jnp.bfloat16)).astype(jnp.float32)
        for low_piece in fronted
    ]
    query_blocks = to_blocks(lowered[0], GROUP)
    key_blocks = to_blocks(lowered[1], GROUP)
    value_blocks = to_blocks(lowered[2], GROUP)
    beta_logit = project(w_beta)
    decay_pre = project(w_decay)
    (beta_rows, decays), gate_back = jax.vjp(
        gate_values,
        beta_logit,
        decay_pre,
        decay_log.astype(jnp.float32),
        decay_bias.astype(jnp.float32),
    )
    beta_blocks = to_blocks(beta_rows.reshape(seq_count, length, heads_here), GROUP)
    decay_blocks = to_blocks(decays.reshape(seq_count, length, heads_here), GROUP)
    pair_count = seq_count * heads_here
    start_ext = jnp.concatenate(
        [
            jnp.broadcast_to(
                jnp.eye(key_width, dtype=jnp.float32), (pair_count, key_width, key_width)
            ),
            jnp.zeros((pair_count, key_width, value_width), jnp.float32),
        ],
        axis=2,
    )
    value_ext = jnp.concatenate(
        [jnp.zeros(value_blocks.shape[:3] + (key_width,), jnp.float32), value_blocks], axis=3
    )
    end_maps = delta_run(query_blocks, key_blocks, value_ext, beta_blocks, decay_blocks, start_ext)[
        1
    ]
    transforms = end_maps[..., :key_width]
    offsets = end_maps[..., key_width:]
    start_state = carry_states(transforms, offsets, False)
    (mixed_blocks, end_state), delta_back = jax.vjp(
        delta_run, query_blocks, key_blocks, value_blocks, beta_blocks, decay_blocks, start_state
    )
    mixed_out = from_blocks(mixed_blocks, seq_count, heads_here).reshape(
        row_count, heads_here, value_width
    )
    gate_pre = project(w_outgate).reshape(row_count, heads_here, value_width)
    gated_out, gated_back = jax.vjp(gated_norm, mixed_out, out_gain.astype(jnp.float32), gate_pre)
    gated_low = gated_out.astype(jnp.bfloat16)
    branch = lax.psum(jnp.dot(gated_low, w_out, preferred_element_type=jnp.float32), "tensor")
    middle = residual + branch
    normed_two, norm_ffn_back = jax.vjp(norm_rows, middle, norm_ffn.astype(jnp.float32))
    normed_two_low = normed_two.astype(jnp.bfloat16)
    gate_ffn = jnp.dot(normed_two_low, w_gate, preferred_element_type=jnp.float32)
    up_ffn = jnp.dot(normed_two_low, w_up, preferred_element_type=jnp.float32)
    hidden, swiglu_back = jax.vjp(swiglu, gate_ffn, up_ffn)
    hidden_low = hidden.astype(jnp.bfloat16)
    feed_out = lax.psum(
        jnp.dot(hidden_low, w_down, preferred_element_type=jnp.float32).astype(jnp.bfloat16),
        "tensor",
    ).astype(jnp.float32)
    output = (middle + feed_out).astype(jnp.bfloat16).reshape(seq_count, length, model_width)
    feed_grad = cotangent.reshape(row_count, model_width)
    grad_down = jnp.einsum("rf,rd->fd", hidden_low, feed_grad, preferred_element_type=jnp.float32)
    hidden_grad = jnp.einsum("rd,fd->rf", feed_grad, w_down, preferred_element_type=jnp.float32)
    gate_ffn_grad, up_ffn_grad = swiglu_back(hidden_grad)
    gate_ffn_low = gate_ffn_grad.astype(jnp.bfloat16)
    up_ffn_low = up_ffn_grad.astype(jnp.bfloat16)
    grad_gate = jnp.einsum(
        "rd,rf->df", normed_two_low, gate_ffn_low, preferred_element_type=jnp.float32
    )
    grad_up = jnp.einsum(
        "rd,rf->df", normed_two_low, up_ffn_low, preferred_element_type=jnp.float32
    )
    two_part = jnp.einsum(
        "rf,df->rd", gate_ffn_low, w_gate, preferred_element_type=jnp.float32
    ) + jnp.einsum("rf,df->rd", up_ffn_low, w_up, preferred_element_type=jnp.float32)
    normed_two_grad = lax.psum(two_part.astype(jnp.bfloat16), "tensor").astype(jnp.float32)
    middle_part, grad_norm_ffn = norm_ffn_back(normed_two_grad)
    middle_grad = feed_grad.astype(jnp.float32) + middle_part
    branch_low = middle_grad.astype(jnp.bfloat16)
    grad_wout = jnp.einsum("rz,rd->zd", gated_low, branch_low, preferred_element_type=jnp.float32)
    gated_grad = jnp.einsum("rd,zd->rz", branch_low, w_out, preferred_element_type=jnp.float32)
    mixed_grad, out_gain_grad, gate_pre_grad = gated_back(gated_grad)
    gate_pre_low = gate_pre_grad.reshape(row_count, -1).astype(jnp.bfloat16)
    mixed_grad_blocks = to_blocks(
        mixed_grad.reshape(seq_count, length, heads_here, value_width), GROUP
    )
    start_grad = delta_back((mixed_grad_blocks, jnp.zeros_like(end_state)))[5]
    end_grad = carry_states(jnp.swapaxes(transforms, 1, 2), start_grad, True)
    full_pass = delta_back((mixed_grad_blocks, end_grad))
    query_grad = from_blocks(full_pass[0], seq_count, heads_here)
    key_grad = from_blocks(full_pass[1], seq_count, heads_here)
    value_grad = from_blocks(full_pass[2], seq_count, heads_here)
    beta_grad = from_blocks(full_pass[3], seq_count, heads_here).reshape(row_count, heads_here)
    decay_grad = from_blocks(full_pass[4], seq_count, heads_here).reshape(row_count, heads_here)
    extended_grad, filters_grad = front_back((query_grad, key_grad, value_grad))
    incoming = from_behind(extended_grad[:, :rim_len], "seq", -1)
    local_grad = extended_grad[:, rim_len:]
    local_grad = jnp.concatenate(
        [local_grad[:, : length - rim_len], local_grad[:, length - rim_len :] + incoming], axis=1
    )
    pre_low = local_grad.reshape(row_count, -1).astype(jnp.bfloat16)
    query_pre_low = pre_low[:, :query_cols]
    key_pre_low = pre_low[:, query_cols : 2 * query_cols]
    value_pre_low = pre_low[:, 2 * query_cols :]
    beta_logit_grad, decay_pre_grad, decay_log_grad, decay_bias_grad = gate_back(
        (beta_grad, decay_grad)
    )
    beta_low = beta_logit_grad.astype(jnp.bfloat16)
    decay_low = decay_pre_grad.astype(jnp.bfloat16)

    def weight_grad(grad_low):
        return jnp.einsum("rd,rc->dc", normed_low, grad_low, preferred_element_type=jnp.float32)

    def input_grad(grad_low, weight):
        return jnp.einsum("rc,dc->rd", grad_low, weight, preferred_element_type=jnp.float32)

    normed_part = (
        input_grad(query_pre_low, w_query)
        + input_grad(key_pre_low, w_key)
        + input_grad(value_pre_low, w_value)
    )
    normed_part = (
        normed_part
        + input_grad(gate_pre_low, w_outgate)
        + input_grad(beta_low, w_beta)
        + input_grad(decay_low, w_decay)
    )
    normed_grad, out_gain_total = (
        lax.psum(normed_part.astype(jnp.bfloat16), "tensor").astype(jnp.float32),
        lax.psum(out_gain_grad.astype(jnp.bfloat16), "tensor").astype(jnp.float32),
    )
    residual_part, grad_norm_mix = norm_mix_back(normed_grad)
    grad_inputs = (
        (middle_grad + residual_part).astype(jnp.bfloat16).reshape(seq_count, length, model_width)
    )
    head_totals = lax.psum((decay_log_grad, decay_bias_grad), ("dp", "seq"))
    members = (
        grad_norm_mix,
        weight_grad(query_pre_low),
        weight_grad(key_pre_low),
        weight_grad(value_pre_low),
        weight_grad(gate_pre_low),
        weight_grad(beta_low),
        weight_grad(decay_low),
        filters_grad[:query_cols],
        filters_grad[query_cols : 2 * query_cols],
        filters_grad[2 * query_cols :],
        out_gain_total,
        grad_wout,
        grad_norm_ffn,
        grad_gate,
        grad_up,
        grad_down,
    )
    shares = (
        lax.psum_scatter(
            members[0].astype(jnp.bfloat16), "seq", scatter_dimension=0, tiled=True
        ).astype(jnp.float32),
        lax.psum_scatter(
            members[1].astype(jnp.bfloat16), "seq", scatter_dimension=0, tiled=True
        ).astype(jnp.float32),
        lax.psum_scatter(
            members[2].astype(jnp.bfloat16), "seq", scatter_dimension=0, tiled=True
        ).astype(jnp.float32),
        lax.psum_scatter(
            members[3].astype(jnp.bfloat16), "seq", scatter_dimension=0, tiled=True
        ).astype(jnp.float32),
        lax.psum_scatter(
            members[4].astype(jnp.bfloat16), "seq", scatter_dimension=0, tiled=True
        ).astype(jnp.float32),
        lax.psum_scatter(
            members[5].astype(jnp.bfloat16), "seq", scatter_dimension=0, tiled=True
        ).astype(jnp.float32),
        lax.psum_scatter(
            members[6].astype(jnp.bfloat16), "seq", scatter_dimension=0, tiled=True
        ).astype(jnp.float32),
        lax.psum_scatter(
            members[7].astype(jnp.bfloat16), "seq", scatter_dimension=0, tiled=True
        ).astype(jnp.float32),
        lax.psum_scatter(
            members[8].astype(jnp.bfloat16), "seq", scatter_dimension=0, tiled=True
        ).astype(jnp.float32),
        lax.psum_scatter(
            members[9].astype(jnp.bfloat16), "seq", scatter_dimension=0, tiled=True
        ).astype(jnp.float32),
        lax.psum_scatter(
            members[10].astype(jnp.bfloat16), "seq", scatter_dimension=0, tiled=True
        ).astype(jnp.float32),
        lax.psum_scatter(
            members[11].astype(jnp.bfloat16), "seq", scatter_dimension=0, tiled=True
        ).astype(jnp.float32),
        lax.psum_scatter(
            members[12].astype(jnp.bfloat16), "seq", scatter_dimension=0, tiled=True
        ).astype(jnp.float32),
        lax.psum_scatter(
            members[13].astype(jnp.bfloat16), "seq", scatter_dimension=0, tiled=True
        ).astype(jnp.float32),
        lax.psum_scatter(
            members[14].astype(jnp.bfloat16), "seq", scatter_dimension=0, tiled=True
        ).astype(jnp.float32),
        lax.psum_scatter(
            members[15].astype(jnp.bfloat16), "seq", scatter_dimension=0, tiled=True
        ).astype(jnp.float32),
    )
    totals = (
        lax.psum(shares[0].astype(jnp.bfloat16), "dp").astype(jnp.float32),
        lax.psum(shares[1].astype(jnp.bfloat16), "dp").astype(jnp.float32),
        lax.psum(shares[2].astype(jnp.bfloat16), "dp").astype(jnp.float32),
        lax.psum(shares[3].astype(jnp.bfloat16), "dp").astype(jnp.float32),
        lax.psum(shares[4].astype(jnp.bfloat16), "dp").astype(jnp.float32),
        lax.psum(shares[5].astype(jnp.bfloat16), "dp").astype(jnp.float32),
        lax.psum(shares[6].astype(jnp.bfloat16), "dp").astype(jnp.float32),
        lax.psum(shares[7].astype(jnp.bfloat16), "dp").astype(jnp.float32),
        lax.psum(shares[8].astype(jnp.bfloat16), "dp").astype(jnp.float32),
        lax.psum(shares[9].astype(jnp.bfloat16), "dp").astype(jnp.float32),
        lax.psum(shares[10].astype(jnp.bfloat16), "dp").astype(jnp.float32),
        lax.psum(shares[11].astype(jnp.bfloat16), "dp").astype(jnp.float32),
        lax.psum(shares[12].astype(jnp.bfloat16), "dp").astype(jnp.float32),
        lax.psum(shares[13].astype(jnp.bfloat16), "dp").astype(jnp.float32),
        lax.psum(shares[14].astype(jnp.bfloat16), "dp").astype(jnp.float32),
        lax.psum(shares[15].astype(jnp.bfloat16), "dp").astype(jnp.float32),
    )
    rounded = [member.astype(jnp.bfloat16) for member in totals]
    return (
        output,
        grad_inputs,
        rounded[0],
        rounded[1],
        rounded[2],
        rounded[3],
        rounded[4],
        rounded[5],
        rounded[6],
        head_totals[0].astype(jnp.bfloat16),
        head_totals[1].astype(jnp.bfloat16),
        rounded[7],
        rounded[8],
        rounded[9],
        rounded[10],
        rounded[11],
        rounded[12],
        rounded[13],
        rounded[14],
        rounded[15],
    )


def solution(mesh):
    return jax.shard_map(
        per_device,
        mesh=mesh,
        in_specs=(
            P("dp", "seq", None),
            P("dp", "seq", None),
            P(),
            P(None, "tensor"),
            P(None, "tensor"),
            P(None, "tensor"),
            P(None, "tensor"),
            P(None, "tensor"),
            P(None, "tensor"),
            P("tensor"),
            P("tensor"),
            P("tensor", None),
            P("tensor", None),
            P("tensor", None),
            P(),
            P("tensor", None),
            P(),
            P(None, "tensor"),
            P(None, "tensor"),
            P("tensor", None),
        ),
        out_specs=(
            P("dp", "seq", None),
            P("dp", "seq", None),
            P("seq"),
            P("seq", "tensor"),
            P("seq", "tensor"),
            P("seq", "tensor"),
            P("seq", "tensor"),
            P("seq", "tensor"),
            P("seq", "tensor"),
            P("tensor"),
            P("tensor"),
            P(("tensor", "seq"), None),
            P(("tensor", "seq"), None),
            P(("tensor", "seq"), None),
            P("seq"),
            P(("tensor", "seq"), None),
            P("seq"),
            P("seq", "tensor"),
            P("seq", "tensor"),
            P(("tensor", "seq"), None),
        ),
        check_vma=False,
    )
```

profile of v0, /device:TPU:1, one launch (start us, length us, event | category | flops | bytes accessed | tf_op | source)
XLA Modules:
  0.0 2198.9 jit_solution(7174917448433314050)
XLA Ops:
  41.0 61.4 %while.139 = (s32[]{:T(128)}, f32[4,128,384]{2,1,0:T(8,128)}, f32[2,4,64]{2,1,0:T(4,128)}, f32[2,4,64,128]{3,2,1,0:T(8,128)S(1)}, f32[2,4,64]{2,1,0:T(4,128)S(1)...) while((s32[]{:T(128)}, f32[4,128,384]{2,1,0:T(8,128)}, f32[2,4,64]{2,1,0:T(4,128)}, ...), condition=%wide.region_4.5_spmd.clone.clone, body=%wide.region_2.0_spmd.clone.clone.sunk | while | flops 403574848 | bytes 5081361 | solution.py:115
  45.6 21.0 custom-call.56
  76.3 21.0 custom-call.56
  107.9 239.6 %while.137 = (s32[]{:T(128)}, f32[4,128,256]{2,1,0:T(8,128)S(1)}, f32[4,128,128]{2,1,0:T(8,128)}, f32[4,128,256]{2,1,0:T(8,128)}, s32[]{:T(128)}) while((s32[]{:T(128)}, f32[4,128,256]{2,1,0:T(8,128)S(1)}, f32[4,128,128]{2,1,0:T(8,128)}, f32[4,128,256]{2,1,0:T(8,128)}, s32[]{:T(128)}) %tuple.311), condition=%wide.region_6.7_spmd, body=%wide.region_5.6_spmd.sunk | while | flops 201457664 | bytes 3932261 | solution.py:127
  352.9 86.9 %while.140 = (s32[]{:T(128)}, f32[4,128,256]{2,1,0:T(8,128)S(1)}, f32[2,4,64,256]{3,2,1,0:T(8,128)}, f32[2,4,64,64]{3,2,1,0:T(8,128)}, f32[2,4,1,64]{3,1,2,0:T(4...) while((s32[]{:T(128)}, f32[4,128,256]{2,1,0:T(8,128)S(1)}, ...), condition=%wide.region_10.11_spmd.clone.clone, body=%wide.region_8.10_spmd.clone.clone.sunk | while | flops 454251072 | bytes 28911916 | solution.py:115
  359.0 21.0 custom-call.57
  402.3 21.0 custom-call.57
  450.6 63.4 %all-reduce.28.cloned.1.call-done = f32[128,1024]{1,0:T(8,128)} async-done(((f32[128,1024]{1,0:T(8,128)}), f32[128,1024]{1,0:T(8,128)}) %all-reduce.28.cloned.1.call-update) | async-done | bytes 524304 | tf_op jit(solution)/shard_map/psum | solution.py:236
  529.4 25.8 %all-reduce.30.cloned.1.call-done = bf16[128,1024]{1,0:T(8,128)(2,1)} async-done(((bf16[128,1024]{1,0:T(8,128)(2,1)}), bf16[128,1024]{1,0:T(8,128)(2,1)}) %all-reduce.30.cloned.1.call-update) | async-done | bytes 262160 | tf_op jit(solution)/shard_map/psum | solution.py:264
  567.3 63.0 %while.142 = (s32[]{:T(128)}, f32[4,128,256]{2,1,0:T(8,128)}, f32[2,4,1,1]{1,3,2,0:T(1,128)}, f32[2,4,64,128]{3,2,1,0:T(8,128)S(1)}, f32[2,4,64,1]{2,1,3,0:T(4,1...) while((s32[]{:T(128)}, f32[4,128,256]{2,1,0:T(8,128)}, ...), condition=%wide.region_19.21_spmd.clone, body=%wide.region_18.20_spmd.clone.sunk | while | flops 403681344 | bytes 5492423 | solution.py:115
  573.1 20.4 custom-call.60
  630.3 243.3 %while.138 = (s32[]{:T(128)}, f32[4,128,256]{2,1,0:T(8,128)S(1)}, f32[4,128,128]{2,1,0:T(8,128)}, f32[4,128,256]{2,1,0:T(8,128)}, s32[]{:T(128)}) while((s32[]{:T(128)}, f32[4,128,256]{2,1,0:T(8,128)S(1)}, f32[4,128,128]{2,1,0:T(8,128)}, f32[4,128,256]{2,1,0:T(8,128)}, s32[]{:T(128)}) %tuple.320), condition=%wide.region_21.23_spmd, body=%wide.region_20.22_spmd.sunk | while | flops 201457664 | bytes 3932261 | solution.py:127
  877.1 168.5 %while.141 = (s32[]{:T(128)}, f32[4,128,256]{2,1,0:T(8,128)S(1)}, f32[2,4,64,128]{3,2,0,1:T(8,128)}, f32[2,4,64,128]{3,2,0,1:T(8,128)}, f32[2,4,64,256]{3,2,1,0:...) while((s32[]{:T(128)}, f32[4,128,256]{2,1,0:T(8,128)S(1)}, ...), condition=%wide.region_33.35_spmd.clone.clone, body=%wide.region_22.34_spmd.clone.clone.sunk | while | flops 920925248 | bytes 36788928 | solution.py:115
  882.4 21.0 custom-call.58
  910.6 21.0 custom-call.59
  966.3 21.0 custom-call.58
  994.6 21.0 custom-call.59
  1119.1 54.6 %reduce-scatter.26.cloned.1.call-done = bf16[64,512]{1,0:T(8,128)(2,1)} async-done(((bf16[1024,512]{1,0:T(8,128)(2,1)}), bf16[64,512]{1,0:T(8,128)(2,1)}) %reduce-scatter.26.cloned.1.call-update) | async-done | bytes 65552 | tf_op jit(solution)/shard_map/reduce_scatter | solution.py:347
  1173.7 75.6 %reduce-scatter.28.cloned.1.call-done = bf16[64,512]{1,0:T(8,128)(2,1)} async-done(((bf16[1024,512]{1,0:T(8,128)(2,1)}), bf16[64,512]{1,0:T(8,128)(2,1)}) %reduce-scatter.28.cloned.1.call-update) | async-done | bytes 65552 | tf_op jit(solution)/shard_map/reduce_scatter | solution.py:350
  1249.3 76.7 %reduce-scatter.34.cloned.1.call-done = bf16[64,1024]{1,0:T(8,128)(2,1)} async-done(((bf16[1024,1024]{1,0:T(8,128)(2,1)}), bf16[64,1024]{1,0:T(8,128)(2,1)}) %reduce-scatter.34.cloned.1.call-update) | async-done | bytes 131088 | tf_op jit(solution)/shard_map/reduce_scatter | solution.py:377
  1326.0 77.1 %reduce-scatter.32.cloned.1.call-done = bf16[64,1024]{1,0:T(8,128)(2,1)} async-done(((bf16[1024,1024]{1,0:T(8,128)(2,1)}), bf16[64,1024]{1,0:T(8,128)(2,1)}) %reduce-scatter.32.cloned.1.call-update) | async-done | bytes 131088 | tf_op jit(solution)/shard_map/reduce_scatter | solution.py:356
  1403.1 76.9 %reduce-scatter.30.cloned.1.call-done = bf16[64,1024]{1,0:T(8,128)(2,1)} async-done(((bf16[1024,1024]{1,0:T(8,128)(2,1)}), bf16[64,1024]{1,0:T(8,128)(2,1)}) %reduce-scatter.30.cloned.1.call-update) | async-done | bytes 131088 | tf_op jit(solution)/shard_map/reduce_scatter | solution.py:353
  1480.0 78.5 %reduce-scatter.36.cloned.1.call-done = bf16[64,1408]{1,0:T(8,128)(2,1)} async-done(((bf16[1024,1408]{1,0:T(8,128)(2,1)}), bf16[64,1408]{1,0:T(8,128)(2,1)}) %reduce-scatter.36.cloned.1.call-update) | async-done | bytes 180240 | tf_op jit(solution)/shard_map/reduce_scatter | solution.py:383
  1558.5 78.6 %reduce-scatter.38.cloned.1.call-done = bf16[64,1408]{1,0:T(8,128)(2,1)} async-done(((bf16[1024,1408]{1,0:T(8,128)(2,1)}), bf16[64,1408]{1,0:T(8,128)(2,1)}) %reduce-scatter.38.cloned.1.call-update) | async-done | bytes 180240 | tf_op jit(solution)/shard_map/reduce_scatter | solution.py:386
  1637.1 78.3 %reduce-scatter.50.cloned.1.call-done = bf16[88,1024]{1,0:T(8,128)(2,1)} async-done(((bf16[1408,1024]{1,0:T(8,128)(2,1)}), bf16[88,1024]{1,0:T(8,128)(2,1)}) %reduce-scatter.50.cloned.1.call-update) | async-done | bytes 180240
  1715.5 135.8 %all-reduce.18 = (bf16[4]{0:T(256)(128)(2,1)}, bf16[4]{0:T(256)(128)(2,1)}) all-reduce(f32[4]{0:T(128)S(1)} %negate_multiply_fusion, f32[4]{0:T(128)S(1)} %get-tuple-element.2531), channel_id=1, replica_groups=mesh['tensor'=2,'dp'=4,'seq'=16] {'dp','seq'}, use_global_device_ids=true, to_apply=%region_54.56 | all-reduce | flops 8 | bytes 48 | tf_op jit(solution)/shard_map/psum | solution.py:324
  1866.1 74.4 %reduce-scatter.48.cloned.1.call-done = bf16[64,4]{1,0:T(8,128)(2,1)} async-done(((bf16[1024,4]{1,0:T(8,128)(2,1)}), bf16[64,4]{1,0:T(8,128)(2,1)}) %reduce-scatter.48.cloned.1.call-update) | async-done | bytes 528
  1941.3 73.6 %reduce-scatter.42.cloned.1.call-done = bf16[64,4]{1,0:T(8,128)(2,1)} async-done(((bf16[1024,4]{1,0:T(8,128)(2,1)}), bf16[64,4]{1,0:T(8,128)(2,1)}) %reduce-scatter.42.cloned.1.call-update) | async-done | bytes 528
  2015.7 38.5 %all-reduce.34.cloned.1.call-done = (bf16[128,1024]{1,0:T(8,128)(2,1)}, bf16[128,1024]{1,0:T(8,128)(2,1)}) async-done(((bf16[128,1024]{1,0:T(8,128)(2,1)}, bf16[128,1024]{1,0:T(8,128)(2,1)}), (bf16[128,1024]{1,0:T(8,128)(2,1)}, bf16[128,1024]{1,0:T(8,128)(2,1)})) %all-reduce.34.cloned.1.call-update) | async-done | bytes 524304 | tf_op jit(solution)/shard_map/psum | solution.py:244
  2055.5 33.8 %all-reduce.19 = (bf16[1024]{0:T(1024)(128)(2,1)S(1)}, bf16[256]{0:T(256)(128)(2,1)S(1)}, bf16[1024]{0:T(1024)(128)(2,1)S(1)}) all-reduce(bf16[1024]{0:T(1024)(128)(2,1)S(1)} %get-tuple-element.2330, bf16[256]{0:T(256)(128)(2,1)S(1)} %copy-done.104, ...), channel_id=2, replica_groups=mesh['tensor'=2,'dp'=4,'seq'=16] {'seq'}, use_global_device_ids=true, to_apply=%region_39.41.clone | all-reduce | flops 2304 | bytes 9216
  2089.4 39.3 %reduce-scatter.40.cloned.1.call-done = bf16[64,4]{1,0:T(8,128)(2,1)} async-done(((bf16[1024,4]{1,0:T(8,128)(2,1)}), bf16[64,4]{1,0:T(8,128)(2,1)}) %reduce-scatter.40.cloned.1.call-update) | async-done | bytes 528
  2147.9 31.7 %all-reduce.32.cloned.1.call-done = (bf16[64,512]{1,0:T(8,128)(2,1)}, bf16[64,512]{1,0:T(8,128)(2,1)}, bf16[64,1024]{1,0:T(8,128)(2,1)}, bf16[64,1024]{1,0:T(8,1...) async-done(((bf16[64,512]{1,0:T(8,128)(2,1)}, bf16[64,512]{1,0:T(8,128)(2,1)}, ...) | async-done | bytes 1064976 | tf_op jit(solution)/shard_map/psum | solution.py:395
  (795 shorter events, 878.6 us)
Async XLA Ops:
  7.2 506.8 %all-reduce.28.cloned.1.call-start = ((), (), s32[]{:S(2)}) async-start(), calls=%async_computation.13 | async-start | bytes 1048576 | tf_op jit(solution)/shard_map/psum | solution.py:236
  110.4 13.7 collective-permute-start
  126.6 13.6 collective-permute-start
  259.8 12.9 collective-permute-start
  275.1 14.2 collective-permute-start
  291.8 15.8 collective-permute-start
  310.1 16.9 collective-permute-start
  329.5 18.0 collective-permute-start
  450.5 104.7 %all-reduce.30.cloned.1.call-start = ((), (), s32[]{:S(2)}) async-start(), calls=%async_computation.14 | async-start | bytes 524288 | tf_op jit(solution)/shard_map/psum | solution.py:264
  524.7 649.0 %reduce-scatter.26.cloned.1.call-start = ((), (), s32[]{:S(2)}) async-start(), calls=%async_computation.15 | async-start | bytes 1114112 | tf_op jit(solution)/shard_map/reduce_scatter | solution.py:347
  632.8 14.4 collective-permute-start.1
  649.7 13.5 collective-permute-start.1
  680.6 14.3 collective-permute-start.1
  784.6 13.1 collective-permute-start.1
  800.2 14.6 collective-permute-start.1
  817.3 16.0 collective-permute-start.1
  835.8 17.1 collective-permute-start.1
  855.4 18.2 collective-permute-start.1
  1076.6 172.7 %reduce-scatter.28.cloned.1.call-start = ((), (), s32[]{:S(2)}) async-start(), calls=%async_computation.16 | async-start | bytes 1114112 | tf_op jit(solution)/shard_map/reduce_scatter | solution.py:350
  1079.1 246.9 %reduce-scatter.34.cloned.1.call-start = ((), (), s32[]{:S(2)}) async-start(), calls=%async_computation.19 | async-start | bytes 2228224 | tf_op jit(solution)/shard_map/reduce_scatter | solution.py:377
  1082.3 320.8 %reduce-scatter.32.cloned.1.call-start = ((), (), s32[]{:S(2)}) async-start(), calls=%async_computation.18 | async-start | bytes 2228224 | tf_op jit(solution)/shard_map/reduce_scatter | solution.py:356
  1085.8 394.2 %reduce-scatter.30.cloned.1.call-start = ((), (), s32[]{:S(2)}) async-start(), calls=%async_computation.17 | async-start | bytes 2228224 | tf_op jit(solution)/shard_map/reduce_scatter | solution.py:353
  1088.9 469.6 %reduce-scatter.36.cloned.1.call-start = ((), (), s32[]{:S(2)}) async-start(), calls=%async_computation.20 | async-start | bytes 3063808 | tf_op jit(solution)/shard_map/reduce_scatter | solution.py:383
  1092.5 544.6 %reduce-scatter.38.cloned.1.call-start = ((), (), s32[]{:S(2)}) async-start(), calls=%async_computation.21 | async-start | bytes 3063808 | tf_op jit(solution)/shard_map/reduce_scatter | solution.py:386
  1096.1 619.3 %reduce-scatter.50.cloned.1.call-start = ((), (), s32[]{:S(2)}) async-start(), calls=%async_computation.27 | async-start | bytes 3063808
  1100.6 750.6 %reduce-scatter.44.cloned.1.call-start = ((), (), s32[]{:S(2)}) async-start(), calls=%async_computation.24 | async-start | bytes 139264
  1107.4 757.9 %reduce-scatter.46.cloned.1.call-start = ((), (), s32[]{:S(2)}) async-start(), calls=%async_computation.25 | async-start | bytes 139264
  1108.7 831.8 %reduce-scatter.48.cloned.1.call-start = ((), (), s32[]{:S(2)}) async-start(), calls=%async_computation.26 | async-start | bytes 278528
  1109.8 905.1 %reduce-scatter.42.cloned.1.call-start = ((), (), s32[]{:S(2)}) async-start(), calls=%async_computation.23 | async-start | bytes 278528
  1110.8 943.5 %all-reduce.34.cloned.1.call-start = ((), (), s32[]{:S(2)}) async-start(), calls=%async_computation.29 | async-start | bytes 1048576 | tf_op jit(solution)/shard_map/psum | solution.py:244
  1116.0 1012.7 %reduce-scatter.40.cloned.1.call-start = ((), (), s32[]{:S(2)}) async-start(), calls=%async_computation.22 | async-start | bytes 278528
  1117.2 1062.5 %all-reduce.32.cloned.1.call-start = ((), (), s32[]{:S(2)}) async-start(), calls=%async_computation.28 | async-start | bytes 2129920 | tf_op jit(solution)/shard_map/psum | solution.py:395
  (165 other events, 4994.2 us)
Sparse Core Ops, SparseCore 0:
  450.6 63.3 all-reduce.27
  524.8 30.3 all-reduce.29
  1076.8 96.9 reduce-scatter.25
  1177.1 72.1 reduce-scatter.27
  1252.5 73.4 reduce-scatter.33
  1329.5 73.6 reduce-scatter.31
  1406.4 73.5 reduce-scatter.29
  1483.7 74.7 reduce-scatter.35
  1562.2 74.8 reduce-scatter.37
  1640.6 74.7 reduce-scatter.49
  1719.5 70.9 reduce-scatter.43
  1794.0 71.2 reduce-scatter.45
  1868.8 71.6 reduce-scatter.47
  1943.5 71.3 reduce-scatter.41
  2018.0 36.2 all-reduce.33
  2057.3 71.3 reduce-scatter.39
  2132.0 47.6 all-reduce.31
where the time goes:
time: 2210 us; the launch traced here: 2200 us
  waiting for transfers between devices  1270 us (57%)
  other arithmetic  277 us (13%)
  matrix products  223 us (10%)
  blocking collectives  184 us (8%)
  local copies, waits for them, and re-layouts  119 us (5%)
  starting transfers between devices  107 us (5%)
    ppermute x32, waiting for transfers between devices, from_behind(): lax.ppermute(value, axis, [(source, source + steps) for source in range(i...  313 us
    unnamed x23, waiting for transfers between devices  279 us
    another operation x34, other arithmetic, advance(): jax.scipy.linalg.solve_triangular(identity + lower_part, target, lower=Tr...  216 us
    dot_general x80, matrix products, product_high(): return jnp.einsum(form, left_op, right_op, precision=highest)  150 us
    psum x1, blocking collectives, per_device(): head_totals = lax.psum((decay_log_grad, decay_bias_grad), ('dp', 'seq'))  136 us
    ppermute x32, starting transfers between devices, from_behind(): lax.ppermute(value, axis, [(source, source + steps) for source in range(i...  106 us
    reduce_scatter x1, waiting for transfers between devices, per_device(): lax.psum_scatter(members[14].astype(jnp.bfloat16), 'seq', scatter_dimensi...  78.6 us
    reduce_scatter x1, waiting for transfers between devices, per_device(): lax.psum_scatter(members[13].astype(jnp.bfloat16), 'seq', scatter_dimensi...  78.5 us
  transfers between devices with their start and end apart: 49, of which 47 were waited for; matrix products, arithmetic and copies ran while one was open for 3% of the time, Pallas kernels for 0%

commit v1 on v0

v1 whole, which is shorter than its diff:
```python
import functools

import jax
import jax.numpy as jnp
from jax import lax
from jax.experimental import pallas as pl
from jax.experimental.pallas import tpu as pltpu
from jax.sharding import PartitionSpec as P

f32 = jnp.float32
bf16 = jnp.bfloat16
epsilon = 1e-05
smallest = 1e-06
TOK = 128
HEADS = 4
DK = 128
DV = 256
QK = HEADS * DK
VW = HEADS * DV
PRE = 2 * QK + VW
SEQ = 16
HALO = 16
MIB = 1024 * 1024


def kernel_call(body, outs, *args, scratch=(), limit=40 * MIB, flops=0, moved=0):
    out_shape = [jax.ShapeDtypeStruct(shape, kind) for shape, kind in outs]
    if not moved:
        moved = sum(a.size * a.dtype.itemsize for a in args)
        moved += sum(o.size * o.dtype.itemsize for o in out_shape)
    return pl.pallas_call(
        body,
        out_shape=out_shape,
        in_specs=[pl.BlockSpec(memory_space=pltpu.VMEM)] * len(args),
        out_specs=[pl.BlockSpec(memory_space=pltpu.VMEM)] * len(outs),
        scratch_shapes=list(scratch),
        compiler_params=pltpu.CompilerParams(vmem_limit_bytes=limit),
        cost_estimate=pl.CostEstimate(flops=flops, bytes_accessed=moved, transcendentals=0),
    )(*args)


def mm(a, b):
    return jnp.dot(a.astype(bf16), b.astype(bf16), preferred_element_type=f32)


def mt(a, b):
    return lax.dot_general(
        a.astype(bf16), b.astype(bf16), (((1,), (1,)), ((), ())), preferred_element_type=f32
    )


def tm(a, b):
    return lax.dot_general(
        a.astype(bf16), b.astype(bf16), (((0,), (0,)), ((), ())), preferred_element_type=f32
    )


def halves(a):
    high = a.astype(bf16)
    return high, (a - high.astype(f32)).astype(bf16)


def mm3(a, b):
    ah, al = halves(a)
    bh, bl = halves(b)
    return mm(jnp.concatenate([ah, al, ah], axis=1), jnp.concatenate([bh, bh, bl], axis=0))


def mm2(a, b):
    ah, al = halves(a)
    return mm(jnp.concatenate([ah, al], axis=1), jnp.concatenate([b, b], axis=0))


def thirds(a):
    high = a.astype(bf16)
    rest = a - high.astype(f32)
    mid = rest.astype(bf16)
    return high, mid, (rest - mid.astype(f32)).astype(bf16)


def masks():
    rows = lax.broadcasted_iota(jnp.int32, (TOK, TOK), 0)
    cols = lax.broadcasted_iota(jnp.int32, (TOK, TOK), 1)
    return rows, cols


def sigmoid(v):
    return 1.0 / (1.0 + jnp.exp(-v))


def fading_of(c_col, c_row, inclusive):
    return jnp.where(inclusive, jnp.exp(jnp.where(inclusive, c_col - c_row, 0.0)), 0.0)


def front_kernel(
    pre, halo, filt, bdv, z_o, q_o, k_o, x_o, c_o, uv_o, uk_o, ol_o, qe_o, send_o, ext
):
    ext[0:HALO] = halo[...].astype(f32)
    ext[HALO:] = pre[...].astype(f32)

    def activated(at, width):
        z = ext[pl.ds(HALO - 3, TOK), at : at + width] * filt[0:1, at : at + width]
        for j in range(1, 4):
            z = z + ext[pl.ds(HALO - 3 + j, TOK), at : at + width] * filt[j : j + 1, at : at + width]
        z_o[:, at : at + width] = z
        return z * sigmoid(z)

    rows, cols = masks()
    inclusive = rows >= cols
    strict = rows > cols
    lower = jnp.where(inclusive, 1.0, 0.0).astype(bf16)
    eye = jnp.where(rows == cols, 1.0, 0.0)
    scal = bdv[...]
    c_all = mm(
        jnp.concatenate([lower, lower, lower], axis=1), jnp.concatenate(thirds(scal), axis=0)
    )
    c_o[...] = c_all
    c_t = c_all.T
    b_t = scal.T
    for h in range(HEADS):
        a_q = activated(h * DK, DK)
        a_k = activated(QK + h * DK, DK)
        a_v = activated(2 * QK + h * DV, DV)
        q = (
            a_q
            * lax.rsqrt(jnp.sum(a_q * a_q, axis=1, keepdims=True) + smallest)
            * DK ** (-0.5)
        ).astype(bf16)
        k = (a_k * lax.rsqrt(jnp.sum(a_k * a_k, axis=1, keepdims=True) + smallest)).astype(bf16)
        v = a_v.astype(bf16)
        q_o[:, h * DK : (h + 1) * DK] = q
        k_o[:, h * DK : (h + 1) * DK] = k
        c_col = c_all[:, HEADS + h : HEADS + h + 1]
        c_row = c_t[HEADS + h : HEADS + h + 1, :]
        b_col = scal[:, h : h + 1]
        b_row = b_t[h : h + 1, :]
        fading = fading_of(c_col, c_row, inclusive)
        low = jnp.where(strict, fading * b_row * mt(k, k), 0.0)
        inv = eye - jnp.where((rows // 2 == cols // 2) & strict, low, 0.0)
        size = 2
        while size < TOK:
            part = (
                (rows // (2 * size) == cols // (2 * size))
                & (rows // size % 2 == 1)
                & (cols // size % 2 == 0)
            )
            inv = inv - mm3(inv, mm3(jnp.where(part, low, 0.0), inv))
            size *= 2
        x_o[h] = inv
        growth = jnp.exp(c_col)
        u_v = mm2(inv, v)
        u_k = mm2(inv * jnp.exp(c_row), k)
        uv_o[:, h * DV : (h + 1) * DV] = u_v
        uk_o[:, h * DK : (h + 1) * DK] = u_k.astype(bf16)
        scores = fading * mt(q, k) * b_row
        ol_o[:, h * DV : (h + 1) * DV] = mm(scores, u_v)
        qe_o[:, h * DK : (h + 1) * DK] = (growth * q.astype(f32) - mm(scores, u_k)).astype(bf16)
        c_last = c_all[TOK - 1 : TOK, HEADS + h : HEADS + h + 1]
        b_k = b_col * jnp.exp(c_last - c_col) * k.astype(f32)
        turned = (eye * jnp.exp(c_last) - tm(u_k, b_k)).astype(bf16)
        offset = tm(u_v, b_k).astype(bf16)
        for g in range(4):
            send_o[h * 4 + g, 0:DK] = turned
            send_o[h * 4 + g, DK : DK + 64] = offset[64 * g : 64 * g + 64]


def scan_kernel(maps, out):
    state = jnp.zeros((64, DK), f32)
    for d in range(SEQ):
        out[d] = state.astype(bf16)
        if d < SEQ - 1:
            turned = maps[d, 0:DK]
            state = mm(
                jnp.concatenate(halves(state), axis=1), jnp.concatenate([turned, turned], axis=0)
            ) + maps[d, DK : DK + 64].astype(f32)


def scan_back_kernel(grads, maps, out):
    state = jnp.zeros((64, DK), f32)
    for d in range(SEQ - 1, -1, -1):
        out[d] = state.astype(bf16)
        if d > 0:
            turned = maps[d, 0:DK]
            state = mt(
                jnp.concatenate(halves(state), axis=1), jnp.concatenate([turned, turned], axis=1)
            ) + grads[d].astype(f32)


def mixed_kernel(ol, qe, st, gate_pre, gain, mixed_o, gated_o):
    for h in range(HEADS):
        at = slice(h * DV, (h + 1) * DV)
        state = st[4 * h : 4 * h + 4].reshape(DV, DK)
        mixed = ol[:, at] + mt(qe[:, h * DK : (h + 1) * DK], state)
        mixed_o[:, at] = mixed
        normed = mixed * lax.rsqrt(jnp.mean(mixed * mixed, axis=1, keepdims=True) + epsilon)
        gate = gate_pre[:, at]
        gated_o[:, at] = (normed * gain[...] * (gate * sigmoid(gate))).astype(bf16)


def mixed_back_kernel(gated_grad, mixed_in, gate_pre, gain, qe, do_o, gp_o, gain_o, sg_o):
    gain_total = jnp.zeros((1, DV), f32)
    for h in range(HEADS):
        at = slice(h * DV, (h + 1) * DV)
        mixed = mixed_in[:, at]
        root = lax.rsqrt(jnp.mean(mixed * mixed, axis=1, keepdims=True) + epsilon)
        m = mixed * root
        gate = gate_pre[:, at]
        sig = sigmoid(gate)
        grad = gated_grad[:, at]
        gm = grad * m
        silu = gate * sig
        gain_total = gain_total + jnp.sum(gm * silu, axis=0, keepdims=True)
        gp_o[:, at] = (gm * gain[...] * (sig * (1.0 + gate * (1.0 - sig)))).astype(bf16)
        e = grad * gain[...] * silu
        d_out = (root * (e - m * jnp.mean(e * m, axis=1, keepdims=True))).astype(bf16)
        do_o[:, at] = d_out
        sg = tm(d_out, qe[:, h * DK : (h + 1) * DK])
        sg_o[4 * h : 4 * h + 4] = sg.astype(bf16).reshape(4, 64, DK)
    gain_o[...] = gain_total


def back_kernel(
    pre, halo, filt, bdv, z_i, q_i, k_i, x_i, c_i, uv_i, uk_i, do_i, st_i, gt_i,
    dz_o, dzh_o, fg_o, dbd_o, ext,
):
    ext[0:HALO] = halo[...].astype(f32)
    ext[HALO:] = pre[...].astype(f32)
    rows, cols = masks()
    inclusive = rows >= cols
    strict = rows > cols
    scal = bdv[...]
    c_all = c_i[...]
    c_t = c_all.T
    b_t = scal.T

    def finish(grad, z, sig, at, width):
        dz = grad * (sig * (1.0 + z * (1.0 - sig)))
        dz_o[:, at : at + width] = dz
        dzh_o[:, at : at + width] = dz[0:HALO].astype(bf16)
        for j in range(4):
            fg_o[j : j + 1, at : at + width] = jnp.sum(
                dz * ext[pl.ds(HALO - 3 + j, TOK), at : at + width], axis=0, keepdims=True
            )

    fg_o[4:8, :] = jnp.zeros((4, PRE), f32)
    lane = lax.broadcasted_iota(jnp.int32, (TOK, TOK), 1)
    cols_acc = jnp.zeros((TOK, TOK), f32)
    sub = lax.broadcasted_iota(jnp.int32, (TOK, TOK), 0)
    rows_acc = jnp.zeros((TOK, TOK), f32)
    for h in range(HEADS):
        atv = slice(h * DV, (h + 1) * DV)
        atk = slice(h * DK, (h + 1) * DK)
        q = q_i[:, atk]
        k = k_i[:, atk]
        q32 = q.astype(f32)
        k32 = k.astype(f32)
        st = st_i[4 * h : 4 * h + 4].reshape(DV, DK)
        gt = gt_i[4 * h : 4 * h + 4].reshape(DV, DK)
        d_out = do_i[:, atv]
        c_col = c_all[:, HEADS + h : HEADS + h + 1]
        c_row = c_t[HEADS + h : HEADS + h + 1, :]
        c_last = c_all[TOK - 1 : TOK, HEADS + h : HEADS + h + 1]
        b_col = scal[:, h : h + 1]
        b_row = b_t[h : h + 1, :]
        fading = fading_of(c_col, c_row, inclusive)
        growth = jnp.exp(c_col)
        remains = jnp.exp(c_last - c_col)
        scores = fading * mt(q, k)
        low_one = jnp.where(strict, fading * mt(k, k), 0.0)
        u = uv_i[:, atv] - mt(uk_i[:, atk], st)
        w = (b_col * u).astype(bf16)
        k_rem = remains * k32
        d_w = tm(scores, d_out) + mt(k_rem, gt)
        d_beta = jnp.sum(u * d_w, axis=1, keepdims=True)
        d_r = tm(x_i[h], b_col * d_w)
        d_rl = d_r.astype(bf16)
        d_low = jnp.where(strict, -mt(d_rl, u), 0.0)
        d_a = jnp.where(inclusive, mt(d_out, w), 0.0)
        d_qk = d_a * fading
        e_beta = d_low * low_one
        e_sum = d_a * scores + e_beta * b_row
        d_kk = d_low * fading * b_row
        d_os = mm(d_out, st)
        d_rs = mm(d_rl, st)
        w_g = mm(w, gt)
        dq = mm(d_qk, k) + growth * d_os
        dk = tm(d_qk, q) + mm(d_kk, k) + tm(d_kk, k) - growth * d_rs + remains * w_g
        rem_sum = jnp.sum(k_rem * w_g, axis=1, keepdims=True)
        d_c = (
            jnp.sum(e_sum, axis=1, keepdims=True)
            + growth * jnp.sum(q32 * d_os - k32 * d_rs, axis=1, keepdims=True)
            - rem_sum
        )
        last = jnp.sum(rem_sum, axis=0, keepdims=True) + jnp.exp(c_last) * jnp.sum(
            jnp.sum(st.astype(f32) * gt.astype(f32), axis=1, keepdims=True), axis=0, keepdims=True
        )
        d_c = d_c + jnp.where(sub[:, 0:1] == TOK - 1, last, 0.0)
        cols_acc = cols_acc + jnp.where(lane == h, d_beta, 0.0)
        cols_acc = cols_acc + jnp.where(lane == HEADS + h, d_c, 0.0)
        rows_acc = rows_acc + jnp.where(sub == h, jnp.sum(e_beta, axis=0, keepdims=True), 0.0)
        rows_acc = rows_acc - jnp.where(
            sub == HEADS + h, jnp.sum(e_sum, axis=0, keepdims=True), 0.0
        )
        for grad, base, scale in ((dq, 0, DK ** (-0.5)), (dk, QK, 1.0)):
            at = base + h * DK
            z = z_i[:, at : at + DK]
            sig = sigmoid(z)
            act = z * sig
            root = lax.rsqrt(jnp.sum(act * act, axis=1, keepdims=True) + smallest)
            unit = act * root
            grad = grad * scale
            d_act = root * (grad - unit * jnp.sum(unit * grad, axis=1, keepdims=True))
            finish(d_act, z, sig, at, DK)
        at = 2 * QK + h * DV
        z = z_i[:, at : at + DV]
        finish(d_r, z, sigmoid(z), at, DV)
    total = cols_acc + rows_acc.T
    upper = jnp.where(rows <= cols, 1.0, 0.0).astype(bf16)
    summed = mm(
        jnp.concatenate([upper, upper, upper], axis=1), jnp.concatenate(thirds(total), axis=0)
    )
    dbd_o[...] = jnp.where(lane < HEADS, total, summed)


def conv_back_kernel(dz, after, filt, pre_o, ext):
    ext[0:TOK] = dz[...]
    ext[TOK:] = after[...].astype(f32)
    for at in range(0, PRE, 256):
        total = ext[pl.ds(3, TOK), at : at + 256] * filt[0:1, at : at + 256]
        for j in range(1, 4):
            total = total + ext[pl.ds(3 - j, TOK), at : at + 256] * filt[j : j + 1, at : at + 256]
        pre_o[:, at : at + 256] = total.astype(bf16)


def padded_rows(left):
    return -(-(left.shape[1] // SEQ) // 16) * 16


def pieces_rows(pieces):
    return sum(padded_rows(left) * (right.shape[1] // 128) for left, right in pieces)


def weight_body(count, added, refs):
    ins = refs[: 2 * count]
    adds = refs[2 * count : 2 * count + added]
    out = refs[2 * count + added]
    turned = refs[2 * count + added + 1]
    offset = 0
    part = 0
    done = 0
    for at in range(count):
        left, right = ins[2 * at], ins[2 * at + 1]
        width = left.shape[1]
        rows = width // SEQ
        padded = padded_rows(left)
        turned[0:width] = left[...].T

        def tile(n, carry, right=right, width=width, rows=rows, padded=padded, offset=offset,
                 part=part, done=done):
            piece = jnp.dot(
                turned[0:width],
                right[:, pl.ds(pl.multiple_of(n * 128, 128), 128)],
                preferred_element_type=f32,
            ).reshape(SEQ, rows, 128)
            if padded > rows:
                piece = jnp.concatenate([piece, jnp.zeros((SEQ, padded - rows, 128), f32)], axis=1)
            if added:
                where = pl.ds(pl.multiple_of(offset - done + n * padded, 16), padded)
                piece = piece + adds[part][:, where].astype(f32)
            where = pl.ds(pl.multiple_of(offset + n * padded, 16), padded)
            out[:, where] = piece.astype(bf16)
            return carry

        lax.fori_loop(0, right.shape[1] // 128, tile, 0)
        offset += padded * (right.shape[1] // 128)
        if added and offset - done == adds[part].shape[1]:
            done = offset
            part += 1


def weight_grads(pieces, adds=()):
    total = pieces_rows(pieces)
    args = [operand for pair in pieces for operand in pair] + list(adds)

    def body(*refs):
        weight_body(len(pieces), len(adds), refs)

    return kernel_call(
        body,
        [((SEQ, total, 128), bf16)],
        *args,
        scratch=[pltpu.VMEM((1408, TOK), bf16)],
        limit=48 * MIB,
        flops=2 * 128 * 128 * SEQ * total,
    )[0]


SPLIT = 272


def spread_body(place, kept, small, small_in, *outs):
    rows = kept.shape[1]
    z_at, x_at = place[0], place[1]
    for s in range(4):
        x_to = lax.rem(x_at + s, 4)
        z_to = lax.rem(z_at + s, 4)
        for other in range(4):
            outs[s][other] = kept[other * 4 + x_to, 0:SPLIT]
            outs[4 + s][other, 0 : rows - SPLIT] = kept[z_to * 4 + other, SPLIT:rows]
            outs[4 + s][other, rows - SPLIT :] = (
                small[z_to * 4 + other].astype(f32) + small_in[z_to * 4 + other].astype(f32)
            ).astype(bf16)


def spread_again_body(place, *refs):
    z_at, x_at = place[0], place[1]
    first, second, outs = refs[0:4], refs[4:8], refs[8:]
    rows = second[0].shape[1]
    for s in range(4):
        z_to = lax.rem(z_at + s, 4)
        x_to = lax.rem(x_at + s, 4)
        total = first[0][z_to].astype(f32)
        other = second[0][x_to].astype(f32)
        for n in range(1, 4):
            total = total + first[n][z_to].astype(f32)
            other = other + second[n][x_to].astype(f32)
        outs[s][...] = total.astype(bf16)
        outs[4 + s][...] = other.astype(bf16)
        outs[4 + s][rows - 16 :] = in_order(
            [second[n][x_to, rows - 16 : rows] for n in range(4)], z_at
        ).astype(bf16)


def in_order(terms, own):
    total = None
    for source in range(4):
        which = lax.rem(own + 4 - source, 4)
        term = jnp.zeros(terms[0].shape, f32)
        for n in range(4):
            term = jnp.where(which == n, terms[n].astype(f32), term)
        total = term if total is None else total + term
    return total


def gather_body(place, *refs):
    out = refs[8]
    rows = out.shape[0]
    total = refs[0][...].astype(f32)
    other = refs[4][...].astype(f32)
    for n in range(1, 4):
        total = total + refs[n][...].astype(f32)
        other = other + refs[4 + n][...].astype(f32)
    out[0:SPLIT] = total.astype(bf16)
    out[SPLIT:] = other.astype(bf16)
    out[rows - 16 :] = in_order(
        [refs[4 + n][rows - SPLIT - 16 : rows - SPLIT] for n in range(4)], place[1]
    ).astype(bf16)


def placed_call(body, outs, place, *args):
    out_shape = [jax.ShapeDtypeStruct(shape, bf16) for shape in outs]
    return pl.pallas_call(
        body,
        out_shape=out_shape,
        in_specs=[pl.BlockSpec(memory_space=pltpu.SMEM)]
        + [pl.BlockSpec(memory_space=pltpu.VMEM)] * len(args),
        out_specs=[pl.BlockSpec(memory_space=pltpu.VMEM)] * len(outs),
        compiler_params=pltpu.CompilerParams(vmem_limit_bytes=40 * MIB),
    )(place, *args)


def along_x(steps):
    return [(z * 4 + x, z * 4 + (x + steps) % 4) for z in range(4) for x in range(4)]


def along_z(steps):
    return [(z * 4 + x, (z + steps) % 4 * 4 + x) for z in range(4) for x in range(4)]


def swap_tensor(value):
    return lax.ppermute(value, "tensor", [(0, 1), (1, 0)])


def swap_core(value):
    return lax.ppermute(value, "dp", [(0, 1), (1, 0), (2, 3), (3, 2)])


def swap_far(value):
    return lax.ppermute(value, "dp", [(0, 2), (2, 0), (1, 3), (3, 1)])


def shift(value, steps):
    first, last = max(0, -steps), min(SEQ, SEQ - steps)
    return lax.ppermute(value, "seq", [(at, at + steps) for at in range(first, last)])


def exchange(value):
    return lax.all_to_all(value, "seq", 0, 0, tiled=True)


def over_dp(shared):
    mine = (shared.astype(f32) + swap_far(shared).astype(f32)).astype(bf16)
    other = swap_core(mine)
    first = lax.axis_index("dp") % 2 == 0
    return jnp.where(first, mine, other), jnp.where(first, other, mine)


def tiles_to_rows(block, rows, padded):
    tiles = block.shape[0] // padded
    return (
        block.reshape(tiles, padded, 128)[:, :rows].transpose(1, 0, 2).reshape(rows, tiles * 128)
    )


def dot(a, b):
    return jnp.dot(a, b, preferred_element_type=f32)


def dot_t(a, b):
    return lax.dot_general(a, b, (((1,), (1,)), ((), ())), preferred_element_type=f32)


def norm_parts(values):
    root = lax.rsqrt(jnp.mean(values * values, axis=-1, keepdims=True) + epsilon)
    return root, values * root


def norm_back(grad, gain, root, unit):
    e = grad * gain
    return root * (e - unit * jnp.mean(e * unit, axis=-1, keepdims=True))


def per_device(
    inputs,
    cotangent,
    norm_mix,
    w_query,
    w_key,
    w_value,
    w_outgate,
    w_beta,
    w_decay,
    decay_log,
    decay_bias,
    conv_query,
    conv_key,
    conv_value,
    out_gain,
    w_out,
    norm_ffn,
    w_gate,
    w_up,
    w_down,
):
    width = inputs.shape[2]
    first = lax.axis_index("dp") % 2 == 0
    at = lax.axis_index("seq")
    place = jnp.stack([at // 4, at % 4]).astype(jnp.int32)
    residual = inputs.reshape(TOK, width).astype(f32)
    feed_grad = cotangent.reshape(TOK, width)
    gain_mix = norm_mix.astype(f32)
    gain_ffn = norm_ffn.astype(f32)
    gain_head = out_gain.astype(f32).reshape(1, DV)
    filters = jnp.concatenate([conv_query, conv_key, conv_value], axis=0).astype(f32)
    filt = jnp.pad(filters.T, ((0, 4), (0, 0)))

    root_mix, unit_mix = norm_parts(residual)
    normed_low = (unit_mix * gain_mix).astype(bf16)
    mixed_pre = jnp.concatenate(
        [dot(normed_low, w_query), dot(normed_low, w_key), dot(normed_low, w_value)], axis=1
    ).astype(bf16)
    halo = shift(mixed_pre[TOK - HALO :], 1)
    beta_rows = jax.nn.sigmoid(dot(normed_low, w_beta))
    decay_at = dot(normed_low, w_decay) + decay_bias.astype(f32)
    decay_rate = -jnp.exp(decay_log.astype(f32))
    decays = decay_rate * jax.nn.softplus(decay_at)
    bdv = jnp.pad(jnp.concatenate([beta_rows, decays], axis=1), ((0, 0), (0, 120)))
    gate_pre = dot(normed_low, w_outgate)

    z, q, k, inverse, c_all, u_v, u_k, out_local, q_eff, maps = kernel_call(
        front_kernel,
        [
            ((TOK, PRE), f32),
            ((TOK, QK), bf16),
            ((TOK, QK), bf16),
            ((HEADS, TOK, TOK), f32),
            ((TOK, TOK), f32),
            ((TOK, VW), f32),
            ((TOK, QK), bf16),
            ((TOK, VW), f32),
            ((TOK, QK), bf16),
            ((SEQ, DK + 64, DK), bf16),
        ],
        mixed_pre,
        halo,
        filt,
        bdv,
        scratch=[pltpu.VMEM((TOK + HALO, PRE), f32)],
    )
    maps = exchange(maps)
    (states,) = kernel_call(scan_kernel, [((SEQ, 64, DK), bf16)], maps)
    states = exchange(states)
    mixed, gated_low = kernel_call(
        mixed_kernel,
        [((TOK, VW), f32), ((TOK, VW), bf16)],
        out_local,
        q_eff,
        states,
        gate_pre,
        gain_head,
    )
    branch = dot(gated_low, w_out).astype(bf16)
    branch_in = swap_tensor(branch)
    hidden_grad = dot_t(feed_grad, w_down)
    middle = residual + (branch.astype(f32) + branch_in.astype(f32))
    root_ffn, unit_ffn = norm_parts(middle)
    two_low = (unit_ffn * gain_ffn).astype(bf16)
    gate_ffn = dot(two_low, w_gate)
    up_ffn = dot(two_low, w_up)
    sig = jax.nn.sigmoid(gate_ffn)
    silu = gate_ffn * sig
    hidden_low = (silu * up_ffn).astype(bf16)
    gate_low = (hidden_grad * up_ffn * (sig * (1.0 + gate_ffn * (1.0 - sig)))).astype(bf16)
    up_low = (hidden_grad * silu).astype(bf16)
    two_part = (dot_t(gate_low, w_gate) + dot_t(up_low, w_up)).astype(bf16)
    two_in = swap_tensor(two_part)
    feed_part = dot(hidden_low, w_down).astype(bf16)
    feed_in = swap_tensor(feed_part)
    output = (middle + (feed_part.astype(f32) + feed_in.astype(f32))).astype(bf16)

    half = width // 2
    ffn_sent = weight_grads(
        [
            (two_low, jnp.where(first, up_low, gate_low)),
            (hidden_low, jnp.where(first, feed_grad[:, half:], feed_grad[:, :half])),
        ]
    )
    ffn_in = swap_core(ffn_sent)

    two_grad = two_part.astype(f32) + two_in.astype(f32)
    grad_norm_ffn = jnp.sum(two_grad * unit_ffn, axis=0)
    middle_grad = feed_grad.astype(f32) + norm_back(two_grad, gain_ffn, root_ffn, unit_ffn)
    branch_low = middle_grad.astype(bf16)
    gated_grad = dot_t(branch_low, w_out)
    mixed_grad, gate_pre_low, gain_grad, start_grad = kernel_call(
        mixed_back_kernel,
        [((TOK, VW), bf16), ((TOK, VW), bf16), ((1, DV), f32), ((SEQ, 64, DK), bf16)],
        gated_grad,
        mixed,
        gate_pre,
        gain_head,
        q_eff,
    )
    out_sent = weight_grads(
        [
            (
                jnp.where(first, gated_low, normed_low),
                jnp.where(first, branch_low, gate_pre_low),
            )
        ]
    )
    out_in = swap_core(out_sent)
    early = weight_grads(
        [
            (two_low, jnp.where(first, gate_low, up_low)),
            (hidden_low, jnp.where(first, feed_grad[:, :half], feed_grad[:, half:])),
            (
                jnp.where(first, normed_low, gated_low),
                jnp.where(first, gate_pre_low, branch_low),
            ),
        ],
        [ffn_in, out_in],
    )
    early = lax.psum_scatter(early, "seq", scatter_dimension=0, tiled=True)

    start_grad = exchange(start_grad)
    (end_grads,) = kernel_call(scan_back_kernel, [((SEQ, 64, DK), bf16)], start_grad, maps)
    end_grads = exchange(end_grads)
    dz, dz_first, filter_grad, scal_grad = kernel_call(
        back_kernel,
        [
            ((TOK, PRE), f32),
            ((HALO, PRE), bf16),
            ((8, PRE), f32),
            ((TOK, TOK), f32),
        ],
        mixed_pre,
        halo,
        filt,
        bdv,
        z,
        q,
        k,
        inverse,
        c_all,
        u_v,
        u_k,
        mixed_grad,
        states,
        end_grads,
        scratch=[pltpu.VMEM((TOK + HALO, PRE), f32)],
    )
    (pre_low,) = kernel_call(
        conv_back_kernel,
        [((TOK, PRE), bf16)],
        dz,
        shift(dz_first, -1),
        filt,
        scratch=[pltpu.VMEM((TOK + HALO, PRE), f32)],
    )
    beta_low = (scal_grad[:, :HEADS] * beta_rows * (1.0 - beta_rows)).astype(bf16)
    decay_grad = scal_grad[:, HEADS : 2 * HEADS]
    decay_pre_grad = decay_grad * decay_rate * jax.nn.sigmoid(decay_at)
    decay_low = decay_pre_grad.astype(bf16)
    log_grad = jnp.sum(decay_grad * decays, axis=0)
    bias_grad = jnp.sum(decay_pre_grad, axis=0)

    part = (
        dot_t(pre_low[:, :QK], w_query)
        + dot_t(pre_low[:, QK : 2 * QK], w_key)
        + dot_t(pre_low[:, 2 * QK :], w_value)
        + dot_t(gate_pre_low, w_outgate)
        + dot_t(beta_low, w_beta)
        + dot_t(decay_low, w_decay)
    ).astype(bf16)
    part = jnp.concatenate(
        [part, jnp.pad(gain_grad.astype(bf16), ((0, 15), (0, width - DV)))], axis=0
    )
    total = part.astype(f32) + swap_tensor(part).astype(f32)
    normed_grad = total[:TOK]
    gain_total = total[TOK, :DV]
    grad_norm_mix = jnp.sum(normed_grad * unit_mix, axis=0)
    grad_inputs = (middle_grad + norm_back(normed_grad, gain_mix, root_mix, unit_mix)).astype(bf16)

    late_sent = weight_grads(
        [(normed_low, jnp.where(first, pre_low[:, 2 * QK :], pre_low[:, : 2 * QK]))]
    )
    late = weight_grads(
        [(normed_low, jnp.where(first, pre_low[:, : 2 * QK], pre_low[:, 2 * QK :]))],
        [swap_core(late_sent)],
    )
    head_grads = jnp.concatenate([log_grad, bias_grad])
    head_high = head_grads.astype(bf16).astype(f32)
    head_parts = jnp.concatenate([head_high, head_grads - head_high])
    taps = filter_grad[0:4].T
    smalls = jnp.concatenate(
        [
            grad_norm_mix.reshape(SEQ, -1),
            grad_norm_ffn.reshape(SEQ, -1),
            gain_total.reshape(SEQ, -1),
            lax.dot_general(
                normed_low, beta_low, (((0,), (0,)), ((), ())), preferred_element_type=f32
            ).reshape(SEQ, -1),
            lax.dot_general(
                normed_low, decay_low, (((0,), (0,)), ((), ())), preferred_element_type=f32
            ).reshape(SEQ, -1),
            taps[:QK].reshape(SEQ, -1),
            taps[QK : 2 * QK].reshape(SEQ, -1),
            taps[2 * QK :].reshape(SEQ, -1),
            jnp.broadcast_to(head_parts, (SEQ, 4 * HEADS)),
        ],
        axis=1,
    ).astype(bf16)
    small_count = smalls.shape[1]
    smalls = jnp.pad(smalls, ((0, 0), (0, 2048 - small_count))).reshape(SEQ, 16, 128)
    late_rows = late.shape[1] + 16
    blocks = placed_call(
        spread_body,
        [(4, SPLIT, 128)] * 4 + [(4, late_rows - SPLIT, 128)] * 4,
        place,
        late,
        smalls,
        swap_core(smalls),
    )
    moved = [blocks[0]] + [lax.ppermute(blocks[s], "seq", along_x(s)) for s in range(1, 4)]
    moved += [blocks[4]] + [lax.ppermute(blocks[4 + s], "seq", along_z(s)) for s in range(1, 4)]
    blocks = placed_call(
        spread_again_body,
        [(SPLIT, 128)] * 4 + [(late_rows - SPLIT, 128)] * 4,
        place,
        *moved,
    )
    moved = [blocks[0]] + [lax.ppermute(blocks[s], "seq", along_z(s)) for s in range(1, 4)]
    moved += [blocks[4]] + [lax.ppermute(blocks[4 + s], "seq", along_x(s)) for s in range(1, 4)]
    (late,) = placed_call(gather_body, [(late_rows, 128)], place, *moved)

    early_first, early_second = over_dp(early.reshape(-1, 128))
    late_first, late_second = over_dp(late)
    gate_rows = 64 * (w_gate.shape[1] // 128)
    down_rows = 96 * (half // 128)
    grad_gate = tiles_to_rows(early_first[:gate_rows], 64, 64)
    grad_up = tiles_to_rows(early_second[:gate_rows], 64, 64)
    grad_down = jnp.concatenate(
        [
            tiles_to_rows(part_rows[gate_rows : gate_rows + down_rows], 88, 96)
            for part_rows in (early_first, early_second)
        ],
        axis=1,
    )
    grad_outgate = tiles_to_rows(early_first[gate_rows + down_rows :], 64, 64)
    grad_wout = tiles_to_rows(early_second[gate_rows + down_rows :], 64, 64)
    late_count = late_rows - 16
    grad_qk = tiles_to_rows(late_first[:late_count], 64, 64)
    grad_value = tiles_to_rows(late_second[:late_count], 64, 64)
    flat = late_first[late_count:].reshape(-1)

    sizes = [64, 64, 16, 64 * HEADS, 64 * HEADS, 32 * 4, 32 * 4, 64 * 4, 4 * HEADS]
    shares = []
    start = 0
    for size in sizes:
        shares.append(flat[start : start + size])
        start += size
    head_total = shares[8].astype(f32)
    head_total = (head_total[: 2 * HEADS] + head_total[2 * HEADS :]).astype(bf16)
    return (
        output.reshape(inputs.shape),
        grad_inputs.reshape(inputs.shape),
        shares[0],
        grad_qk[:, :QK],
        grad_qk[:, QK:],
        grad_value,
        grad_outgate,
        shares[3].reshape(64, HEADS),
        shares[4].reshape(64, HEADS),
        head_total[:HEADS],
        head_total[HEADS:],
        shares[5].reshape(32, 4),
        shares[6].reshape(32, 4),
        shares[7].reshape(64, 4),
        shares[2],
        grad_wout,
        shares[1],
        grad_gate,
        grad_up,
        grad_down,
    )


def solution(mesh):
    return jax.shard_map(
        per_device,
        mesh=mesh,
        in_specs=(
            P("dp", "seq", None),
            P("dp", "seq", None),
            P(),
            P(None, "tensor"),
            P(None, "tensor"),
            P(None, "tensor"),
            P(None, "tensor"),
            P(None, "tensor"),
            P(None, "tensor"),
            P("tensor"),
            P("tensor"),
            P("tensor", None),
            P("tensor", None),
            P("tensor", None),
            P(),
            P("tensor", None),
            P(),
            P(None, "tensor"),
            P(None, "tensor"),
            P("tensor", None),
        ),
        out_specs=(
            P("dp", "seq", None),
            P("dp", "seq", None),
            P("seq"),
            P("seq", "tensor"),
            P("seq", "tensor"),
            P("seq", "tensor"),
            P("seq", "tensor"),
            P("seq", "tensor"),
            P("seq", "tensor"),
            P("tensor"),
            P("tensor"),
            P(("tensor", "seq"), None),
            P(("tensor", "seq"), None),
            P(("tensor", "seq"), None),
            P("seq"),
            P(("tensor", "seq"), None),
            P("seq"),
            P("seq", "tensor"),
            P("seq", "tensor"),
            P(("tensor", "seq"), None),
        ),
        check_vma=False,
    )
```

time: 2210 us -> 292 us (0.13)
  waiting for transfers between devices: 1270 us -> 86.8 us
  other arithmetic: 277 us -> 14.1 us
  matrix products: 223 us -> 24.6 us
  blocking collectives: 184 us -> 0 us
  local copies, waits for them, and re-layouts: 119 us -> 41.4 us
  Pallas kernels: 0 us -> 46.1 us
  starting transfers between devices: 107 us -> 62 us
    reduce_scatter x7 -> x0, waiting for transfers between devices: 518 us -> none  [the longest x1 78.6 us: per_device(): lax.psum_scatter(members[14].astype(jnp.bfloat16), 'seq', scatter_dimensi...]
    unnamed x23 -> x2, waiting for transfers between devices: 279 us -> 0.02 us
    ppermute x32 -> x26, waiting for transfers between devices: 313 us -> 55.1 us  [the longest x2 16.2 us: swap_far(): return lax.ppermute(value, 'dp', [(0, 2), (2, 0), (1, 3), (3, 1)])]
    another operation x58 -> x2, other arithmetic: 221 us -> 0.15 us  [the longest x34 216 us: advance(): jax.scipy.linalg.solve_triangular(identity + lower_part, target, lower=Tr...]
    dot_general x112 -> x22, matrix products: 206 us -> 24.6 us  [the longest x10 12.7 us: dot(): return jnp.dot(a, b, preferred_element_type=f32)]
    psum x4 -> x0, waiting for transfers between devices: 159 us -> none  [the longest x1 63.4 us: per_device(): lax.psum(jnp.dot(gated_low, w_out, preferred_element_type=jnp.float32), '...]
    psum x3 -> x0, blocking collectives: 150 us -> none  [the longest x1 136 us: per_device(): head_totals = lax.psum((decay_log_grad, decay_bias_grad), ('dp', 'seq'))]
    ppermute x32 -> x26, starting transfers between devices: 106 us -> 43.5 us  [the longest x6 15.9 us: swap_core(): return lax.ppermute(value, 'dp', [(0, 1), (1, 0), (2, 3), (3, 2)])]
  transfers between devices with their start and end apart: 49 -> 31, of which waited for: 47 -> 18; matrix products, arithmetic and copies ran while one was open for 3% -> 13% of each run, Pallas kernels for 0% -> 7%
where the time goes in v1:
time: 292 us; the launch traced here: 290 us
  waiting for transfers between devices  86.8 us (30%)
  starting transfers between devices  62 us (21%)
  Pallas kernels  46.1 us (16%)
  local copies, waits for them, and re-layouts  41.4 us (14%)
  matrix products  24.6 us (8%)
  between operations  15.2 us (5%)
  other arithmetic  14.1 us (5%)
    pallas_call x12, Pallas kernels, kernel_call(): pl.pallas_call(body, out_shape=out_shape, in_specs=[pl.BlockSpec(memory_s...  43.9 us
    all_to_all x4, waiting for transfers between devices, exchange(): return lax.all_to_all(value, 'seq', 0, 0, tiled=True)  31.7 us
    unnamed x153, local copies, waits for them, and re-layouts  28.4 us
    all_to_all x4, starting transfers between devices, exchange(): return lax.all_to_all(value, 'seq', 0, 0, tiled=True)  18.4 us
    ppermute x2, waiting for transfers between devices, swap_far(): return lax.ppermute(value, 'dp', [(0, 2), (2, 0), (1, 3), (3, 1)])  16.2 us
    ppermute x6, starting transfers between devices, swap_core(): return lax.ppermute(value, 'dp', [(0, 1), (1, 0), (2, 3), (3, 2)])  15.9 us
    ppermute x4, waiting for transfers between devices, swap_tensor(): return lax.ppermute(value, 'tensor', [(0, 1), (1, 0)])  15.1 us
    ppermute x3, waiting for transfers between devices, per_device(): lax.ppermute(blocks[4 + s], 'seq', along_z(s))  12.9 us
  transfers between devices with their start and end apart: 31, of which 18 were waited for; matrix products, arithmetic and copies ran while one was open for 13% of the time, Pallas kernels for 7%

profile of v1, /device:TPU:1, one launch (start us, length us, event | category | flops | bytes accessed | tf_op | source)
XLA Modules:
  0.0 290.1 jit_solution(16401428732605076276)
XLA Ops:
  12.9 4.1 %collective-permute-start = (bf16[16,2048]{1,0:T(8,128)(2,1)S(1)}, bf16[16,2048]{1,0:T(8,128)(2,1)S(1)}, u32[]{:S(2)}, u32[]{:S(2)}) collective-permute-start(bf16[16,2048]{1,0:T(8,128)(2,1)S(1)} %slice.181), channel_id=1, source_target_pairs={{0,1},{1,2},{2,3},{3,4},{4,5},{5,6},{6,7},{7,8},{8,9},{9,10},{10,1... | collective-permute-start | bytes 196616 | tf_op jit(solution)/shard_map/ppermute | solution.py:494
  18.8 9.8 %shard_map.347 = (f32[128,2048]{1,0:T(8,128)S(1)}, bf16[128,512]{1,0:T(8,128)(2,1)S(1)}, bf16[128,512]{1,0:T(8,128)(2,1)S(1)}, f32[4,128,128]{2,1,0:T(8,128)S(1)...) custom-call(bf16[128,2048]{1,0:T(8,128)(2,1)S(1)} %pad_maximum_fusio, ...), custom_call_target="tpu_custom_call" | custom-call | bytes 4456448 | tf_op jit(solution)/shard_map/pallas_call | solution.py:31
  36.2 7.7 %all-to-all-start = ((bf16[16,192,128]{2,1,0:T(8,128)(2,1)}), bf16[16,192,128]{2,1,0:T(8,128)(2,1)}, u32[]{:S(2)}, u32[]{:S(2)}) async-start(bf16[16,192,128]{2,1,0:T(8,128)(2,1)} %copy-done.15), calls=%async_computation | async-start | bytes 1572864 | tf_op jit(solution)/shard_map/all_to_all | solution.py:498
  43.9 12.4 %all-to-all-done.maps = bf16[16,192,128]{2,1,0:T(8,128)(2,1)} async-done(((bf16[16,192,128]{2,1,0:T(8,128)(2,1)}), bf16[16,192,128]{2,1,0:T(8,128)(2,1)}, u32[]{:S(2)}, u32[]{:S(2)}) %all-to-all-start) | async-done | bytes 786464 | tf_op jit(solution)/shard_map/all_to_all | solution.py:498
  56.3 3.0 %shard_map.348 = bf16[16,64,128]{2,1,0:T(8,128)(2,1)S(1)} custom-call(bf16[16,192,128]{2,1,0:T(8,128)(2,1)} %all-to-all-done.maps), custom_call_target="tpu_custom_call" | custom-call | bytes 1048576 | tf_op jit(solution)/shard_map/pallas_call | solution.py:31
  60.0 3.5 %all-to-all-start.1 = ((bf16[16,64,128]{2,1,0:T(8,128)(2,1)}), bf16[16,64,128]{2,1,0:T(8,128)(2,1)S(1)}, u32[]{:S(2)}, u32[]{:S(2)}) async-start(bf16[16,64,128]{2,1,0:T(8,128)(2,1)} %copy-done.8), calls=%async_computation.1 | async-start | bytes 524288 | tf_op jit(solution)/shard_map/all_to_all | solution.py:498
  66.5 4.6 %all-to-all-done.1.st.st_i = bf16[16,64,128]{2,1,0:T(8,128)(2,1)S(1)} async-done(((bf16[16,64,128]{2,1,0:T(8,128)(2,1)}), bf16[16,64,128]{2,1,0:T(8,128)(2,1)S(1)}, u32[]{:S(2)}, u32[]{:S(2)}) %all-to-all-start.1) | async-done | bytes 262176 | tf_op jit(solution)/shard_map/all_to_all | solution.py:498
  80.2 3.2 %collective-permute-done.1 = bf16[128,1024]{1,0:T(8,128)(2,1)} collective-permute-done((bf16[128,1024]{1,0:T(8,128)(2,1)}, bf16[128,1024]{1,0:T(8,128)(2,1)}, u32[]{:S(2)}, u32[]{:S(2)}) %collective-permute-start.1) | collective-permute-done | bytes 262176 | tf_op jit(solution)/shard_map/ppermute | solution.py:481
  90.5 3.6 %shard_map.359 = bf16[16,1088,128]{2,1,0:T(8,128)(2,1)S(1)} custom-call(bf16[128,1024]{1,0:T(8,128)(2,1)S(1)} %multiply_convert_fusion.3.refs_0_, bf16[128,1408]{1,0:T(8,128)(2,1)S(1)} %get-tuple-element.176.refs_1_, bf16[128,1408]{1,0:T(8,128)(2,1)S(1)} %get-tuple-element.218.refs_2_, bf16[128,512]{1,0:T(8,128)(2,1)S(1)} %get-tuple-element.193.refs_3_), custom_call_target="tpu_custom_call" | custom-call | flops 570425344 | bytes 5570560 | tf_op jit(solution)/shard_map/pallas_call | solution.py:31
  94.1 5.5 %collective-permute-start.22 = (bf16[16,1088,128]{2,1,0:T(8,128)(2,1)S(1)}, bf16[16,1088,128]{2,1,0:T(8,128)(2,1)}, u32[]{:S(2)}, u32[]{:S(2)}) collective-permute-start(bf16[16,1088,128]{2,1,0:T(8,128)(2,1)S(1)} %shard_map.359), channel_id=1, source_target_pairs={{0,16},{16,0},{32,48},{48,32},{1,17},{17,1},{33,49},{49,33},{2,18}... | collective-permute-start | bytes 13369352 | tf_op jit(solution)/shard_map/ppermute | solution.py:485
  105.2 5.8 %collective-permute-done.3 = bf16[128,1024]{1,0:T(8,128)(2,1)S(1)} collective-permute-done((bf16[128,1024]{1,0:T(8,128)(2,1)S(1)}, bf16[128,1024]{1,0:T(8,128)(2,1)S(1)}, u32[]{:S(2)}, u32[]{:S(2)}) %collective-permute-start.3) | collective-permute-done | bytes 262176 | tf_op jit(solution)/shard_map/ppermute | solution.py:481
  111.3 5.4 %collective-permute-done.2 = bf16[128,1024]{1,0:T(8,128)(2,1)S(1)} collective-permute-done((bf16[128,1024]{1,0:T(8,128)(2,1)S(1)}, bf16[128,1024]{1,0:T(8,128)(2,1)S(1)}, u32[]{:S(2)}, u32[]{:S(2)}) %collective-permute-start.2) | collective-permute-done | bytes 262176 | tf_op jit(solution)/shard_map/ppermute | solution.py:481
  124.7 3.7 %collective-permute-done.23.refs_7_ = bf16[16,512,128]{2,1,0:T(8,128)(2,1)S(1)} collective-permute-done((bf16[16,512,128]{2,1,0:T(8,128)(2,1)S(1)}, bf16[16,512,128]{2,1,0:T(8,128)(2,1)S(1)}, u32[]{:S(2)}, u32[]{:S(2)}) %collective-permute-start.23) | collective-permute-done | bytes 2097184 | tf_op jit(solution)/shard_map/ppermute | solution.py:485
  128.4 10.4 %shard_map.361 = bf16[16,1600,128]{2,1,0:T(8,128)(2,1)} custom-call(bf16[128,1024]{1,0:T(8,128)(2,1)S(1)} %multiply_convert_fusion.3.refs_0_, bf16[128,1408]{1,0:T(8,128)(2,1)S(1)} %broadcast_select_fusion.3.refs_1_, bf16[128,1408]{1,0:T(8,128)(2,1)S(1)} %get-tuple-element.218.refs_2_, bf16[128,512]{1,0:T(8,128)(2,1)S(1)} %get-tuple-element.194.refs_3_, ...), custom_call_target="tpu_custom_call" | custom-call | flops 838860800 | bytes 14745600 | tf_op jit(solution)/shard_map/pallas_call | solution.py:31
  138.9 3.7 %all-to-all-start.2 = ((bf16[16,64,128]{2,1,0:T(8,128)(2,1)}), bf16[16,64,128]{2,1,0:T(8,128)(2,1)S(1)}, u32[]{:S(2)}, u32[]{:S(2)}) async-start(bf16[16,64,128]{2,1,0:T(8,128)(2,1)} %get-tuple-element.69), calls=%async_computation.2 | async-start | bytes 524288 | tf_op jit(solution)/shard_map/all_to_all | solution.py:498
  142.7 8.3 %all-to-all-done.2.grads = bf16[16,64,128]{2,1,0:T(8,128)(2,1)S(1)} async-done(((bf16[16,64,128]{2,1,0:T(8,128)(2,1)}), bf16[16,64,128]{2,1,0:T(8,128)(2,1)S(1)}, u32[]{:S(2)}, u32[]{:S(2)}) %all-to-all-start.2) | async-done | bytes 262176 | tf_op jit(solution)/shard_map/all_to_all | solution.py:498
  151.0 3.7 %shard_map.351 = bf16[16,64,128]{2,1,0:T(8,128)(2,1)} custom-call(bf16[16,64,128]{2,1,0:T(8,128)(2,1)S(1)} %all-to-all-done.2.grads, bf16[16,192,128]{2,1,0:T(8,128)(2,1)} %all-to-all-done.maps), custom_call_target="tpu_custom_call" | custom-call | bytes 1310720 | tf_op jit(solution)/shard_map/pallas_call | solution.py:31
  154.6 3.5 %all-to-all-start.3 = ((bf16[16,64,128]{2,1,0:T(8,128)(2,1)}), bf16[16,64,128]{2,1,0:T(8,128)(2,1)S(1)}, u32[]{:S(2)}, u32[]{:S(2)}) async-start(bf16[16,64,128]{2,1,0:T(8,128)(2,1)} %shard_map.351), calls=%async_computation.3 | async-start | bytes 524288 | tf_op jit(solution)/shard_map/all_to_all | solution.py:498
  158.2 3.4 %fusion.55 = f32[128,1024]{1,0:T(8,128)} fusion(bf16[128,1024]{1,0:T(8,128)(2,1)S(1)} %copy-done.12, bf16[1024,1024]{1,0:T(8,128)(2,1)} %param.26), kind=kOutput, calls=%fused_computation.134 | convolution fusion | flops 268435456 | bytes 2883584 | tf_op jit(solution)/shard_map/dot_general | solution.py:520
  161.5 6.3 %all-to-all-done.3.gt_i = bf16[16,64,128]{2,1,0:T(8,128)(2,1)S(1)} async-done(((bf16[16,64,128]{2,1,0:T(8,128)(2,1)}), bf16[16,64,128]{2,1,0:T(8,128)(2,1)S(1)}, u32[]{:S(2)}, u32[]{:S(2)}) %all-to-all-start.3) | async-done | bytes 262176 | tf_op jit(solution)/shard_map/all_to_all | solution.py:498
  177.2 3.6 %shard_map.352 = (f32[128,2048]{1,0:T(8,128)S(1)}, bf16[16,2048]{1,0:T(8,128)(2,1)S(1)}, f32[8,2048]{1,0:T(8,128)S(1)}, f32[128,128]{1,0:T(8,128)S(1)}) custom-call(bf16[128,2048]{1,0:T(8,128)(2,1)S(1)} %copy-done.3, bf16[16,2048]{1,0:T(8,128)(2,1)S(1)} %copy-done.30, f32[8,2048]{1,0:T(8,128)S(1)} %pad_convert_fusion.filt, ...), custom_call_target="tpu_custom_call" | custom-call | bytes 5046272 | tf_op jit(solution)/shard_map/pallas_call | solution.py:31
  184.0 3.2 %collective-permute-done.4.after = bf16[16,2048]{1,0:T(8,128)(2,1)S(1)} collective-permute-done((bf16[16,2048]{1,0:T(8,128)(2,1)S(1)}, bf16[16,2048]{1,0:T(8,128)(2,1)S(1)}, u32[]{:S(2)}, u32[]{:S(2)}) %collective-permute-start.4) | collective-permute-done | bytes 65568 | tf_op jit(solution)/shard_map/ppermute | solution.py:494
  190.0 3.2 %collective-permute-start.6 = (bf16[16,512,128]{2,1,0:T(8,128)(2,1)S(1)}, bf16[16,512,128]{2,1,0:T(8,128)(2,1)}, u32[]{:S(2)}, u32[]{:S(2)}) collective-permute-start(bf16[16,512,128]{2,1,0:T(8,128)(2,1)S(1)} %shard_map.354), channel_id=1, source_target_pairs={{0,16},{16,0},{32,48},{48,32},{1,17},{17,1},{33,49},{49,33},{2,18}... | collective-permute-start | bytes 6291464 | tf_op jit(solution)/shard_map/ppermute | solution.py:485
  208.9 3.5 %shard_map.355.kept = bf16[16,512,128]{2,1,0:T(8,128)(2,1)S(1)} custom-call(bf16[128,1024]{1,0:T(8,128)(2,1)S(1)} %fusion.15.refs_0_, bf16[128,1024]{1,0:T(8,128)(2,1)S(1)} %get-tuple-element.190.refs_1_, bf16[16,512,128]{2,1,0:T(8,128)(2,1)} %collective-permute-done.6.refs_2_), custom_call_target="tpu_custom_call" | custom-call | flops 268435456 | bytes 4718592 | tf_op jit(solution)/shard_map/pallas_call | solution.py:31
  213.2 3.8 %collective-permute-start.9 = (bf16[4,272,128]{2,1,0:T(8,128)(2,1)S(1)}, bf16[4,272,128]{2,1,0:T(8,128)(2,1)S(1)}, u32[]{:S(2)}, u32[]{:S(2)}) collective-permute-start(bf16[4,272,128]{2,1,0:T(8,128)(2,1)S(1)} %get-tuple-element.78), channel_id=1, source_target_pairs={{0,2},{1,3},{2,0},{3,1},{4,6},{5,7},{6,4},{7,5},{8,10},{9,11},{10,... | collective-permute-start | bytes 835592 | tf_op jit(solution)/shard_map/ppermute | solution.py:775
  218.5 5.6 %collective-permute-done.11.refs_5_ = bf16[4,256,128]{2,1,0:T(8,128)(2,1)S(1)} collective-permute-done((bf16[4,256,128]{2,1,0:T(8,128)(2,1)S(1)}, bf16[4,256,128]{2,1,0:T(8,128)(2,1)S(1)}, u32[]{:S(2)}, u32[]{:S(2)}) %collective-permute-start.11) | collective-permute-done | bytes 262176 | tf_op jit(solution)/shard_map/ppermute | solution.py:776
  224.4 5.3 %collective-permute-done.12.refs_6_ = bf16[4,256,128]{2,1,0:T(8,128)(2,1)S(1)} collective-permute-done((bf16[4,256,128]{2,1,0:T(8,128)(2,1)S(1)}, bf16[4,256,128]{2,1,0:T(8,128)(2,1)S(1)}, u32[]{:S(2)}, u32[]{:S(2)}) %collective-permute-start.12) | collective-permute-done | bytes 262176 | tf_op jit(solution)/shard_map/ppermute | solution.py:776
  232.7 3.2 %collective-permute-start.14 = (bf16[272,128]{1,0:T(8,128)(2,1)S(1)}, bf16[272,128]{1,0:T(8,128)(2,1)S(1)}, u32[]{:S(2)}, u32[]{:S(2)}) collective-permute-start(bf16[272,128]{1,0:T(8,128)(2,1)S(1)} %get-tuple-element.85), channel_id=1, source_target_pairs={{0,4},{1,5},{2,6},{3,7},{4,8},{5,9},{6,10},{7,11},{8,12},{9,13},{1... | collective-permute-start | bytes 208904 | tf_op jit(solution)/shard_map/ppermute | solution.py:783
  238.2 6.2 %collective-permute-start.18 = (bf16[256,128]{1,0:T(8,128)(2,1)S(1)}, bf16[256,128]{1,0:T(8,128)(2,1)S(1)}, u32[]{:S(2)}, u32[]{:S(2)}) collective-permute-start(bf16[256,128]{1,0:T(8,128)(2,1)S(1)} %get-tuple-element.90), channel_id=1, source_target_pairs={{0,2},{1,3},{2,0},{3,1},{4,6},{5,7},{6,4},{7,5},{8,10},{9,11},{10,... | collective-permute-start | bytes 196616 | tf_op jit(solution)/shard_map/ppermute | solution.py:784
  249.0 5.3 %collective-permute-done.20 = bf16[528,128]{1,0:T(8,128)(2,1)S(1)} collective-permute-done((bf16[528,128]{1,0:T(8,128)(2,1)S(1)}, bf16[528,128]{1,0:T(8,128)(2,1)S(1)}, u32[]{:S(2)}, u32[]{:S(2)}) %collective-permute-start.20) | collective-permute-done | bytes 135200 | tf_op jit(solution)/shard_map/ppermute | solution.py:489
  254.4 4.1 %collective-permute-start.21 = (bf16[528,128]{1,0:T(8,128)(2,1)S(1)}, bf16[528,128]{1,0:T(8,128)(2,1)S(1)}, u32[]{:S(2)}, u32[]{:S(2)}) collective-permute-start(bf16[528,128]{1,0:T(8,128)(2,1)S(1)} %add_convert_fusion.2), channel_id=1, source_target_pairs={{0,16},{16,0},{32,48},{48,32},{1,17},{17,1},{33,49},{49,33},{2,18}... | collective-permute-start | bytes 405512 | tf_op jit(solution)/shard_map/ppermute | solution.py:485
  266.0 10.8 %collective-permute-done.24 = bf16[1600,128]{1,0:T(8,128)(2,1)S(1)} collective-permute-done((bf16[1600,128]{1,0:T(8,128)(2,1)}, bf16[1600,128]{1,0:T(8,128)(2,1)S(1)}, u32[]{:S(2)}, u32[]{:S(2)}) %collective-permute-start.24) | collective-permute-done | bytes 409632 | tf_op jit(solution)/shard_map/ppermute | solution.py:489
  (303 shorter events, 105.4 us)
Async XLA Ops:
  7.2 81.0 %copy-start = (bf16[1408,1024]{1,0:T(8,128)(2,1)S(1)}, bf16[1408,1024]{1,0:T(8,128)(2,1)}, u32[]{:S(2)}) copy-start(bf16[1408,1024]{1,0:T(8,128)(2,1)} %param.39) | copy-start | bytes 8650756
  12.9 5.9 %collective-permute-start = (bf16[16,2048]{1,0:T(8,128)(2,1)S(1)}, bf16[16,2048]{1,0:T(8,128)(2,1)S(1)}, u32[]{:S(2)}, u32[]{:S(2)}) collective-permute-start(bf16[16,2048]{1,0:T(8,128)(2,1)S(1)} %slice.181), channel_id=1, source_target_pairs={{0,1},{1,2},{2,3},{3,4},{4,5},{5,6},{6,7},{7,8},{8,9},{9,10},{10,1... | collective-permute-start | bytes 196616 | tf_op jit(solution)/shard_map/ppermute | solution.py:494
  36.2 20.2 %all-to-all-start = ((bf16[16,192,128]{2,1,0:T(8,128)(2,1)}), bf16[16,192,128]{2,1,0:T(8,128)(2,1)}, u32[]{:S(2)}, u32[]{:S(2)}) async-start(bf16[16,192,128]{2,1,0:T(8,128)(2,1)} %copy-done.15), calls=%async_computation | async-start | bytes 1572864 | tf_op jit(solution)/shard_map/all_to_all | solution.py:498
  60.0 11.0 %all-to-all-start.1 = ((bf16[16,64,128]{2,1,0:T(8,128)(2,1)}), bf16[16,64,128]{2,1,0:T(8,128)(2,1)S(1)}, u32[]{:S(2)}, u32[]{:S(2)}) async-start(bf16[16,64,128]{2,1,0:T(8,128)(2,1)} %copy-done.8), calls=%async_computation.1 | async-start | bytes 524288 | tf_op jit(solution)/shard_map/all_to_all | solution.py:498
  63.6 200.8 %reduce-scatter.4.cloned.1.call-start = ((), (), s32[]{:S(2)}) async-start(), calls=%async_computation.5 | async-start | bytes 6963200
  77.9 5.5 %collective-permute-start.1 = (bf16[128,1024]{1,0:T(8,128)(2,1)}, bf16[128,1024]{1,0:T(8,128)(2,1)}, u32[]{:S(2)}, u32[]{:S(2)}) collective-permute-start(bf16[128,1024]{1,0:T(8,128)(2,1)} %convolution_convert_fusion.1), channel_id=1, source_target_pairs={{0,64},{64,0},{1,65},{65,1},{2,66},{66,2},{3,67},{67,3},{4,68},{68... | collective-permute-start | bytes 786440 | tf_op jit(solution)/shard_map/ppermute | solution.py:481
  94.1 34.3 %collective-permute-start.22 = (bf16[16,1088,128]{2,1,0:T(8,128)(2,1)S(1)}, bf16[16,1088,128]{2,1,0:T(8,128)(2,1)}, u32[]{:S(2)}, u32[]{:S(2)}) collective-permute-start(bf16[16,1088,128]{2,1,0:T(8,128)(2,1)S(1)} %shard_map.359), channel_id=1, source_target_pairs={{0,16},{16,0},{32,48},{48,32},{1,17},{17,1},{33,49},{49,33},{2,18}... | collective-permute-start | bytes 13369352 | tf_op jit(solution)/shard_map/ppermute | solution.py:485
  103.0 8.0 %collective-permute-start.3 = (bf16[128,1024]{1,0:T(8,128)(2,1)S(1)}, bf16[128,1024]{1,0:T(8,128)(2,1)S(1)}, u32[]{:S(2)}, u32[]{:S(2)}) collective-permute-start(bf16[128,1024]{1,0:T(8,128)(2,1)S(1)} %fusion.5), channel_id=1, source_target_pairs={{0,64},{64,0},{1,65},{65,1},{2,66},{66,2},{3,67},{67,3},{4,68},{68... | collective-permute-start | bytes 786440 | tf_op jit(solution)/shard_map/ppermute | solution.py:481
  105.0 11.6 %collective-permute-start.2 = (bf16[128,1024]{1,0:T(8,128)(2,1)S(1)}, bf16[128,1024]{1,0:T(8,128)(2,1)S(1)}, u32[]{:S(2)}, u32[]{:S(2)}) collective-permute-start(bf16[128,1024]{1,0:T(8,128)(2,1)S(1)} %convolution_convert_fusion), channel_id=1, source_target_pairs={{0,64},{64,0},{1,65},{65,1},{2,66},{66,2},{3,67},{67,3},{4,68},{68... | collective-permute-start | bytes 786440 | tf_op jit(solution)/shard_map/ppermute | solution.py:481
  123.7 4.7 %collective-permute-start.23 = (bf16[16,512,128]{2,1,0:T(8,128)(2,1)S(1)}, bf16[16,512,128]{2,1,0:T(8,128)(2,1)S(1)}, u32[]{:S(2)}, u32[]{:S(2)}) collective-permute-start(bf16[16,512,128]{2,1,0:T(8,128)(2,1)S(1)} %shard_map.360), channel_id=1, source_target_pairs={{0,16},{16,0},{32,48},{48,32},{1,17},{17,1},{33,49},{49,33},{2,18}... | collective-permute-start | bytes 6291464 | tf_op jit(solution)/shard_map/ppermute | solution.py:485
  138.9 12.1 %all-to-all-start.2 = ((bf16[16,64,128]{2,1,0:T(8,128)(2,1)}), bf16[16,64,128]{2,1,0:T(8,128)(2,1)S(1)}, u32[]{:S(2)}, u32[]{:S(2)}) async-start(bf16[16,64,128]{2,1,0:T(8,128)(2,1)} %get-tuple-element.69), calls=%async_computation.2 | async-start | bytes 524288 | tf_op jit(solution)/shard_map/all_to_all | solution.py:498
  154.6 13.2 %all-to-all-start.3 = ((bf16[16,64,128]{2,1,0:T(8,128)(2,1)}), bf16[16,64,128]{2,1,0:T(8,128)(2,1)S(1)}, u32[]{:S(2)}, u32[]{:S(2)}) async-start(bf16[16,64,128]{2,1,0:T(8,128)(2,1)} %shard_map.351), calls=%async_computation.3 | async-start | bytes 524288 | tf_op jit(solution)/shard_map/all_to_all | solution.py:498
  180.9 6.3 %collective-permute-start.4 = (bf16[16,2048]{1,0:T(8,128)(2,1)S(1)}, bf16[16,2048]{1,0:T(8,128)(2,1)S(1)}, u32[]{:S(2)}, u32[]{:S(2)}) collective-permute-start(bf16[16,2048]{1,0:T(8,128)(2,1)S(1)} %get-tuple-element.71), channel_id=1, source_target_pairs={{1,0},{2,1},{3,2},{4,3},{5,4},{6,5},{7,6},{8,7},{9,8},{10,9},{11,1... | collective-permute-start | bytes 196616 | tf_op jit(solution)/shard_map/ppermute | solution.py:494
  190.0 18.9 %collective-permute-start.6 = (bf16[16,512,128]{2,1,0:T(8,128)(2,1)S(1)}, bf16[16,512,128]{2,1,0:T(8,128)(2,1)}, u32[]{:S(2)}, u32[]{:S(2)}) collective-permute-start(bf16[16,512,128]{2,1,0:T(8,128)(2,1)S(1)} %shard_map.354), channel_id=1, source_target_pairs={{0,16},{16,0},{32,48},{48,32},{1,17},{17,1},{33,49},{49,33},{2,18}... | collective-permute-start | bytes 6291464 | tf_op jit(solution)/shard_map/ppermute | solution.py:485
  195.8 8.9 %collective-permute-start.5 = (bf16[144,1024]{1,0:T(8,128)(2,1)}, bf16[144,1024]{1,0:T(8,128)(2,1)}, u32[]{:S(2)}, u32[]{:S(2)}) collective-permute-start(bf16[144,1024]{1,0:T(8,128)(2,1)} %fusion.24), channel_id=1, source_target_pairs={{0,64},{64,0},{1,65},{65,1},{2,66},{66,2},{3,67},{67,3},{4,68},{68... | collective-permute-start | bytes 884744 | tf_op jit(solution)/shard_map/ppermute | solution.py:481
  207.9 4.5 %collective-permute-start.7 = (bf16[16,16,128]{2,1,0:T(8,128)(2,1)S(1)}, bf16[16,16,128]{2,1,0:T(8,128)(2,1)S(1)}, u32[]{:S(2)}, u32[]{:S(2)}) collective-permute-start(bf16[16,16,128]{2,1,0:T(8,128)(2,1)S(1)} %bitcast.125), channel_id=1, source_target_pairs={{0,16},{16,0},{32,48},{48,32},{1,17},{17,1},{33,49},{49,33},{2,18}... | collective-permute-start | bytes 196616 | tf_op jit(solution)/shard_map/ppermute | solution.py:485
  213.1 11.0 %collective-permute-start.11 = (bf16[4,256,128]{2,1,0:T(8,128)(2,1)S(1)}, bf16[4,256,128]{2,1,0:T(8,128)(2,1)S(1)}, u32[]{:S(2)}, u32[]{:S(2)}) collective-permute-start(bf16[4,256,128]{2,1,0:T(8,128)(2,1)S(1)} %get-tuple-element.81), channel_id=1, source_target_pairs={{0,4},{1,5},{2,6},{3,7},{4,8},{5,9},{6,10},{7,11},{8,12},{9,13},{1... | collective-permute-start | bytes 786440 | tf_op jit(solution)/shard_map/ppermute | solution.py:776
  213.2 18.5 %collective-permute-start.8 = (bf16[4,272,128]{2,1,0:T(8,128)(2,1)S(1)}, bf16[4,272,128]{2,1,0:T(8,128)(2,1)S(1)}, u32[]{:S(2)}, u32[]{:S(2)}) collective-permute-start(bf16[4,272,128]{2,1,0:T(8,128)(2,1)S(1)} %get-tuple-element.77), channel_id=1, source_target_pairs={{0,1},{1,2},{2,3},{3,0},{4,5},{5,6},{6,7},{7,4},{8,9},{9,10},{10,1... | collective-permute-start | bytes 835592 | tf_op jit(solution)/shard_map/ppermute | solution.py:775
  213.2 18.5 %collective-permute-start.9 = (bf16[4,272,128]{2,1,0:T(8,128)(2,1)S(1)}, bf16[4,272,128]{2,1,0:T(8,128)(2,1)S(1)}, u32[]{:S(2)}, u32[]{:S(2)}) collective-permute-start(bf16[4,272,128]{2,1,0:T(8,128)(2,1)S(1)} %get-tuple-element.78), channel_id=1, source_target_pairs={{0,2},{1,3},{2,0},{3,1},{4,6},{5,7},{6,4},{7,5},{8,10},{9,11},{10,... | collective-permute-start | bytes 835592 | tf_op jit(solution)/shard_map/ppermute | solution.py:775
  217.1 14.6 %collective-permute-start.10 = (bf16[4,272,128]{2,1,0:T(8,128)(2,1)S(1)}, bf16[4,272,128]{2,1,0:T(8,128)(2,1)S(1)}, u32[]{:S(2)}, u32[]{:S(2)}) collective-permute-start(bf16[4,272,128]{2,1,0:T(8,128)(2,1)S(1)} %get-tuple-element.79), channel_id=1, source_target_pairs={{0,3},{1,0},{2,1},{3,2},{4,7},{5,4},{6,5},{7,6},{8,11},{9,8},{10,9... | collective-permute-start | bytes 835592 | tf_op jit(solution)/shard_map/ppermute | solution.py:775
  217.1 12.6 %collective-permute-start.12 = (bf16[4,256,128]{2,1,0:T(8,128)(2,1)S(1)}, bf16[4,256,128]{2,1,0:T(8,128)(2,1)S(1)}, u32[]{:S(2)}, u32[]{:S(2)}) collective-permute-start(bf16[4,256,128]{2,1,0:T(8,128)(2,1)S(1)} %get-tuple-element.82), channel_id=1, source_target_pairs={{0,8},{1,9},{2,10},{3,11},{4,12},{5,13},{6,14},{7,15},{8,0},{9,1},... | collective-permute-start | bytes 786440 | tf_op jit(solution)/shard_map/ppermute | solution.py:776
  224.1 7.6 %collective-permute-start.13 = (bf16[4,256,128]{2,1,0:T(8,128)(2,1)S(1)}, bf16[4,256,128]{2,1,0:T(8,128)(2,1)S(1)}, u32[]{:S(2)}, u32[]{:S(2)}) collective-permute-start(bf16[4,256,128]{2,1,0:T(8,128)(2,1)S(1)} %get-tuple-element.83), channel_id=1, source_target_pairs={{0,12},{1,13},{2,14},{3,15},{4,0},{5,1},{6,2},{7,3},{8,4},{9,5},{1... | collective-permute-start | bytes 786440 | tf_op jit(solution)/shard_map/ppermute | solution.py:776
  232.6 11.9 %collective-permute-start.17 = (bf16[256,128]{1,0:T(8,128)(2,1)S(1)}, bf16[256,128]{1,0:T(8,128)(2,1)S(1)}, u32[]{:S(2)}, u32[]{:S(2)}) collective-permute-start(bf16[256,128]{1,0:T(8,128)(2,1)S(1)} %get-tuple-element.89), channel_id=1, source_target_pairs={{0,1},{1,2},{2,3},{3,0},{4,5},{5,6},{6,7},{7,4},{8,9},{9,10},{10,1... | collective-permute-start | bytes 196616 | tf_op jit(solution)/shard_map/ppermute | solution.py:784
  232.7 15.6 %collective-permute-start.14 = (bf16[272,128]{1,0:T(8,128)(2,1)S(1)}, bf16[272,128]{1,0:T(8,128)(2,1)S(1)}, u32[]{:S(2)}, u32[]{:S(2)}) collective-permute-start(bf16[272,128]{1,0:T(8,128)(2,1)S(1)} %get-tuple-element.85), channel_id=1, source_target_pairs={{0,4},{1,5},{2,6},{3,7},{4,8},{5,9},{6,10},{7,11},{8,12},{9,13},{1... | collective-permute-start | bytes 208904 | tf_op jit(solution)/shard_map/ppermute | solution.py:783
  235.8 12.4 %collective-permute-start.15 = (bf16[272,128]{1,0:T(8,128)(2,1)S(1)}, bf16[272,128]{1,0:T(8,128)(2,1)S(1)}, u32[]{:S(2)}, u32[]{:S(2)}) collective-permute-start(bf16[272,128]{1,0:T(8,128)(2,1)S(1)} %get-tuple-element.86), channel_id=1, source_target_pairs={{0,8},{1,9},{2,10},{3,11},{4,12},{5,13},{6,14},{7,15},{8,0},{9,1},... | collective-permute-start | bytes 208904 | tf_op jit(solution)/shard_map/ppermute | solution.py:783
  237.2 11.1 %collective-permute-start.16 = (bf16[272,128]{1,0:T(8,128)(2,1)S(1)}, bf16[272,128]{1,0:T(8,128)(2,1)S(1)}, u32[]{:S(2)}, u32[]{:S(2)}) collective-permute-start(bf16[272,128]{1,0:T(8,128)(2,1)S(1)} %get-tuple-element.87), channel_id=1, source_target_pairs={{0,12},{1,13},{2,14},{3,15},{4,0},{5,1},{6,2},{7,3},{8,4},{9,5},{1... | collective-permute-start | bytes 208904 | tf_op jit(solution)/shard_map/ppermute | solution.py:783
  238.2 7.9 %collective-permute-start.18 = (bf16[256,128]{1,0:T(8,128)(2,1)S(1)}, bf16[256,128]{1,0:T(8,128)(2,1)S(1)}, u32[]{:S(2)}, u32[]{:S(2)}) collective-permute-start(bf16[256,128]{1,0:T(8,128)(2,1)S(1)} %get-tuple-element.90), channel_id=1, source_target_pairs={{0,2},{1,3},{2,0},{3,1},{4,6},{5,7},{6,4},{7,5},{8,10},{9,11},{10,... | collective-permute-start | bytes 196616 | tf_op jit(solution)/shard_map/ppermute | solution.py:784
  244.5 3.8 %collective-permute-start.19 = (bf16[256,128]{1,0:T(8,128)(2,1)S(1)}, bf16[256,128]{1,0:T(8,128)(2,1)S(1)}, u32[]{:S(2)}, u32[]{:S(2)}) collective-permute-start(bf16[256,128]{1,0:T(8,128)(2,1)S(1)} %get-tuple-element.91), channel_id=1, source_target_pairs={{0,3},{1,0},{2,1},{3,2},{4,7},{5,4},{6,5},{7,6},{8,11},{9,8},{10,9... | collective-permute-start | bytes 196616 | tf_op jit(solution)/shard_map/ppermute | solution.py:784
  248.9 5.4 %collective-permute-start.20 = (bf16[528,128]{1,0:T(8,128)(2,1)S(1)}, bf16[528,128]{1,0:T(8,128)(2,1)S(1)}, u32[]{:S(2)}, u32[]{:S(2)}) collective-permute-start(bf16[528,128]{1,0:T(8,128)(2,1)S(1)} %shard_map.358), channel_id=1, source_target_pairs={{0,32},{32,0},{16,48},{48,16},{1,33},{33,1},{17,49},{49,17},{2,34}... | collective-permute-start | bytes 405512 | tf_op jit(solution)/shard_map/ppermute | solution.py:489
  254.4 5.1 %collective-permute-start.21 = (bf16[528,128]{1,0:T(8,128)(2,1)S(1)}, bf16[528,128]{1,0:T(8,128)(2,1)S(1)}, u32[]{:S(2)}, u32[]{:S(2)}) collective-permute-start(bf16[528,128]{1,0:T(8,128)(2,1)S(1)} %add_convert_fusion.2), channel_id=1, source_target_pairs={{0,16},{16,0},{32,48},{48,32},{1,17},{17,1},{33,49},{49,33},{2,18}... | collective-permute-start | bytes 405512 | tf_op jit(solution)/shard_map/ppermute | solution.py:485
  264.4 12.4 %collective-permute-start.24 = (bf16[1600,128]{1,0:T(8,128)(2,1)}, bf16[1600,128]{1,0:T(8,128)(2,1)S(1)}, u32[]{:S(2)}, u32[]{:S(2)}) collective-permute-start(bf16[1600,128]{1,0:T(8,128)(2,1)} %bitcast.139), channel_id=1, source_target_pairs={{0,32},{32,0},{16,48},{48,16},{1,33},{33,1},{17,49},{49,17},{2,34}... | collective-permute-start | bytes 1228808 | tf_op jit(solution)/shard_map/ppermute | solution.py:489
  277.9 2.6 collective-permute-start.25
  (72 other events, 425.3 us)
Sparse Core Ops, SparseCore 0:
  139.0 81.1 reduce-scatter.3

commit v2 on v1

v2 whole, which is shorter than its diff:
```python
import functools
import math

import jax
import jax.numpy as jnp
from jax import lax
from jax.experimental import pallas as pl
from jax.experimental.pallas import tpu as pltpu
from jax.sharding import PartitionSpec as P

f32 = jnp.float32
bf16 = jnp.bfloat16
epsilon = 1e-05
smallest = 1e-06
TOK = 128
HEADS = 4
DK = 128
DV = 256
QK = HEADS * DK
VW = HEADS * DV
PRE = 2 * QK + VW
SEQ = 16
HALO = 16
MIB = 1024 * 1024


def kernel_call(body, outs, *args, scratch=(), spare=4 * MIB, flops=0, far=(), far_outs=(), main=()):
    out_shape = [
        pltpu.HBM(shape, kind) if n in far_outs or n in main else jax.ShapeDtypeStruct(shape, kind)
        for n, (shape, kind) in enumerate(outs)
    ]
    moved = sum(a.size * a.dtype.itemsize for a in args)
    for shape, kind in outs:
        moved += math.prod(shape) * jnp.dtype(kind).itemsize
    limit = moved + spare
    return pl.pallas_call(
        body,
        out_shape=out_shape,
        in_specs=[
            pl.BlockSpec(memory_space=pltpu.HBM if n in far else pltpu.VMEM)
            for n in range(len(args))
        ],
        out_specs=[
            pl.BlockSpec(memory_space=pltpu.HBM if n in far_outs else pltpu.VMEM)
            for n in range(len(outs))
        ],
        scratch_shapes=list(scratch),
        compiler_params=pltpu.CompilerParams(vmem_limit_bytes=limit),
        cost_estimate=pl.CostEstimate(flops=flops, bytes_accessed=moved, transcendentals=0),
    )(*args)


def mm(a, b):
    return jnp.dot(a.astype(bf16), b.astype(bf16), preferred_element_type=f32)


def mt(a, b):
    return lax.dot_general(
        a.astype(bf16), b.astype(bf16), (((1,), (1,)), ((), ())), preferred_element_type=f32
    )


def tm(a, b):
    return lax.dot_general(
        a.astype(bf16), b.astype(bf16), (((0,), (0,)), ((), ())), preferred_element_type=f32
    )


def halves(a):
    high = a.astype(bf16)
    return high, (a - high.astype(f32)).astype(bf16)


def mm3(a, b):
    ah, al = halves(a)
    bh, bl = halves(b)
    return mm(jnp.concatenate([ah, al, ah], axis=1), jnp.concatenate([bh, bh, bl], axis=0))


def mm2(a, b):
    ah, al = halves(a)
    return mm(jnp.concatenate([ah, al], axis=1), jnp.concatenate([b, b], axis=0))


def thirds(a):
    high = a.astype(bf16)
    rest = a - high.astype(f32)
    mid = rest.astype(bf16)
    return high, mid, (rest - mid.astype(f32)).astype(bf16)


def masks():
    rows = lax.broadcasted_iota(jnp.int32, (TOK, TOK), 0)
    cols = lax.broadcasted_iota(jnp.int32, (TOK, TOK), 1)
    return rows, cols


def sigmoid(v):
    return 1.0 / (1.0 + jnp.exp(-v))


def fading_of(c_col, c_row, inclusive):
    return jnp.where(inclusive, jnp.exp(jnp.where(inclusive, c_col - c_row, 0.0)), 0.0)


AT_Q = PRE
AT_K = PRE + QK
AT_U = PRE + 2 * QK
KEPT_LOW = ((TOK + HALO, PRE + 3 * QK), bf16)
AT_X = VW
AT_C = VW + QK
AT_B = AT_C + TOK
AT_S = AT_B + TOK
KEPT = ((TOK + 8, PRE), f32)


def front_kernel(
    pre, halo, filt, bdv, slopes, low_hbm, kept_hbm, out_o, send_o, ext, low_o, kept_o, sems
):
    low_o[0:HALO, 0:PRE] = halo[...]
    low_o[HALO:, 0:PRE] = pre[...]
    low_o[TOK:, PRE:] = jnp.zeros((HALO, 3 * QK), bf16)
    ext[0:HALO] = halo[...].astype(f32)
    ext[HALO:] = pre[...].astype(f32)
    kept_o[TOK:, :] = filt[...]
    kept_o[0:TOK, AT_B : AT_B + TOK] = bdv[...]
    kept_o[0:TOK, AT_S : AT_S + TOK] = slopes[...]
    kept_o[0:TOK, AT_S + TOK :] = jnp.zeros((TOK, PRE - AT_S - TOK), f32)

    def activated(at, width):
        z = ext[pl.ds(HALO - 3, TOK), at : at + width] * filt[0:1, at : at + width]
        for j in range(1, 4):
            z = z + ext[pl.ds(HALO - 3 + j, TOK), at : at + width] * filt[j : j + 1, at : at + width]
        return z * sigmoid(z)

    rows, cols = masks()
    inclusive = rows >= cols
    strict = rows > cols
    lower = jnp.where(inclusive, 1.0, 0.0).astype(bf16)
    eye = jnp.where(rows == cols, 1.0, 0.0)
    scal = bdv[...]
    c_all = mm(
        jnp.concatenate([lower, lower, lower], axis=1), jnp.concatenate(thirds(scal), axis=0)
    )
    kept_o[0:TOK, AT_C : AT_C + TOK] = c_all
    c_t = c_all.T
    b_t = scal.T
    heads = range(HEADS)
    qs, ks, vs, lows, invs, fadings = [], [], [], [], [], []
    for h in heads:
        a_q = activated(h * DK, DK)
        a_k = activated(QK + h * DK, DK)
        q = (
            a_q
            * lax.rsqrt(jnp.sum(a_q * a_q, axis=1, keepdims=True) + smallest)
            * DK ** (-0.5)
        ).astype(bf16)
        k = (a_k * lax.rsqrt(jnp.sum(a_k * a_k, axis=1, keepdims=True) + smallest)).astype(bf16)
        low_o[0:TOK, AT_Q + h * DK : AT_Q + (h + 1) * DK] = q
        low_o[0:TOK, AT_K + h * DK : AT_K + (h + 1) * DK] = k
        qs.append(q)
        ks.append(k)
        fading = fading_of(
            c_all[:, HEADS + h : HEADS + h + 1], c_t[HEADS + h : HEADS + h + 1, :], inclusive
        )
        fadings.append(fading)
        lows.append(jnp.where(strict, fading * b_t[h : h + 1, :] * mt(k, k), 0.0))
    pairs = (rows // 2 == cols // 2) & strict
    invs = [eye - jnp.where(pairs, low, 0.0) for low in lows]
    size = 2
    while size < TOK:
        part = (
            (rows // (2 * size) == cols // (2 * size))
            & (rows // size % 2 == 1)
            & (cols // size % 2 == 0)
        )
        steps = [mm3(jnp.where(part, lows[h], 0.0), invs[h]) for h in heads]
        invs = [invs[h] - mm3(invs[h], steps[h]) for h in heads]
        size *= 2
    vs = [activated(2 * QK + h * DV, DV).astype(bf16) for h in heads]
    u_vs = [mm2(invs[h], vs[h]) for h in heads]
    u_ks = [mm2(invs[h] * jnp.exp(c_t[HEADS + h : HEADS + h + 1, :]), ks[h]) for h in heads]
    for h in heads:
        u_v, u_k, q, k = u_vs[h], u_ks[h], qs[h], ks[h]
        c_col = c_all[:, HEADS + h : HEADS + h + 1]
        b_col = scal[:, h : h + 1]
        kept_o[0:TOK, AT_X + h * TOK : AT_X + (h + 1) * TOK] = invs[h]
        kept_o[0:TOK, h * DV : (h + 1) * DV] = u_v
        low_o[0:TOK, AT_U + h * DK : AT_U + (h + 1) * DK] = u_k.astype(bf16)
        scores = fadings[h] * mt(q, k) * b_t[h : h + 1, :]
        out_o[:, h * DV : (h + 1) * DV] = mm(scores, u_v)
        out_o[:, VW + h * DK : VW + (h + 1) * DK] = (
            jnp.exp(c_col) * q.astype(f32) - mm(scores, u_k)
        )
        c_last = c_all[TOK - 1 : TOK, HEADS + h : HEADS + h + 1]
        b_k = b_col * jnp.exp(c_last - c_col) * k.astype(f32)
        turned = (eye * jnp.exp(c_last) - tm(u_k, b_k)).astype(bf16)
        offset = tm(u_v, b_k).astype(bf16)
        for g in range(4):
            send_o[h * 4 + g, 0:DK] = turned
            send_o[h * 4 + g, DK : DK + 64] = offset[64 * g : 64 * g + 64]
    copies = [
        pltpu.make_async_copy(low_o, low_hbm, sems.at[0]),
        pltpu.make_async_copy(kept_o, kept_hbm, sems.at[1]),
    ]
    for copy in copies:
        copy.start()
    for copy in copies:
        copy.wait()


def scan_kernel(maps, out):
    state = jnp.zeros((64, DK), f32)
    for d in range(SEQ):
        out[d] = state.astype(bf16)
        if d < SEQ - 1:
            turned = maps[d, 0:DK]
            state = mm(
                jnp.concatenate(halves(state), axis=1), jnp.concatenate([turned, turned], axis=0)
            ) + maps[d, DK : DK + 64].astype(f32)


def scan_back_kernel(grads, maps, out):
    state = jnp.zeros((64, DK), f32)
    for d in range(SEQ - 1, -1, -1):
        out[d] = state.astype(bf16)
        if d > 0:
            turned = maps[d, 0:DK]
            state = mt(
                jnp.concatenate(halves(state), axis=1), jnp.concatenate([turned, turned], axis=1)
            ) + grads[d].astype(f32)


def mixed_kernel(out_hbm, st, gate_hbm, gain, mixed_o, gated_o, out, gate_pre, sems):
    finish_copies(fetch([(out_hbm, out), (gate_hbm, gate_pre)], sems))
    for h in range(HEADS):
        at = slice(h * DV, (h + 1) * DV)
        state = st[4 * h : 4 * h + 4].reshape(DV, DK)
        mixed = out[:, at] + mt(out[:, VW + h * DK : VW + (h + 1) * DK], state)
        mixed_o[:, at] = mixed
        normed = mixed * lax.rsqrt(jnp.mean(mixed * mixed, axis=1, keepdims=True) + epsilon)
        gate = gate_pre[:, at]
        gated_o[:, at] = (normed * gain[...] * (gate * sigmoid(gate))).astype(bf16)


def mixed_back_kernel(gated_grad, mixed_in, gate_pre, gain, out, do_o, gp_o, gain_o, sg_o):
    gain_total = jnp.zeros((1, DV), f32)
    for h in range(HEADS):
        at = slice(h * DV, (h + 1) * DV)
        mixed = mixed_in[:, at]
        root = lax.rsqrt(jnp.mean(mixed * mixed, axis=1, keepdims=True) + epsilon)
        m = mixed * root
        gate = gate_pre[:, at]
        sig = sigmoid(gate)
        grad = gated_grad[:, at]
        gm = grad * m
        silu = gate * sig
        gain_total = gain_total + jnp.sum(gm * silu, axis=0, keepdims=True)
        gp_o[:, at] = (gm * gain[...] * (sig * (1.0 + gate * (1.0 - sig)))).astype(bf16)
        e = grad * gain[...] * silu
        d_out = (root * (e - m * jnp.mean(e * m, axis=1, keepdims=True))).astype(bf16)
        do_o[:, at] = d_out
        sg = tm(d_out, out[:, VW + h * DK : VW + (h + 1) * DK])
        sg_o[4 * h : 4 * h + 4] = sg.astype(bf16).reshape(4, 64, DK)
    gain_o[...] = gain_total


def back_kernel(
    low_hbm, kept_hbm, do_hbm, st_hbm, gt_i, dz_o, dzh_o, fg_o, low_o, head_o,
    ext, low_i, kept_i, do_i, st_i, sems,
):
    copies = [
        pltpu.make_async_copy(source, target, sems.at[n])
        for n, (source, target) in enumerate(
            ((low_hbm, low_i), (kept_hbm, kept_i), (do_hbm, do_i), (st_hbm, st_i))
        )
    ]
    for copy in copies:
        copy.start()
    for copy in copies:
        copy.wait()
    ext[...] = low_i[:, 0:PRE].astype(f32)
    filt = kept_i[TOK:, :]
    rows, cols = masks()
    inclusive = rows >= cols
    strict = rows > cols
    scal = kept_i[0:TOK, AT_B : AT_B + TOK]
    c_all = kept_i[0:TOK, AT_C : AT_C + TOK]
    c_t = c_all.T
    b_t = scal.T

    def before_silu(at, width):
        z = ext[pl.ds(HALO - 3, TOK), at : at + width] * filt[0:1, at : at + width]
        for j in range(1, 4):
            z = z + ext[pl.ds(HALO - 3 + j, TOK), at : at + width] * filt[j : j + 1, at : at + width]
        return z

    def finish(grad, z, sig, at, width):
        dz = grad * (sig * (1.0 + z * (1.0 - sig)))
        dz_o[:, at : at + width] = dz
        dzh_o[:, at : at + width] = dz[0:HALO].astype(bf16)
        for j in range(4):
            fg_o[j : j + 1, at : at + width] = jnp.sum(
                dz * ext[pl.ds(HALO - 3 + j, TOK), at : at + width], axis=0, keepdims=True
            )

    fg_o[4:8, :] = jnp.zeros((4, PRE), f32)
    lane = lax.broadcasted_iota(jnp.int32, (TOK, TOK), 1)
    cols_acc = jnp.zeros((TOK, TOK), f32)
    sub = lax.broadcasted_iota(jnp.int32, (TOK, TOK), 0)
    rows_acc = jnp.zeros((TOK, TOK), f32)
    heads = range(HEADS)
    at_v = [slice(h * DV, (h + 1) * DV) for h in heads]
    q = [low_i[0:TOK, AT_Q + h * DK : AT_Q + (h + 1) * DK] for h in heads]
    k = [low_i[0:TOK, AT_K + h * DK : AT_K + (h + 1) * DK] for h in heads]
    st = [st_i[4 * h : 4 * h + 4].reshape(DV, DK) for h in heads]
    gt = [gt_i[4 * h : 4 * h + 4].reshape(DV, DK) for h in heads]
    c_col = [c_all[:, HEADS + h : HEADS + h + 1] for h in heads]
    c_row = [c_t[HEADS + h : HEADS + h + 1, :] for h in heads]
    c_last = [c_all[TOK - 1 : TOK, HEADS + h : HEADS + h + 1] for h in heads]
    b_col = [scal[:, h : h + 1] for h in heads]
    b_row = [b_t[h : h + 1, :] for h in heads]
    fading = [fading_of(c_col[h], c_row[h], inclusive) for h in heads]
    growth = [jnp.exp(c_col[h]) for h in heads]
    remains = [jnp.exp(c_last[h] - c_col[h]) for h in heads]
    scores = [fading[h] * mt(q[h], k[h]) for h in heads]
    low_one = [jnp.where(strict, fading[h] * mt(k[h], k[h]), 0.0) for h in heads]
    u = [
        kept_i[0:TOK, at_v[h]]
        - mt(low_i[0:TOK, AT_U + h * DK : AT_U + (h + 1) * DK], st[h])
        for h in heads
    ]
    w = [(b_col[h] * u[h]).astype(bf16) for h in heads]
    k_rem = [remains[h] * k[h].astype(f32) for h in heads]
    d_w = [tm(scores[h], do_i[:, at_v[h]]) + mt(k_rem[h], gt[h]) for h in heads]
    d_beta = [jnp.sum(u[h] * d_w[h], axis=1, keepdims=True) for h in heads]
    d_r = [
        tm(kept_i[0:TOK, AT_X + h * TOK : AT_X + (h + 1) * TOK], b_col[h] * d_w[h]) for h in heads
    ]
    d_rl = [d_r[h].astype(bf16) for h in heads]
    d_low = [jnp.where(strict, -mt(d_rl[h], u[h]), 0.0) for h in heads]
    d_a = [jnp.where(inclusive, mt(do_i[:, at_v[h]], w[h]), 0.0) for h in heads]
    d_qk = [d_a[h] * fading[h] for h in heads]
    e_beta = [d_low[h] * low_one[h] for h in heads]
    e_sum = [d_a[h] * scores[h] + e_beta[h] * b_row[h] for h in heads]
    d_kk = [d_low[h] * fading[h] * b_row[h] for h in heads]
    d_os = [mm(do_i[:, at_v[h]], st[h]) for h in heads]
    d_rs = [mm(d_rl[h], st[h]) for h in heads]
    w_g = [mm(w[h], gt[h]) for h in heads]
    dq = [mm(d_qk[h], k[h]) + growth[h] * d_os[h] for h in heads]
    dk = [
        tm(d_qk[h], q[h])
        + mm(d_kk[h], k[h])
        + tm(d_kk[h], k[h])
        - growth[h] * d_rs[h]
        + remains[h] * w_g[h]
        for h in heads
    ]
    for h in heads:
        rem_sum = jnp.sum(k_rem[h] * w_g[h], axis=1, keepdims=True)
        d_c = (
            jnp.sum(e_sum[h], axis=1, keepdims=True)
            + growth[h]
            * jnp.sum(
                q[h].astype(f32) * d_os[h] - k[h].astype(f32) * d_rs[h], axis=1, keepdims=True
            )
            - rem_sum
        )
        last = jnp.sum(rem_sum, axis=0, keepdims=True) + jnp.exp(c_last[h]) * jnp.sum(
            jnp.sum(st[h].astype(f32) * gt[h].astype(f32), axis=1, keepdims=True),
            axis=0,
            keepdims=True,
        )
        d_c = d_c + jnp.where(sub[:, 0:1] == TOK - 1, last, 0.0)
        cols_acc = cols_acc + jnp.where(lane == h, d_beta[h], 0.0)
        cols_acc = cols_acc + jnp.where(lane == HEADS + h, d_c, 0.0)
        rows_acc = rows_acc + jnp.where(sub == h, jnp.sum(e_beta[h], axis=0, keepdims=True), 0.0)
        rows_acc = rows_acc - jnp.where(
            sub == HEADS + h, jnp.sum(e_sum[h], axis=0, keepdims=True), 0.0
        )
    for h in heads:
        for grad, base, scale in ((dq[h], 0, DK ** (-0.5)), (dk[h], QK, 1.0)):
            at = base + h * DK
            z = before_silu(at, DK)
            sig = sigmoid(z)
            act = z * sig
            root = lax.rsqrt(jnp.sum(act * act, axis=1, keepdims=True) + smallest)
            unit = act * root
            grad = grad * scale
            d_act = root * (grad - unit * jnp.sum(unit * grad, axis=1, keepdims=True))
            finish(d_act, z, sig, at, DK)
        at = 2 * QK + h * DV
        z = before_silu(at, DV)
        finish(d_r[h], z, sigmoid(z), at, DV)
    total = cols_acc + rows_acc.T
    upper = jnp.where(rows <= cols, 1.0, 0.0).astype(bf16)
    summed = mm(
        jnp.concatenate([upper, upper, upper], axis=1), jnp.concatenate(thirds(total), axis=0)
    )
    grads = jnp.where(lane < HEADS, total, summed)
    sloped = grads * kept_i[0:TOK, AT_S : AT_S + TOK]
    low_o[...] = sloped.astype(bf16)
    head_o[0:1, :] = jnp.sum(grads * scal, axis=0, keepdims=True)
    head_o[1:2, :] = jnp.sum(sloped, axis=0, keepdims=True)
    head_o[2:8, :] = jnp.zeros((6, TOK), f32)


def conv_back_kernel(dz, after, filt, pre_o, ext):
    ext[0:TOK] = dz[...]
    ext[TOK:] = after[...].astype(f32)
    for at in range(0, PRE, 256):
        total = ext[pl.ds(3, TOK), at : at + 256] * filt[0:1, at : at + 256]
        for j in range(1, 4):
            total = total + ext[pl.ds(3 - j, TOK), at : at + 256] * filt[j : j + 1, at : at + 256]
        pre_o[:, at : at + 256] = total.astype(bf16)


def input_grad_kernel(part, part_in, middle_grad, inputs, gain_mix, grad_o):
    grad = part[...].astype(f32) + part_in[...].astype(f32)
    values = inputs[...].astype(f32)
    root = lax.rsqrt(jnp.mean(values * values, axis=1, keepdims=True) + epsilon)
    unit = values * root
    e = grad * gain_mix[...]
    grad_o[...] = (
        middle_grad[...] + root * (e - unit * jnp.mean(e * unit, axis=1, keepdims=True))
    ).astype(bf16)


def smalls_kernel(part, inputs, gain, ffn_gain_grad, normed, logits, taps, heads, small_o):
    values = inputs[...].astype(f32)
    root = lax.rsqrt(jnp.mean(values * values, axis=1, keepdims=True) + epsilon)
    mix_grad = jnp.sum(part[...].astype(f32) * (values * root), axis=0, keepdims=True)
    gain_grad = gain[...]
    logit_grads = tm(logits[...], normed[...])[0:8]
    log_grad = heads[0:1, HEADS : 2 * HEADS]
    bias_grad = heads[1:2, HEADS : 2 * HEADS]
    head = jnp.concatenate([log_grad, bias_grad], axis=1)
    high = head.astype(bf16).astype(f32)
    head = jnp.concatenate([high, head - high, jnp.zeros((1, 64 - 4 * HEADS), f32)], axis=1)
    ffn = ffn_gain_grad[...]
    tap = taps[0:4, :]
    for j in range(SEQ):
        wide = slice(64 * j, 64 * j + 64)
        small_o[j] = jnp.concatenate(
            [
                jnp.concatenate([mix_grad[:, wide], ffn[:, wide]], axis=1),
                jnp.concatenate(
                    [gain_grad[:, 16 * j : 16 * j + 16], jnp.zeros((1, 48), f32), head], axis=1
                ),
                jnp.zeros((2, 128), f32),
                jnp.concatenate([logit_grads[0:4, wide], logit_grads[4:8, wide]], axis=1),
                jnp.concatenate(
                    [
                        tap[:, 2 * QK + 64 * j : 2 * QK + 64 * j + 64],
                        tap[:, 32 * j : 32 * j + 32],
                        tap[:, QK + 32 * j : QK + 32 * j + 32],
                    ],
                    axis=1,
                ),
                jnp.zeros((4, 128), f32),
            ],
            axis=0,
        ).astype(bf16)


def padded_rows(left):
    return -(-(left.shape[1] // SEQ) // 16) * 16


def pieces_rows(pieces):
    return sum(padded_rows(left) * (right.shape[1] // 128) for left, right in pieces)


def weight_body(count, added, refs):
    ins = refs[: 2 * count]
    adds = refs[2 * count : 2 * count + added]
    out = refs[2 * count + added]
    turned = refs[2 * count + added + 1]
    offset = 0
    part = 0
    done = 0
    for at in range(count):
        left, right = ins[2 * at], ins[2 * at + 1]
        width = left.shape[1]
        rows = width // SEQ
        padded = padded_rows(left)
        turned[0:width] = left[...].T

        def tiles(n, count, right=right, width=width, rows=rows, padded=padded, offset=offset,
                  part=part, done=done):
            wide = jnp.dot(
                turned[0:width],
                right[:, pl.ds(pl.multiple_of(n * 128, 128), 128 * count)],
                preferred_element_type=f32,
            )
            for m in range(count):
                piece = wide[:, m * 128 : (m + 1) * 128].reshape(SEQ, rows, 128)
                if padded > rows:
                    piece = jnp.concatenate(
                        [piece, jnp.zeros((SEQ, padded - rows, 128), f32)], axis=1
                    )
                if part < added:
                    where = pl.ds(pl.multiple_of(offset - done + (n + m) * padded, 16), padded)
                    piece = piece + adds[part][:, where].astype(f32)
                where = pl.ds(pl.multiple_of(offset + (n + m) * padded, 16), padded)
                out[:, where] = piece.astype(bf16)

        def pair(n, carry, tiles=tiles):
            tiles(2 * n, 2)
            return carry

        count_here = right.shape[1] // 128
        lax.fori_loop(0, count_here // 2, pair, 0)
        if count_here % 2:
            tiles(count_here - 1, 1)
        offset += padded * (right.shape[1] // 128)
        if part < added and offset - done == adds[part].shape[1]:
            done = offset
            part += 1


def weight_grads(pieces, adds=()):
    total = pieces_rows(pieces)
    args = [operand for pair in pieces for operand in pair] + list(adds)

    def body(*refs):
        weight_body(len(pieces), len(adds), refs)

    return kernel_call(
        body,
        [((SEQ, total, 128), bf16)],
        *args,
        scratch=[pltpu.VMEM((1408, TOK), bf16)],
        spare=6 * MIB,
        flops=2 * 128 * 128 * SEQ * total,
        main=(0,),
    )[0]


def fetch(pairs, sems, first=0):
    copies = [
        pltpu.make_async_copy(source, target, sems.at[first + n])
        for n, (source, target) in enumerate(pairs)
    ]
    for copy in copies:
        copy.start()
    return copies


def finish_copies(copies):
    for copy in copies:
        copy.wait()


def late_body(place, normed, pre_kept, late_in, smalls, *refs):
    outs = refs[0:8]
    turned, kept, late_add, sems = refs[8:]
    rows = kept.shape[2] // 2
    fetched = fetch([(late_in, late_add)], sems)
    sent = []
    for s in range(4):
        x_to = lax.rem(place[1] + s, 4)
        sent += fetch([(smalls.at[:, x_to], outs[s].at[:, pl.ds(rows, 16)])], sems, 1 + s)
    turned[...] = normed[...].T
    finish_copies(fetched)
    for n in range(pre_kept.shape[1] // 256):
        wide = jnp.dot(
            turned[...], pre_kept[:, n * 256 : (n + 1) * 256], preferred_element_type=f32
        )
        for m in range(2):
            where = slice((2 * n + m) * 64, (2 * n + m + 1) * 64)
            piece = wide[:, m * 128 : (m + 1) * 128].reshape(SEQ, 64, 128)
            piece = piece + late_add[:, where].astype(f32)
            kept[:, :, where] = piece.astype(bf16).reshape(4, 4, 64, 128)
        if 2 * (n + 1) * 64 == rows:
            for s in range(4):
                x_to = lax.rem(place[1] + s, 4)
                sent += fetch(
                    [(kept.at[:, x_to, pl.ds(0, rows)], outs[s].at[:, pl.ds(0, rows)])], sems, 5 + s
                )
    for s in range(4):
        z_to = lax.rem(place[0] + s, 4)
        sent += fetch([(kept.at[z_to, :, pl.ds(rows, rows)], outs[4 + s])], sems, 9 + s)
    finish_copies(sent)


def in_order(terms, own):
    total = None
    for source in range(4):
        which = lax.rem(own + 4 - source, 4)
        term = jnp.zeros(terms[0].shape, f32)
        for n in range(4):
            term = jnp.where(which == n, terms[n].astype(f32), term)
        total = term if total is None else total + term
    return total


def plain_sum(terms):
    total = terms[0].astype(f32)
    for term in terms[1:]:
        total = total + term.astype(f32)
    return total


def sum_spread_body(place, *refs):
    outs, parts, sems = refs[8:16], refs[16:24], refs[24]
    finish_copies(fetch(zip(refs[0:8], parts), sems))
    first, second = parts[0:4], parts[4:8]
    rows = first[0].shape[1]
    for s in range(4):
        z_to = lax.rem(place[0] + s, 4)
        x_to = lax.rem(place[1] + s, 4)
        outs[s][...] = plain_sum([part[z_to] for part in first]).astype(bf16)
        outs[s][rows - 16 :] = in_order(
            [part[z_to, rows - 16 : rows] for part in first], place[1]
        ).astype(bf16)
        outs[4 + s][...] = plain_sum([part[x_to] for part in second]).astype(bf16)


def sum_body(place, *refs):
    out, parts, sems = refs[8], refs[9:17], refs[17]
    finish_copies(fetch(zip(refs[0:8], parts), sems))
    first, second = parts[0:4], parts[4:8]
    rows = first[0].shape[0]
    out[0:rows] = plain_sum([part[...] for part in first]).astype(bf16)
    out[rows - 16 : rows] = in_order(
        [part[rows - 16 : rows] for part in first], place[0]
    ).astype(bf16)
    out[rows:] = plain_sum([part[...] for part in second]).astype(bf16)


def fill(first, mine, other, out, core, at, rows=64, padded=64, count=None, first_tile=0):
    same = first if core == 0 else jnp.logical_not(first)
    for n in range(out.shape[1] // 128 if count is None else count):
        spot = slice(at + n * padded, at + n * padded + padded)
        block = jnp.where(same, mine[spot].astype(f32), other[spot].astype(f32))
        column = (first_tile + n) * 128
        out[:, column : column + 128] = block.astype(bf16)[0:rows]


def unpack_early_body(place, mine, other, gate_o, up_o, down_o, outgate_o, wout_o):
    put = functools.partial(fill, place[2] == 0, mine, other)
    put(gate_o, 0, 0)
    put(up_o, 1, 0)
    at = gate_o.shape[1] // 128 * 64
    tiles = down_o.shape[1] // 256
    put(down_o, 0, at, 88, 96, tiles)
    put(down_o, 1, at, 88, 96, tiles, tiles)
    at += 96 * tiles
    put(outgate_o, 0, at)
    put(wout_o, 1, at)


def unpack_late_body(
    place, mine, other, over_tensor, over_both, query_o, key_o, value_o, mix_o, ffn_o, gain_o,
    log_o, bias_o, beta_o, decay_o, taps_q_o, taps_k_o, taps_v_o,
):
    put = functools.partial(fill, place[2] == 0, mine, other)
    half = VW // 4
    put(query_o, 0, 0)
    put(key_o, 0, half + 16)
    put(value_o, 1, 0, count=4)
    put(value_o, 1, half + 16, count=4, first_tile=4)
    small = mine[half : half + 16].astype(f32) + other[half : half + 16].astype(f32)
    both = small[0:2] + (over_tensor[0:2].astype(f32) + over_both[0:2].astype(f32))
    mix_o[...] = both[0:1, 0:64].astype(bf16)
    ffn_o[...] = small[0:1, 64:128].astype(bf16)
    gain_o[...] = both[1:2, 0:16].astype(bf16)
    for n, out in enumerate((log_o, bias_o)):
        start = 64 + n * HEADS
        out[...] = (
            small[1:2, start : start + HEADS]
            + small[1:2, start + 2 * HEADS : start + 3 * HEADS]
        ).astype(bf16)
    beta_o[...] = small[4:8, 0:64].astype(bf16)
    decay_o[...] = small[4:8, 64:128].astype(bf16)
    taps_q_o[...] = small[8:12, 64:96].astype(bf16)
    taps_k_o[...] = small[8:12, 96:128].astype(bf16)
    taps_v_o[...] = small[8:12, 0:64].astype(bf16)


def placed_call(body, outs, place, *args, main=False, far=(), far_outs=(), scratch=(), limit=12):
    kind = pltpu.HBM if main else jax.ShapeDtypeStruct
    return pl.pallas_call(
        body,
        out_shape=[kind(shape, bf16) for shape in outs],
        in_specs=[pl.BlockSpec(memory_space=pltpu.SMEM)]
        + [
            pl.BlockSpec(memory_space=pltpu.HBM if n in far else pltpu.VMEM)
            for n in range(len(args))
        ],
        out_specs=[
            pl.BlockSpec(memory_space=pltpu.HBM if n in far_outs else pltpu.VMEM)
            for n in range(len(outs))
        ],
        scratch_shapes=list(scratch),
        compiler_params=pltpu.CompilerParams(vmem_limit_bytes=limit * MIB),
    )(place, *args)


def along_x(steps):
    return [(z * 4 + x, z * 4 + (x + steps) % 4) for z in range(4) for x in range(4)]


def along_z(steps):
    return [(z * 4 + x, (z + steps) % 4 * 4 + x) for z in range(4) for x in range(4)]


def swap_tensor(value):
    return lax.ppermute(value, "tensor", [(0, 1), (1, 0)])


def swap_core(value):
    return lax.ppermute(value, "dp", [(0, 1), (1, 0), (2, 3), (3, 2)])


def swap_both(value):
    pairs = [(t * 4 + d, (1 - t) * 4 + d // 2 * 2 + 1 - d % 2) for t in range(2) for d in range(4)]
    return lax.ppermute(value, ("tensor", "dp"), pairs)


def swap_far(value):
    return lax.ppermute(value, "dp", [(0, 2), (2, 0), (1, 3), (3, 1)])


def shift(value, steps):
    first, last = max(0, -steps), min(SEQ, SEQ - steps)
    return lax.ppermute(value, "seq", [(at, at + steps) for at in range(first, last)])


def exchange(value):
    return lax.all_to_all(value, "seq", 0, 0, tiled=True)


def dot(a, b):
    return jnp.dot(a, b, preferred_element_type=f32)


def dot_t(a, b):
    return lax.dot_general(a, b, (((1,), (1,)), ((), ())), preferred_element_type=f32)


def norm_parts(values):
    root = lax.rsqrt(jnp.mean(values * values, axis=-1, keepdims=True) + epsilon)
    return root, values * root


def norm_back(grad, gain, root, unit):
    e = grad * gain
    return root * (e - unit * jnp.mean(e * unit, axis=-1, keepdims=True))


def per_device(
    inputs,
    cotangent,
    norm_mix,
    w_query,
    w_key,
    w_value,
    w_outgate,
    w_beta,
    w_decay,
    decay_log,
    decay_bias,
    conv_query,
    conv_key,
    conv_value,
    out_gain,
    w_out,
    norm_ffn,
    w_gate,
    w_up,
    w_down,
):
    width = inputs.shape[2]
    first = lax.axis_index("dp") % 2 == 0
    at = lax.axis_index("seq")
    place = jnp.stack([at // 4, at % 4, lax.axis_index("dp") % 2]).astype(jnp.int32)
    residual = inputs.reshape(TOK, width).astype(f32)
    feed_grad = cotangent.reshape(TOK, width)
    gain_mix = norm_mix.astype(f32)
    gain_ffn = norm_ffn.astype(f32)
    gain_head = out_gain.astype(f32).reshape(1, DV)
    filters = jnp.concatenate([conv_query, conv_key, conv_value], axis=0).astype(f32)
    filt = jnp.pad(filters.T, ((0, 4), (0, 0)))

    root_mix, unit_mix = norm_parts(residual)
    normed_low = (unit_mix * gain_mix).astype(bf16)
    mixed_pre = jnp.concatenate(
        [dot(normed_low, w_query), dot(normed_low, w_key), dot(normed_low, w_value)], axis=1
    ).astype(bf16)
    halo = shift(mixed_pre[TOK - HALO :], 1)
    beta_rows = jax.nn.sigmoid(dot(normed_low, w_beta))
    decay_at = dot(normed_low, w_decay) + decay_bias.astype(f32)
    decay_rate = -jnp.exp(decay_log.astype(f32))
    decays = decay_rate * jax.nn.softplus(decay_at)

    def lanes(values, others):
        return jnp.pad(jnp.concatenate([values, others], axis=1), ((0, 0), (0, 120)))

    bdv = lanes(beta_rows, decays)
    slopes = lanes(beta_rows * (1.0 - beta_rows), decay_rate * jax.nn.sigmoid(decay_at))
    gate_pre = dot(normed_low, w_outgate)

    kept_low, kept, out_local, maps = kernel_call(
        front_kernel,
        [KEPT_LOW, KEPT, ((TOK, VW + QK), f32), ((SEQ, DK + 64, DK), bf16)],
        mixed_pre,
        halo,
        filt,
        bdv,
        slopes,
        scratch=[
            pltpu.VMEM((TOK + HALO, PRE), f32),
            pltpu.VMEM(*KEPT_LOW),
            pltpu.VMEM(*KEPT),
            pltpu.SemaphoreType.DMA((2,)),
        ],
        far_outs=(0, 1),
        main=(3,),
    )
    maps = exchange(maps)
    (states,) = kernel_call(scan_kernel, [((SEQ, 64, DK), bf16)], maps, main=(0,))
    states = exchange(states)
    mixed, gated_low = kernel_call(
        mixed_kernel,
        [((TOK, VW), f32), ((TOK, VW), bf16)],
        out_local,
        states,
        gate_pre,
        gain_head,
        scratch=[
            pltpu.VMEM((TOK, VW + QK), f32),
            pltpu.VMEM((TOK, VW), f32),
            pltpu.SemaphoreType.DMA((2,)),
        ],
        far=(0, 2),
    )
    branch = dot(gated_low, w_out).astype(bf16)
    branch_in = swap_tensor(branch)
    hidden_grad = dot_t(feed_grad, w_down)
    middle = residual + (branch.astype(f32) + branch_in.astype(f32))
    root_ffn, unit_ffn = norm_parts(middle)
    two_low = (unit_ffn * gain_ffn).astype(bf16)
    gate_ffn = dot(two_low, w_gate)
    up_ffn = dot(two_low, w_up)
    sig = jax.nn.sigmoid(gate_ffn)
    silu = gate_ffn * sig
    hidden_low = (silu * up_ffn).astype(bf16)
    gate_low = (hidden_grad * up_ffn * (sig * (1.0 + gate_ffn * (1.0 - sig)))).astype(bf16)
    up_low = (hidden_grad * silu).astype(bf16)
    half = width // 2
    ffn_sent = weight_grads(
        [
            (two_low, jnp.where(first, up_low, gate_low)),
            (hidden_low, jnp.where(first, feed_grad[:, half:], feed_grad[:, :half])),
        ]
    )
    ffn_in = swap_core(ffn_sent)
    ffn_sent, gate_next, up_next = lax.optimization_barrier((ffn_sent, gate_low, up_low))
    two_part = (dot_t(gate_next, w_gate) + dot_t(up_next, w_up)).astype(bf16)
    two_in = swap_tensor(two_part)

    two_grad = two_part.astype(f32) + two_in.astype(f32)
    grad_norm_ffn = jnp.sum(two_grad * unit_ffn, axis=0)
    middle_grad = feed_grad.astype(f32) + norm_back(two_grad, gain_ffn, root_ffn, unit_ffn)
    branch_low = middle_grad.astype(bf16)
    gated_grad = dot_t(branch_low, w_out)
    mixed_grad, gate_pre_low, gain_grad, start_grad = kernel_call(
        mixed_back_kernel,
        [((TOK, VW), bf16), ((TOK, VW), bf16), ((1, DV), f32), ((SEQ, 64, DK), bf16)],
        gated_grad,
        mixed,
        gate_pre,
        gain_head,
        out_local,
        main=(3,),
    )
    out_sent = weight_grads(
        [
            (
                jnp.where(first, gated_low, normed_low),
                jnp.where(first, branch_low, gate_pre_low),
            )
        ]
    )
    early = weight_grads(
        [
            (two_low, jnp.where(first, gate_low, up_low)),
            (hidden_low, jnp.where(first, feed_grad[:, :half], feed_grad[:, half:])),
            (
                jnp.where(first, normed_low, gated_low),
                jnp.where(first, gate_pre_low, branch_low),
            ),
        ],
        [ffn_in, swap_core(out_sent)],
    )
    early = lax.optimization_barrier(
        lax.psum_scatter(early, "seq", scatter_dimension=0, tiled=True)
    )
    start_grad = exchange(start_grad)
    (end_grads,) = kernel_call(
        scan_back_kernel, [((SEQ, 64, DK), bf16)], start_grad, maps, main=(0,)
    )
    end_grads = exchange(end_grads)
    end_grads, hidden_last = lax.optimization_barrier((end_grads, hidden_low))
    feed_part = dot(hidden_last, w_down).astype(bf16)
    feed_in = swap_tensor(feed_part)
    output = (middle + (feed_part.astype(f32) + feed_in.astype(f32))).astype(bf16)
    dz, dz_first, filter_grad, logit_low, head_grads = kernel_call(
        back_kernel,
        [
            ((TOK, PRE), f32),
            ((HALO, PRE), bf16),
            ((8, PRE), f32),
            ((TOK, TOK), bf16),
            ((8, TOK), f32),
        ],
        kept_low,
        kept,
        mixed_grad,
        states,
        end_grads,
        scratch=[
            pltpu.VMEM((TOK + HALO, PRE), f32),
            pltpu.VMEM(*KEPT_LOW),
            pltpu.VMEM(*KEPT),
            pltpu.VMEM((TOK, VW), bf16),
            pltpu.VMEM((SEQ, 64, DK), bf16),
            pltpu.SemaphoreType.DMA((4,)),
        ],
        far=(0, 1, 2, 3),
        main=(1,),
    )
    (pre_low,) = kernel_call(
        conv_back_kernel,
        [((TOK, PRE), bf16)],
        dz,
        shift(dz_first, -1),
        filt,
        scratch=[pltpu.VMEM((TOK + HALO, PRE), f32)],
    )
    part = (
        dot_t(pre_low[:, :QK], w_query)
        + dot_t(pre_low[:, QK : 2 * QK], w_key)
        + dot_t(pre_low[:, 2 * QK :], w_value)
        + dot_t(gate_pre_low, w_outgate)
        + dot_t(logit_low[:, :HEADS], w_beta)
        + dot_t(logit_low[:, HEADS : 2 * HEADS], w_decay)
    ).astype(bf16)
    late_sent = weight_grads(
        [(normed_low, jnp.where(first, pre_low[:, 2 * QK :], pre_low[:, : 2 * QK]))]
    )
    late_in = swap_core(late_sent)
    (smalls,) = kernel_call(
        smalls_kernel,
        [((SEQ, 16, 128), bf16)],
        part,
        inputs.reshape(TOK, width),
        gain_grad,
        grad_norm_ffn.reshape(1, width),
        normed_low,
        logit_low,
        filter_grad,
        head_grads,
    )
    half_rows = VW // 4
    small_rows = half_rows + 16
    blocks = placed_call(
        late_body,
        [(4, small_rows, 128)] * 4 + [(4, half_rows, 128)] * 4,
        place,
        normed_low,
        jnp.where(first, pre_low[:, : 2 * QK], pre_low[:, 2 * QK :]),
        late_in,
        smalls.reshape(4, 4, 16, 128),
        main=True,
        far=(2,),
        far_outs=range(8),
        scratch=[
            pltpu.VMEM((width, TOK), bf16),
            pltpu.VMEM((4, 4, 2 * half_rows, 128), bf16),
            pltpu.VMEM((SEQ, 2 * half_rows, 128), bf16),
            pltpu.SemaphoreType.DMA((13,)),
        ],
        limit=16,
    )
    moved = [blocks[0]] + [lax.ppermute(blocks[s], "seq", along_x(s)) for s in range(1, 4)]
    moved += [blocks[4]] + [lax.ppermute(blocks[4 + s], "seq", along_z(s)) for s in range(1, 4)]
    *blocks, part_next = lax.optimization_barrier((*blocks, part))
    part_in = swap_tensor(part_next)
    (grad_inputs,) = kernel_call(
        input_grad_kernel,
        [((TOK, width), bf16)],
        part_next,
        part_in,
        middle_grad,
        inputs.reshape(TOK, width),
        gain_mix.reshape(1, width),
    )
    *moved, grad_inputs, output = lax.optimization_barrier((*moved, grad_inputs, output))
    step_shapes = [(4, small_rows, 128)] * 4 + [(4, half_rows, 128)] * 4
    blocks = placed_call(
        sum_spread_body,
        [(small_rows, 128)] * 4 + [(half_rows, 128)] * 4,
        place,
        *moved,
        main=True,
        far=range(8),
        scratch=[pltpu.VMEM(shape, bf16) for shape in step_shapes]
        + [pltpu.SemaphoreType.DMA((8,))],
        limit=60,
    )
    moved = [blocks[0]] + [lax.ppermute(blocks[s], "seq", along_z(s)) for s in range(1, 4)]
    moved += [blocks[4]] + [lax.ppermute(blocks[4 + s], "seq", along_x(s)) for s in range(1, 4)]
    *_, early = lax.optimization_barrier((*blocks, early.reshape(-1, 128)))
    early_far = swap_far(early)
    *moved, early, early_far = lax.optimization_barrier((*moved, early, early_far))
    (late,) = placed_call(
        sum_body,
        [(small_rows + half_rows, 128)],
        place,
        *moved,
        main=True,
        far=range(8),
        scratch=[pltpu.VMEM(shape[1:], bf16) for shape in step_shapes]
        + [pltpu.SemaphoreType.DMA((8,))],
        limit=60,
    )
    late, early, early_far = lax.optimization_barrier((late, early, early_far))
    late_far = swap_far(late)
    columns = w_gate.shape[1]
    early = (early.astype(f32) + early_far.astype(f32)).astype(bf16)
    grad_gate, grad_up, grad_down, grad_outgate, grad_wout = placed_call(
        unpack_early_body,
        [(64, columns), (64, columns), (88, width), (64, VW), (64, width)],
        place,
        early,
        swap_core(early),
    )
    late_far, grad_gate, grad_up, grad_down, grad_outgate, grad_wout = lax.optimization_barrier(
        (late_far, grad_gate, grad_up, grad_down, grad_outgate, grad_wout)
    )
    late = (late.astype(f32) + late_far.astype(f32)).astype(bf16)
    small = late[half_rows:small_rows]
    shares = placed_call(
        unpack_late_body,
        [
            (64, QK),
            (64, QK),
            (64, VW),
            (1, 64),
            (1, 64),
            (1, 16),
            (1, HEADS),
            (1, HEADS),
            (4, 64),
            (4, 64),
            (4, 32),
            (4, 32),
            (4, 64),
        ],
        place,
        late,
        swap_core(late),
        swap_tensor(small),
        swap_both(small),
    )
    grad_query, grad_key, grad_value = shares[:3]
    mix, ffn, gain, log, bias, beta, decay, taps_q, taps_k, taps_v = shares[3:]
    return (
        output.reshape(inputs.shape),
        grad_inputs.reshape(inputs.shape),
        mix.reshape(-1),
        grad_query,
        grad_key,
        grad_value,
        grad_outgate,
        beta.T,
        decay.T,
        log.reshape(-1),
        bias.reshape(-1),
        taps_q.T,
        taps_k.T,
        taps_v.T,
        gain.reshape(-1),
        grad_wout,
        ffn.reshape(-1),
        grad_gate,
        grad_up,
        grad_down,
    )


def solution(mesh):
    return jax.shard_map(
        per_device,
        mesh=mesh,
        in_specs=(
            P("dp", "seq", None),
            P("dp", "seq", None),
            P(),
            P(None, "tensor"),
            P(None, "tensor"),
            P(None, "tensor"),
            P(None, "tensor"),
            P(None, "tensor"),
            P(None, "tensor"),
            P("tensor"),
            P("tensor"),
            P("tensor", None),
            P("tensor", None),
            P("tensor", None),
            P(),
            P("tensor", None),
            P(),
            P(None, "tensor"),
            P(None, "tensor"),
            P("tensor", None),
        ),
        out_specs=(
            P("dp", "seq", None),
            P("dp", "seq", None),
            P("seq"),
            P("seq", "tensor"),
            P("seq", "tensor"),
            P("seq", "tensor"),
            P("seq", "tensor"),
            P("seq", "tensor"),
            P("seq", "tensor"),
            P("tensor"),
            P("tensor"),
            P(("tensor", "seq"), None),
            P(("tensor", "seq"), None),
            P(("tensor", "seq"), None),
            P("seq"),
            P(("tensor", "seq"), None),
            P("seq"),
            P("seq", "tensor"),
            P("seq", "tensor"),
            P(("tensor", "seq"), None),
        ),
        check_vma=False,
    )
```

time: 292 us -> 252 us (0.86)
  local copies, waits for them, and re-layouts: 41.4 us -> 9.28 us
  waiting for transfers between devices: 86.8 us -> 60 us
  blocking collectives: 0 us -> 25.3 us
  Pallas kernels: 46.1 us -> 52.3 us
  starting transfers between devices: 62 us -> 56 us
  other arithmetic: 14.1 us -> 9.37 us
    all_to_all x0 -> x2, blocking collectives: none -> 25.3 us  [exchange(): return lax.all_to_all(value, 'seq', 0, 0, tiled=True)]
    unnamed x153 -> x120, local copies, waits for them, and re-layouts: 28.4 us -> 9.05 us
    all_to_all x4 -> x2, waiting for transfers between devices: 31.7 us -> 16.4 us  [exchange(): return lax.all_to_all(value, 'seq', 0, 0, tiled=True)]
    ppermute x2, waiting for transfers between devices: 16.2 us -> 4.01 us  [swap_far(): return lax.ppermute(value, 'dp', [(0, 2), (2, 0), (1, 3), (3, 1)])]
    pallas_call x3 -> x5, Pallas kernels: 2.16 us -> 12.9 us  [placed_call(): pl.pallas_call(body, out_shape=[kind(shape, bf16) for shape in outs], in_...]
    reshape x14 -> x0, local copies, waits for them, and re-layouts: 6.88 us -> none  [the longest x2 2.54 us: per_device(): smalls = jnp.concatenate([grad_norm_mix.reshape(SEQ, -1), grad_norm_ffn.r...]
    all_to_all x4 -> x2, starting transfers between devices: 18.4 us -> 11.7 us  [exchange(): return lax.all_to_all(value, 'seq', 0, 0, tiled=True)]
    ppermute x4 -> x5, waiting for transfers between devices: 15.1 us -> 9.55 us  [swap_tensor(): return lax.ppermute(value, 'tensor', [(0, 1), (1, 0)])]
  transfers between devices with their start and end apart: 31 -> 30, of which waited for: 18 -> 15; matrix products, arithmetic and copies ran while one was open for 13% -> 8% of each run, Pallas kernels for 7% -> 11%
where the time goes in v2:
time: 252 us; the launch traced here: 251 us
  waiting for transfers between devices  60 us (24%)
  starting transfers between devices  56 us (22%)
  Pallas kernels  52.3 us (21%)
  blocking collectives  25.3 us (10%)
  matrix products  23.7 us (9%)
  between operations  15 us (6%)
  other arithmetic  9.37 us (4%)
  local copies, waits for them, and re-layouts  9.28 us (4%)
    pallas_call x13, Pallas kernels, kernel_call(): pl.pallas_call(body, out_shape=out_shape, in_specs=[pl.BlockSpec(memory_s...  39.4 us
    all_to_all x2, blocking collectives, exchange(): return lax.all_to_all(value, 'seq', 0, 0, tiled=True)  25.3 us
    all_to_all x2, waiting for transfers between devices, exchange(): return lax.all_to_all(value, 'seq', 0, 0, tiled=True)  16.4 us
    ppermute x3, waiting for transfers between devices, per_device(): lax.ppermute(blocks[4 + s], 'seq', along_z(s))  15 us
    ppermute x5, starting transfers between devices, swap_core(): return lax.ppermute(value, 'dp', [(0, 1), (1, 0), (2, 3), (3, 2)])  14.7 us
    dot_general x10, matrix products, dot(): return jnp.dot(a, b, preferred_element_type=f32)  14.2 us
    pallas_call x5, Pallas kernels, placed_call(): pl.pallas_call(body, out_shape=[kind(shape, bf16) for shape in outs], in_...  12.9 us
    all_to_all x2, starting transfers between devices, exchange(): return lax.all_to_all(value, 'seq', 0, 0, tiled=True)  11.7 us
  transfers between devices with their start and end apart: 30, of which 15 were waited for; matrix products, arithmetic and copies ran while one was open for 8% of the time, Pallas kernels for 11%

profile of v2, /device:TPU:1, one launch (start us, length us, event | category | flops | bytes accessed | tf_op | source)
XLA Modules:
  0.0 251.0 jit_solution(4851321875707114243)
XLA Ops:
  13.7 3.9 %collective-permute-start = (bf16[16,2048]{1,0:T(8,128)(2,1)S(1)}, bf16[16,2048]{1,0:T(8,128)(2,1)S(1)}, u32[]{:S(2)}, u32[]{:S(2)}) collective-permute-start(bf16[16,2048]{1,0:T(8,128)(2,1)S(1)} %slice.45), channel_id=1, source_target_pairs={{0,1},{1,2},{2,3},{3,4},{4,5},{5,6},{6,7},{7,8},{8,9},{9,10},{10,1... | collective-permute-start | bytes 196616 | tf_op jit(solution)/shard_map/ppermute | solution.py:728
  20.0 6.5 %shard_map.347 = (bf16[144,3584]{1,0:T(8,128)(2,1)}, f32[136,2048]{1,0:T(8,128)}, f32[128,1536]{1,0:T(8,128)S(1)}, bf16[16,192,128]{2,1,0:T(8,128)(2,1)}) custom-call(bf16[128,2048]{1,0:T(8,128)(2,1)S(1)} %copy-done.11, bf16[16,2048]{1,0:T(8,128)(2,1)S(1)} %collective-permute-done.halo, f32[8,2048]{1,0:T(8,128)S(1)} %pad_convert_fusion.filt, ...), custom_call_target="tpu_custom_call" | custom-call | bytes 4505600 | tf_op jit(solution)/shard_map/pallas_call | solution.py:36
  27.4 8.2 %all-to-all-start = ((bf16[16,192,128]{2,1,0:T(8,128)(2,1)}), bf16[16,192,128]{2,1,0:T(8,128)(2,1)}, u32[]{:S(2)}, u32[]{:S(2)}) async-start(bf16[16,192,128]{2,1,0:T(8,128)(2,1)} %get-tuple-element.107), calls=%async_computation | async-start | bytes 1572864 | tf_op jit(solution)/shard_map/all_to_all | solution.py:732
  36.3 11.8 %all-to-all-done.maps = bf16[16,192,128]{2,1,0:T(8,128)(2,1)} async-done(((bf16[16,192,128]{2,1,0:T(8,128)(2,1)}), bf16[16,192,128]{2,1,0:T(8,128)(2,1)}, u32[]{:S(2)}, u32[]{:S(2)}) %all-to-all-start) | async-done | bytes 786464 | tf_op jit(solution)/shard_map/all_to_all | solution.py:732
  48.1 3.7 %shard_map.348 = bf16[16,64,128]{2,1,0:T(8,128)(2,1)} custom-call(bf16[16,192,128]{2,1,0:T(8,128)(2,1)} %all-to-all-done.maps), custom_call_target="tpu_custom_call" | custom-call | bytes 1048576 | tf_op jit(solution)/shard_map/pallas_call | solution.py:36
  51.8 3.5 %all-to-all-start.1 = ((bf16[16,64,128]{2,1,0:T(8,128)(2,1)}), bf16[16,64,128]{2,1,0:T(8,128)(2,1)S(1)}, u32[]{:S(2)}, u32[]{:S(2)}) async-start(bf16[16,64,128]{2,1,0:T(8,128)(2,1)} %shard_map.348), calls=%async_computation.1 | async-start | bytes 524288 | tf_op jit(solution)/shard_map/all_to_all | solution.py:732
  55.3 2.8 %fusion.28.gate_hbm.gate_pre = f32[128,1024]{1,0:T(8,128)} fusion(bf16[128,1024]{1,0:T(8,128)(2,1)S(1)} %fusion.12.refs_0_.normed, bf16[1024,1024]{1,0:T(8,128)(2,1)} %param.26), kind=kOutput, calls=%fused_computation.76 | convolution fusion | flops 268435456 | bytes 2883584 | tf_op jit(solution)/shard_map/dot_general | solution.py:736
  58.2 4.6 %all-to-all-done.1.st.st_hbm = bf16[16,64,128]{2,1,0:T(8,128)(2,1)S(1)} async-done(((bf16[16,64,128]{2,1,0:T(8,128)(2,1)}), bf16[16,64,128]{2,1,0:T(8,128)(2,1)S(1)}, u32[]{:S(2)}, u32[]{:S(2)}) %all-to-all-start.1) | async-done | bytes 262176 | tf_op jit(solution)/shard_map/all_to_all | solution.py:732
  66.4 2.8 %convolution_convert_fusion.1 = bf16[128,1024]{1,0:T(8,128)(2,1)} fusion(bf16[128,1024]{1,0:T(8,128)(2,1)S(1)} %get-tuple-element.108, bf16[1024,1024]{1,0:T(8,128)(2,1)} %param.35), kind=kOutput, calls=%fused_computation.9 | convolution fusion | flops 268566528 | bytes 2621440 | tf_op jit(solution)/shard_map/dot_general | solution.py:736
  79.7 4.7 %shard_map.350 = bf16[16,1088,128]{2,1,0:T(8,128)(2,1)} custom-call(bf16[128,1024]{1,0:T(8,128)(2,1)S(1)} %multiply_convert_fusion.3.refs_0_, bf16[128,1408]{1,0:T(8,128)(2,1)S(1)} %broadcast_select_fusion.1.refs_1_, bf16[128,1408]{1,0:T(8,128)(2,1)S(1)} %multiply_convert_fusion.refs_2_, bf16[128,512]{1,0:T(8,128)(2,1)S(1)} %get-tuple-element.202.refs_3_), custom_call_target="tpu_custom_call" | custom-call | flops 570425344 | bytes 5570560 | tf_op jit(solution)/shard_map/pallas_call | solution.py:36
  84.4 5.2 %collective-permute-start.19 = (bf16[16,1088,128]{2,1,0:T(8,128)(2,1)}, bf16[16,1088,128]{2,1,0:T(8,128)(2,1)S(1)}, u32[]{:S(2)}, u32[]{:S(2)}) collective-permute-start(bf16[16,1088,128]{2,1,0:T(8,128)(2,1)} %shard_map.350), channel_id=1, source_target_pairs={{0,16},{16,0},{32,48},{48,32},{1,17},{17,1},{33,49},{49,33},{2,18}... | collective-permute-start | bytes 13369352 | tf_op jit(solution)/shard_map/ppermute | solution.py:714
  93.6 5.6 %collective-permute-done.2 = bf16[128,1024]{1,0:T(8,128)(2,1)S(1)} collective-permute-done((bf16[128,1024]{1,0:T(8,128)(2,1)S(1)}, bf16[128,1024]{1,0:T(8,128)(2,1)S(1)}, u32[]{:S(2)}, u32[]{:S(2)}) %collective-permute-start.2) | collective-permute-done | bytes 262176 | tf_op jit(solution)/shard_map/ppermute | solution.py:710
  103.1 2.7 %shard_map.360 = bf16[16,512,128]{2,1,0:T(8,128)(2,1)} custom-call(bf16[128,1024]{1,0:T(8,128)(2,1)S(1)} %get-tuple-element.197.refs_0_, bf16[128,1024]{1,0:T(8,128)(2,1)S(1)} %get-tuple-element.195.refs_1_), custom_call_target="tpu_custom_call" | custom-call | flops 268435456 | bytes 2621440 | tf_op jit(solution)/shard_map/pallas_call | solution.py:36
  107.4 4.0 %collective-permute-done.20.refs_7_ = bf16[16,512,128]{2,1,0:T(8,128)(2,1)S(1)} collective-permute-done((bf16[16,512,128]{2,1,0:T(8,128)(2,1)}, bf16[16,512,128]{2,1,0:T(8,128)(2,1)S(1)}, u32[]{:S(2)}, u32[]{:S(2)}) %collective-permute-start.20) | collective-permute-done | bytes 2097184 | tf_op jit(solution)/shard_map/ppermute | solution.py:714
  111.4 6.6 %shard_map.361 = bf16[16,1600,128]{2,1,0:T(8,128)(2,1)} custom-call(bf16[128,1024]{1,0:T(8,128)(2,1)S(1)} %multiply_convert_fusion.3.refs_0_, bf16[128,1408]{1,0:T(8,128)(2,1)S(1)} %get-tuple-element.190.refs_1_, bf16[128,1408]{1,0:T(8,128)(2,1)S(1)} %multiply_convert_fusion.refs_2_, bf16[128,512]{1,0:T(8,128)(2,1)S(1)} %get-tuple-element.201.refs_3_, ...), custom_call_target="tpu_custom_call" | custom-call | flops 838860800 | bytes 14745600 | tf_op jit(solution)/shard_map/pallas_call | solution.py:36
  118.0 12.1 %all_to_all.20.grads = bf16[16,64,128]{2,1,0:T(8,128)(2,1)S(1)} all-to-all(bf16[16,64,128]{2,1,0:T(8,128)(2,1)} %get-tuple-element.113), channel_id=1, replica_groups=mesh['tensor'=2,'dp'=4,'seq'=16] {'seq'}, dimensions={0} | all-to-all | bytes 524288 | tf_op jit(solution)/shard_map/all_to_all | solution.py:732
  130.1 3.7 %shard_map.352 = bf16[16,64,128]{2,1,0:T(8,128)(2,1)} custom-call(bf16[16,64,128]{2,1,0:T(8,128)(2,1)S(1)} %all_to_all.20.grads, bf16[16,192,128]{2,1,0:T(8,128)(2,1)} %all-to-all-done.maps), custom_call_target="tpu_custom_call" | custom-call | bytes 1310720 | tf_op jit(solution)/shard_map/pallas_call | solution.py:36
  133.8 13.3 %all_to_all.21.gt_i = bf16[16,64,128]{2,1,0:T(8,128)(2,1)S(1)} all-to-all(bf16[16,64,128]{2,1,0:T(8,128)(2,1)} %shard_map.352), channel_id=1, replica_groups=mesh['tensor'=2,'dp'=4,'seq'=16] {'seq'}, dimensions={0} | all-to-all | bytes 524288 | tf_op jit(solution)/shard_map/all_to_all | solution.py:732
  147.1 4.9 %shard_map.353 = (f32[128,2048]{1,0:T(8,128)S(1)}, bf16[16,2048]{1,0:T(8,128)(2,1)}, f32[8,2048]{1,0:T(8,128)S(1)}, bf16[128,128]{1,0:T(8,128)(2,1)S(1)}, f32[8,128]{1,0:T(8,128)S(1)}) custom-call(bf16[144,3584]{1,0:T(8,128)(2,1)S(1)} %copy-done.19, f32[136,2048]{1,0:T(8,128)S(1)} %copy-done.14, bf16[128,1024]{1,0:T(8,128)(2,1)S(1)} %copy-done.23, ...), custom_call_target="tpu_custom_call" | custom-call | bytes 4149248 | tf_op jit(solution)/shard_map/pallas_call | solution.py:36
  153.3 5.3 %collective-permute-done.3.after = bf16[16,2048]{1,0:T(8,128)(2,1)S(1)} collective-permute-done((bf16[16,2048]{1,0:T(8,128)(2,1)}, bf16[16,2048]{1,0:T(8,128)(2,1)S(1)}, u32[]{:S(2)}, u32[]{:S(2)}) %collective-permute-start.3) | collective-permute-done | bytes 65568 | tf_op jit(solution)/shard_map/ppermute | solution.py:728
  159.4 2.7 %shard_map.355 = bf16[16,512,128]{2,1,0:T(8,128)(2,1)} custom-call(bf16[128,1024]{1,0:T(8,128)(2,1)S(1)} %fusion.12.refs_0_.normed, bf16[128,1024]{1,0:T(8,128)(2,1)S(1)} %get-tuple-element.199.refs_1_), custom_call_target="tpu_custom_call" | custom-call | flops 268435456 | bytes 2621440 | tf_op jit(solution)/shard_map/pallas_call | solution.py:36
  173.9 4.0 %shard_map.357 = (bf16[4,272,128]{2,1,0:T(8,128)(2,1)}, bf16[4,272,128]{2,1,0:T(8,128)(2,1)}, bf16[4,272,128]{2,1,0:T(8,128)(2,1)}, bf16[4,272,128]{2,1,0:T(8,12...) custom-call(s32[3]{0:T(128)S(1)} %pad_add_fusion.place, ...), custom_call_target="tpu_custom_call" | custom-call | tf_op jit(solution)/shard_map/pallas_call | solution.py:684
  179.0 4.0 %collective-permute-start.6 = (bf16[4,272,128]{2,1,0:T(8,128)(2,1)}, bf16[4,272,128]{2,1,0:T(8,128)(2,1)S(1)}, u32[]{:S(2)}, u32[]{:S(2)}) collective-permute-start(bf16[4,272,128]{2,1,0:T(8,128)(2,1)} %get-tuple-element.124), channel_id=1, source_target_pairs={{0,2},{1,3},{2,0},{3,1},{4,6},{5,7},{6,4},{7,5},{8,10},{9,11},{10,... | collective-permute-start | bytes 835592 | tf_op jit(solution)/shard_map/ppermute | solution.py:988
  183.0 2.6 %collective-permute-done.11.part_in = bf16[128,1024]{1,0:T(8,128)(2,1)S(1)} collective-permute-done((bf16[128,1024]{1,0:T(8,128)(2,1)S(1)}, bf16[128,1024]{1,0:T(8,128)(2,1)S(1)}, u32[]{:S(2)}, u32[]{:S(2)}) %collective-permute-start.11) | collective-permute-done | bytes 262176 | tf_op jit(solution)/shard_map/ppermute | solution.py:710
  190.2 6.9 %collective-permute-done.9.refs_6_ = bf16[4,256,128]{2,1,0:T(8,128)(2,1)S(1)} collective-permute-done((bf16[4,256,128]{2,1,0:T(8,128)(2,1)}, bf16[4,256,128]{2,1,0:T(8,128)(2,1)S(1)}, u32[]{:S(2)}, u32[]{:S(2)}) %collective-permute-start.9) | collective-permute-done | bytes 262176 | tf_op jit(solution)/shard_map/ppermute | solution.py:989
  197.1 6.9 %collective-permute-done.10.refs_7_ = bf16[4,256,128]{2,1,0:T(8,128)(2,1)S(1)} collective-permute-done((bf16[4,256,128]{2,1,0:T(8,128)(2,1)}, bf16[4,256,128]{2,1,0:T(8,128)(2,1)S(1)}, u32[]{:S(2)}, u32[]{:S(2)}) %collective-permute-start.10) | collective-permute-done | bytes 262176 | tf_op jit(solution)/shard_map/ppermute | solution.py:989
  205.4 3.5 %shard_map.359 = (bf16[272,128]{1,0:T(8,128)(2,1)}, bf16[272,128]{1,0:T(8,128)(2,1)}, bf16[272,128]{1,0:T(8,128)(2,1)}, bf16[272,128]{1,0:T(8,128)(2,1)}, bf16[2...) custom-call(s32[3]{0:T(128)} %copy-done.24, ...), custom_call_target="tpu_custom_call" | custom-call | tf_op jit(solution)/shard_map/pallas_call | solution.py:684
  208.9 2.8 %collective-permute-start.21 = (bf16[1600,128]{1,0:T(8,128)(2,1)}, bf16[1600,128]{1,0:T(8,128)(2,1)S(1)}, u32[]{:S(2)}, u32[]{:S(2)}) collective-permute-start(bf16[1600,128]{1,0:T(8,128)(2,1)} %bitcast.75), channel_id=1, source_target_pairs={{0,32},{32,0},{16,48},{48,16},{1,33},{33,1},{17,49},{49,17},{2,34}... | collective-permute-start | bytes 1228808 | tf_op jit(solution)/shard_map/ppermute | solution.py:723
  212.8 2.7 %collective-permute-start.17 = (bf16[256,128]{1,0:T(8,128)(2,1)}, bf16[256,128]{1,0:T(8,128)(2,1)S(1)}, u32[]{:S(2)}, u32[]{:S(2)}) collective-permute-start(bf16[256,128]{1,0:T(8,128)(2,1)} %get-tuple-element.148), channel_id=1, source_target_pairs={{0,2},{1,3},{2,0},{3,1},{4,6},{5,7},{6,4},{7,5},{8,10},{9,11},{10,... | collective-permute-start | bytes 196616 | tf_op jit(solution)/shard_map/ppermute | solution.py:1015
  216.3 3.1 %collective-permute-start.14 = (bf16[272,128]{1,0:T(8,128)(2,1)}, bf16[272,128]{1,0:T(8,128)(2,1)S(1)}, u32[]{:S(2)}, u32[]{:S(2)}) collective-permute-start(bf16[272,128]{1,0:T(8,128)(2,1)} %get-tuple-element.144), channel_id=1, source_target_pairs={{0,8},{1,9},{2,10},{3,11},{4,12},{5,13},{6,14},{7,15},{8,0},{9,1},... | collective-permute-start | bytes 208904 | tf_op jit(solution)/shard_map/ppermute | solution.py:1014
  227.6 4.3 %collective-permute-start.23 = (bf16[1600,128]{1,0:T(8,128)(2,1)S(1)}, bf16[1600,128]{1,0:T(8,128)(2,1)S(1)}, u32[]{:S(2)}, u32[]{:S(2)}) collective-permute-start(bf16[1600,128]{1,0:T(8,128)(2,1)S(1)} %add_convert_fusion.mine), channel_id=1, source_target_pairs={{0,16},{16,0},{32,48},{48,32},{1,17},{17,1},{33,49},{49,33},{2,18}... | collective-permute-start | bytes 1228808 | tf_op jit(solution)/shard_map/ppermute | solution.py:714
  234.7 4.0 %collective-permute-done.22 = bf16[528,128]{1,0:T(8,128)(2,1)S(1)} collective-permute-done((bf16[528,128]{1,0:T(8,128)(2,1)}, bf16[528,128]{1,0:T(8,128)(2,1)S(1)}, u32[]{:S(2)}, u32[]{:S(2)}) %collective-permute-start.22) | collective-permute-done | bytes 135200 | tf_op jit(solution)/shard_map/ppermute | solution.py:723
  (223 shorter events, 72.5 us)
Async XLA Ops:
  7.2 71.5 %copy-start = (bf16[1024,1408]{1,0:T(8,128)(2,1)S(1)}, bf16[1024,1408]{1,0:T(8,128)(2,1)}, u32[]{:S(2)}) copy-start(bf16[1024,1408]{1,0:T(8,128)(2,1)} %param.37) | copy-start | bytes 8650756
  13.7 5.3 %collective-permute-start = (bf16[16,2048]{1,0:T(8,128)(2,1)S(1)}, bf16[16,2048]{1,0:T(8,128)(2,1)S(1)}, u32[]{:S(2)}, u32[]{:S(2)}) collective-permute-start(bf16[16,2048]{1,0:T(8,128)(2,1)S(1)} %slice.45), channel_id=1, source_target_pairs={{0,1},{1,2},{2,3},{3,4},{4,5},{5,6},{6,7},{7,8},{8,9},{9,10},{10,1... | collective-permute-start | bytes 196616 | tf_op jit(solution)/shard_map/ppermute | solution.py:728
  27.4 20.7 %all-to-all-start = ((bf16[16,192,128]{2,1,0:T(8,128)(2,1)}), bf16[16,192,128]{2,1,0:T(8,128)(2,1)}, u32[]{:S(2)}, u32[]{:S(2)}) async-start(bf16[16,192,128]{2,1,0:T(8,128)(2,1)} %get-tuple-element.107), calls=%async_computation | async-start | bytes 1572864 | tf_op jit(solution)/shard_map/all_to_all | solution.py:732
  51.8 11.0 %all-to-all-start.1 = ((bf16[16,64,128]{2,1,0:T(8,128)(2,1)}), bf16[16,64,128]{2,1,0:T(8,128)(2,1)S(1)}, u32[]{:S(2)}, u32[]{:S(2)}) async-start(bf16[16,64,128]{2,1,0:T(8,128)(2,1)} %shard_map.348), calls=%async_computation.1 | async-start | bytes 524288 | tf_op jit(solution)/shard_map/all_to_all | solution.py:732
  55.3 153.6 %reduce-scatter.4.cloned.1.call-start = ((), (), s32[]{:S(2)}) async-start(), calls=%async_computation.5 | async-start | bytes 6963200
  69.3 5.5 %collective-permute-start.1 = (bf16[128,1024]{1,0:T(8,128)(2,1)}, bf16[128,1024]{1,0:T(8,128)(2,1)}, u32[]{:S(2)}, u32[]{:S(2)}) collective-permute-start(bf16[128,1024]{1,0:T(8,128)(2,1)} %convolution_convert_fusion.1), channel_id=1, source_target_pairs={{0,64},{64,0},{1,65},{65,1},{2,66},{66,2},{3,67},{67,3},{4,68},{68... | collective-permute-start | bytes 786440 | tf_op jit(solution)/shard_map/ppermute | solution.py:710
  84.4 27.0 %collective-permute-start.19 = (bf16[16,1088,128]{2,1,0:T(8,128)(2,1)}, bf16[16,1088,128]{2,1,0:T(8,128)(2,1)S(1)}, u32[]{:S(2)}, u32[]{:S(2)}) collective-permute-start(bf16[16,1088,128]{2,1,0:T(8,128)(2,1)} %shard_map.350), channel_id=1, source_target_pairs={{0,16},{16,0},{32,48},{48,32},{1,17},{17,1},{33,49},{49,33},{2,18}... | collective-permute-start | bytes 13369352 | tf_op jit(solution)/shard_map/ppermute | solution.py:714
  91.8 7.4 %collective-permute-start.2 = (bf16[128,1024]{1,0:T(8,128)(2,1)S(1)}, bf16[128,1024]{1,0:T(8,128)(2,1)S(1)}, u32[]{:S(2)}, u32[]{:S(2)}) collective-permute-start(bf16[128,1024]{1,0:T(8,128)(2,1)S(1)} %fusion.5), channel_id=1, source_target_pairs={{0,64},{64,0},{1,65},{65,1},{2,66},{66,2},{3,67},{67,3},{4,68},{68... | collective-permute-start | bytes 786440 | tf_op jit(solution)/shard_map/ppermute | solution.py:710
  105.8 5.6 %collective-permute-start.20 = (bf16[16,512,128]{2,1,0:T(8,128)(2,1)}, bf16[16,512,128]{2,1,0:T(8,128)(2,1)S(1)}, u32[]{:S(2)}, u32[]{:S(2)}) collective-permute-start(bf16[16,512,128]{2,1,0:T(8,128)(2,1)} %shard_map.360), channel_id=1, source_target_pairs={{0,16},{16,0},{32,48},{48,32},{1,17},{17,1},{33,49},{49,33},{2,18}... | collective-permute-start | bytes 6291464 | tf_op jit(solution)/shard_map/ppermute | solution.py:714
  152.0 6.6 %collective-permute-start.3 = (bf16[16,2048]{1,0:T(8,128)(2,1)}, bf16[16,2048]{1,0:T(8,128)(2,1)S(1)}, u32[]{:S(2)}, u32[]{:S(2)}) collective-permute-start(bf16[16,2048]{1,0:T(8,128)(2,1)} %get-tuple-element.116), channel_id=1, source_target_pairs={{1,0},{2,1},{3,2},{4,3},{5,4},{6,5},{7,6},{8,7},{9,8},{10,9},{11,1... | collective-permute-start | bytes 196616 | tf_op jit(solution)/shard_map/ppermute | solution.py:728
  162.1 11.8 %collective-permute-start.4 = (bf16[16,512,128]{2,1,0:T(8,128)(2,1)}, bf16[16,512,128]{2,1,0:T(8,128)(2,1)}, u32[]{:S(2)}, u32[]{:S(2)}) collective-permute-start(bf16[16,512,128]{2,1,0:T(8,128)(2,1)} %shard_map.355), channel_id=1, source_target_pairs={{0,16},{16,0},{32,48},{48,32},{1,17},{17,1},{33,49},{49,33},{2,18}... | collective-permute-start | bytes 6291464 | tf_op jit(solution)/shard_map/ppermute | solution.py:714
  169.8 13.1 %collective-permute-start.12 = (bf16[128,1024]{1,0:T(8,128)(2,1)S(1)}, bf16[128,1024]{1,0:T(8,128)(2,1)S(1)}, u32[]{:S(2)}, u32[]{:S(2)}) collective-permute-start(bf16[128,1024]{1,0:T(8,128)(2,1)S(1)} %convolution_convert_fusion), channel_id=1, source_target_pairs={{0,64},{64,0},{1,65},{65,1},{2,66},{66,2},{3,67},{67,3},{4,68},{68... | collective-permute-start | bytes 786440 | tf_op jit(solution)/shard_map/ppermute | solution.py:710
  178.0 7.6 %collective-permute-start.11 = (bf16[128,1024]{1,0:T(8,128)(2,1)S(1)}, bf16[128,1024]{1,0:T(8,128)(2,1)S(1)}, u32[]{:S(2)}, u32[]{:S(2)}) collective-permute-start(bf16[128,1024]{1,0:T(8,128)(2,1)S(1)} %fusion.4.part), channel_id=1, source_target_pairs={{0,64},{64,0},{1,65},{65,1},{2,66},{66,2},{3,67},{67,3},{4,68},{68... | collective-permute-start | bytes 786440 | tf_op jit(solution)/shard_map/ppermute | solution.py:710
  178.5 8.6 %collective-permute-start.8 = (bf16[4,256,128]{2,1,0:T(8,128)(2,1)}, bf16[4,256,128]{2,1,0:T(8,128)(2,1)S(1)}, u32[]{:S(2)}, u32[]{:S(2)}) collective-permute-start(bf16[4,256,128]{2,1,0:T(8,128)(2,1)} %get-tuple-element.127), channel_id=1, source_target_pairs={{0,4},{1,5},{2,6},{3,7},{4,8},{5,9},{6,10},{7,11},{8,12},{9,13},{1... | collective-permute-start | bytes 786440 | tf_op jit(solution)/shard_map/ppermute | solution.py:989
  178.9 25.0 %collective-permute-start.5 = (bf16[4,272,128]{2,1,0:T(8,128)(2,1)}, bf16[4,272,128]{2,1,0:T(8,128)(2,1)S(1)}, u32[]{:S(2)}, u32[]{:S(2)}) collective-permute-start(bf16[4,272,128]{2,1,0:T(8,128)(2,1)} %get-tuple-element.123), channel_id=1, source_target_pairs={{0,1},{1,2},{2,3},{3,0},{4,5},{5,6},{6,7},{7,4},{8,9},{9,10},{10,1... | collective-permute-start | bytes 835592 | tf_op jit(solution)/shard_map/ppermute | solution.py:988
  179.0 25.0 %collective-permute-start.6 = (bf16[4,272,128]{2,1,0:T(8,128)(2,1)}, bf16[4,272,128]{2,1,0:T(8,128)(2,1)S(1)}, u32[]{:S(2)}, u32[]{:S(2)}) collective-permute-start(bf16[4,272,128]{2,1,0:T(8,128)(2,1)} %get-tuple-element.124), channel_id=1, source_target_pairs={{0,2},{1,3},{2,0},{3,1},{4,6},{5,7},{6,4},{7,5},{8,10},{9,11},{10,... | collective-permute-start | bytes 835592 | tf_op jit(solution)/shard_map/ppermute | solution.py:988
  183.0 21.7 %collective-permute-start.7 = (bf16[4,272,128]{2,1,0:T(8,128)(2,1)}, bf16[4,272,128]{2,1,0:T(8,128)(2,1)}, u32[]{:S(2)}, u32[]{:S(2)}) collective-permute-start(bf16[4,272,128]{2,1,0:T(8,128)(2,1)} %get-tuple-element.125), channel_id=1, source_target_pairs={{0,3},{1,0},{2,1},{3,2},{4,7},{5,4},{6,5},{7,6},{8,11},{9,8},{10,9... | collective-permute-start | bytes 835592 | tf_op jit(solution)/shard_map/ppermute | solution.py:988
  185.6 11.4 %collective-permute-start.9 = (bf16[4,256,128]{2,1,0:T(8,128)(2,1)}, bf16[4,256,128]{2,1,0:T(8,128)(2,1)S(1)}, u32[]{:S(2)}, u32[]{:S(2)}) collective-permute-start(bf16[4,256,128]{2,1,0:T(8,128)(2,1)} %get-tuple-element.128), channel_id=1, source_target_pairs={{0,8},{1,9},{2,10},{3,11},{4,12},{5,13},{6,14},{7,15},{8,0},{9,1},... | collective-permute-start | bytes 786440 | tf_op jit(solution)/shard_map/ppermute | solution.py:989
  187.0 16.9 %collective-permute-start.10 = (bf16[4,256,128]{2,1,0:T(8,128)(2,1)}, bf16[4,256,128]{2,1,0:T(8,128)(2,1)S(1)}, u32[]{:S(2)}, u32[]{:S(2)}) collective-permute-start(bf16[4,256,128]{2,1,0:T(8,128)(2,1)} %get-tuple-element.129), channel_id=1, source_target_pairs={{0,12},{1,13},{2,14},{3,15},{4,0},{5,1},{6,2},{7,3},{8,4},{9,5},{1... | collective-permute-start | bytes 786440 | tf_op jit(solution)/shard_map/ppermute | solution.py:989
  190.2 43.0 %copy-start.25 = (s32[3]{0:T(128)S(1)}, s32[3]{0:T(128)}, u32[]{:S(2)}) copy-start(s32[3]{0:T(128)} %copy-done.24) | copy-start | bytes 40
  208.9 14.3 %collective-permute-start.21 = (bf16[1600,128]{1,0:T(8,128)(2,1)}, bf16[1600,128]{1,0:T(8,128)(2,1)S(1)}, u32[]{:S(2)}, u32[]{:S(2)}) collective-permute-start(bf16[1600,128]{1,0:T(8,128)(2,1)} %bitcast.75), channel_id=1, source_target_pairs={{0,32},{32,0},{16,48},{48,16},{1,33},{33,1},{17,49},{49,17},{2,34}... | collective-permute-start | bytes 1228808 | tf_op jit(solution)/shard_map/ppermute | solution.py:723
  211.7 7.8 %collective-permute-start.16 = (bf16[256,128]{1,0:T(8,128)(2,1)}, bf16[256,128]{1,0:T(8,128)(2,1)S(1)}, u32[]{:S(2)}, u32[]{:S(2)}) collective-permute-start(bf16[256,128]{1,0:T(8,128)(2,1)} %get-tuple-element.147), channel_id=1, source_target_pairs={{0,1},{1,2},{2,3},{3,0},{4,5},{5,6},{6,7},{7,4},{8,9},{9,10},{10,1... | collective-permute-start | bytes 196616 | tf_op jit(solution)/shard_map/ppermute | solution.py:1015
  212.8 7.0 %collective-permute-start.17 = (bf16[256,128]{1,0:T(8,128)(2,1)}, bf16[256,128]{1,0:T(8,128)(2,1)S(1)}, u32[]{:S(2)}, u32[]{:S(2)}) collective-permute-start(bf16[256,128]{1,0:T(8,128)(2,1)} %get-tuple-element.148), channel_id=1, source_target_pairs={{0,2},{1,3},{2,0},{3,1},{4,6},{5,7},{6,4},{7,5},{8,10},{9,11},{10,... | collective-permute-start | bytes 196616 | tf_op jit(solution)/shard_map/ppermute | solution.py:1015
  215.6 7.6 %collective-permute-start.13 = (bf16[272,128]{1,0:T(8,128)(2,1)}, bf16[272,128]{1,0:T(8,128)(2,1)S(1)}, u32[]{:S(2)}, u32[]{:S(2)}) collective-permute-start(bf16[272,128]{1,0:T(8,128)(2,1)} %get-tuple-element.143), channel_id=1, source_target_pairs={{0,4},{1,5},{2,6},{3,7},{4,8},{5,9},{6,10},{7,11},{8,12},{9,13},{1... | collective-permute-start | bytes 208904 | tf_op jit(solution)/shard_map/ppermute | solution.py:1014
  216.3 6.9 %collective-permute-start.14 = (bf16[272,128]{1,0:T(8,128)(2,1)}, bf16[272,128]{1,0:T(8,128)(2,1)S(1)}, u32[]{:S(2)}, u32[]{:S(2)}) collective-permute-start(bf16[272,128]{1,0:T(8,128)(2,1)} %get-tuple-element.144), channel_id=1, source_target_pairs={{0,8},{1,9},{2,10},{3,11},{4,12},{5,13},{6,14},{7,15},{8,0},{9,1},... | collective-permute-start | bytes 208904 | tf_op jit(solution)/shard_map/ppermute | solution.py:1014
  219.5 3.7 %collective-permute-start.15 = (bf16[272,128]{1,0:T(8,128)(2,1)}, bf16[272,128]{1,0:T(8,128)(2,1)S(1)}, u32[]{:S(2)}, u32[]{:S(2)}) collective-permute-start(bf16[272,128]{1,0:T(8,128)(2,1)} %get-tuple-element.145), channel_id=1, source_target_pairs={{0,12},{1,13},{2,14},{3,15},{4,0},{5,1},{6,2},{7,3},{8,4},{9,5},{1... | collective-permute-start | bytes 208904 | tf_op jit(solution)/shard_map/ppermute | solution.py:1014
  219.9 3.3 %collective-permute-start.18 = (bf16[256,128]{1,0:T(8,128)(2,1)}, bf16[256,128]{1,0:T(8,128)(2,1)S(1)}, u32[]{:S(2)}, u32[]{:S(2)}) collective-permute-start(bf16[256,128]{1,0:T(8,128)(2,1)} %get-tuple-element.149), channel_id=1, source_target_pairs={{0,3},{1,0},{2,1},{3,2},{4,7},{5,4},{6,5},{7,6},{8,11},{9,8},{10,9... | collective-permute-start | bytes 196616 | tf_op jit(solution)/shard_map/ppermute | solution.py:1015
  227.6 5.6 %collective-permute-start.23 = (bf16[1600,128]{1,0:T(8,128)(2,1)S(1)}, bf16[1600,128]{1,0:T(8,128)(2,1)S(1)}, u32[]{:S(2)}, u32[]{:S(2)}) collective-permute-start(bf16[1600,128]{1,0:T(8,128)(2,1)S(1)} %add_convert_fusion.mine), channel_id=1, source_target_pairs={{0,16},{16,0},{32,48},{48,32},{1,17},{17,1},{33,49},{49,33},{2,18}... | collective-permute-start | bytes 1228808 | tf_op jit(solution)/shard_map/ppermute | solution.py:714
  231.8 6.9 %collective-permute-start.22 = (bf16[528,128]{1,0:T(8,128)(2,1)}, bf16[528,128]{1,0:T(8,128)(2,1)S(1)}, u32[]{:S(2)}, u32[]{:S(2)}) collective-permute-start(bf16[528,128]{1,0:T(8,128)(2,1)} %shard_map.362), channel_id=1, source_target_pairs={{0,32},{32,0},{16,48},{48,16},{1,33},{33,1},{17,49},{49,17},{2,34}... | collective-permute-start | bytes 405512 | tf_op jit(solution)/shard_map/ppermute | solution.py:723
  238.8 4.0 %collective-permute-start.24 = (bf16[528,128]{1,0:T(8,128)(2,1)S(1)}, bf16[528,128]{1,0:T(8,128)(2,1)S(1)}, u32[]{:S(2)}, u32[]{:S(2)}) collective-permute-start(bf16[528,128]{1,0:T(8,128)(2,1)S(1)} %add_convert_fusion.2.mine), channel_id=1, source_target_pairs={{0,16},{16,0},{32,48},{48,32},{1,17},{17,1},{33,49},{49,33},{2,18}... | collective-permute-start | bytes 405512 | tf_op jit(solution)/shard_map/ppermute | solution.py:714
  239.7 3.1 %collective-permute-start.26 = (bf16[16,128]{1,0:T(8,128)(2,1)S(1)}, bf16[16,128]{1,0:T(8,128)(2,1)S(1)}, u32[]{:S(2)}, u32[]{:S(2)}) collective-permute-start(bf16[16,128]{1,0:T(8,128)(2,1)S(1)} %slice.52), channel_id=1, source_target_pairs={{0,80},{16,64},{32,112},{48,96},{64,16},{80,0},{96,48},{112,32},{1... | collective-permute-start | bytes 12296 | tf_op jit(solution)/shard_map/ppermute | solution.py:719
  240.0 2.8 %collective-permute-start.25 = (bf16[16,128]{1,0:T(8,128)(2,1)S(1)}, bf16[16,128]{1,0:T(8,128)(2,1)S(1)}, u32[]{:S(2)}, u32[]{:S(2)}) collective-permute-start(bf16[16,128]{1,0:T(8,128)(2,1)S(1)} %slice.52), channel_id=1, source_target_pairs={{0,64},{64,0},{1,65},{65,1},{2,66},{66,2},{3,67},{67,3},{4,68},{68... | collective-permute-start | bytes 12296 | tf_op jit(solution)/shard_map/ppermute | solution.py:710
  (58 other events, 425.6 us)
Sparse Core Ops, SparseCore 0:
  118.1 87.9 reduce-scatter.3

commit v3 on v2

--- a/solution.py
+++ b/solution.py
@@ -895,18 +895,14 @@
         ],
         [ffn_in, swap_core(out_sent)],
     )
+    start_grad, early = lax.optimization_barrier((exchange(start_grad), early))
     early = lax.optimization_barrier(
         lax.psum_scatter(early, "seq", scatter_dimension=0, tiled=True)
     )
-    start_grad = exchange(start_grad)
     (end_grads,) = kernel_call(
         scan_back_kernel, [((SEQ, 64, DK), bf16)], start_grad, maps, main=(0,)
     )
     end_grads = exchange(end_grads)
-    end_grads, hidden_last = lax.optimization_barrier((end_grads, hidden_low))
-    feed_part = dot(hidden_last, w_down).astype(bf16)
-    feed_in = swap_tensor(feed_part)
-    output = (middle + (feed_part.astype(f32) + feed_in.astype(f32))).astype(bf16)
     dz, dz_first, filter_grad, logit_low, head_grads = kernel_call(
         back_kernel,
         [
@@ -987,7 +983,10 @@
     )
     moved = [blocks[0]] + [lax.ppermute(blocks[s], "seq", along_x(s)) for s in range(1, 4)]
     moved += [blocks[4]] + [lax.ppermute(blocks[4 + s], "seq", along_z(s)) for s in range(1, 4)]
-    *blocks, part_next = lax.optimization_barrier((*blocks, part))
+    *_, part_next, hidden_last = lax.optimization_barrier((*blocks, part, hidden_low))
+    feed_part = dot(hidden_last, w_down).astype(bf16)
+    feed_in = swap_tensor(feed_part)
+    output = (middle + (feed_part.astype(f32) + feed_in.astype(f32))).astype(bf16)
     part_in = swap_tensor(part_next)
     (grad_inputs,) = kernel_call(
         input_grad_kernel,
@@ -1013,9 +1012,8 @@
     )
     moved = [blocks[0]] + [lax.ppermute(blocks[s], "seq", along_z(s)) for s in range(1, 4)]
     moved += [blocks[4]] + [lax.ppermute(blocks[4 + s], "seq", along_x(s)) for s in range(1, 4)]
-    *_, early = lax.optimization_barrier((*blocks, early.reshape(-1, 128)))
+    *moved, early = lax.optimization_barrier((*moved, early.reshape(-1, 128)))
     early_far = swap_far(early)
-    *moved, early, early_far = lax.optimization_barrier((*moved, early, early_far))
     (late,) = placed_call(
         sum_body,
         [(small_rows + half_rows, 128)],
@@ -1027,8 +1025,7 @@
         + [pltpu.SemaphoreType.DMA((8,))],
         limit=60,
     )
-    late, early, early_far = lax.optimization_barrier((late, early, early_far))
-    late_far = swap_far(late)
+    late_far, early, early_far = lax.optimization_barrier((swap_far(late), early, early_far))
     columns = w_gate.shape[1]
     early = (early.astype(f32) + early_far.astype(f32)).astype(bf16)
     grad_gate, grad_up, grad_down, grad_outgate, grad_wout = placed_call(
@@ -1037,9 +1034,6 @@
         place,
         early,
         swap_core(early),
-    )
-    late_far, grad_gate, grad_up, grad_down, grad_outgate, grad_wout = lax.optimization_barrier(
-        (late_far, grad_gate, grad_up, grad_down, grad_outgate, grad_wout)
     )
     late = (late.astype(f32) + late_far.astype(f32)).astype(bf16)
     small = late[half_rows:small_rows]

time: 252 us -> 248 us (0.984)
  blocking collectives: 25.3 us -> 17.2 us
  Pallas kernels: 52.3 us -> 55.5 us
    all_to_all x2 -> x1, blocking collectives: 25.3 us -> 17.2 us  [exchange(): return lax.all_to_all(value, 'seq', 0, 0, tiled=True)]
    ppermute x5, waiting for transfers between devices: 5.13 us -> 0.55 us  [swap_core(): return lax.ppermute(value, 'dp', [(0, 1), (1, 0), (2, 3), (3, 2)])]
    unnamed x2, waiting for transfers between devices: 0.04 us -> 3.73 us
    all_to_all x2 -> x3, starting transfers between devices: 11.7 us -> 15.3 us  [exchange(): return lax.all_to_all(value, 'seq', 0, 0, tiled=True)]
    ppermute x2, waiting for transfers between devices: 4.01 us -> 7.39 us  [swap_far(): return lax.ppermute(value, 'dp', [(0, 2), (2, 0), (1, 3), (3, 1)])]
    ppermute x5, starting transfers between devices: 14.7 us -> 11.6 us  [swap_core(): return lax.ppermute(value, 'dp', [(0, 1), (1, 0), (2, 3), (3, 2)])]
    pallas_call x13, Pallas kernels: 39.4 us -> 42.4 us  [kernel_call(): pl.pallas_call(body, out_shape=out_shape, in_specs=[pl.BlockSpec(memory_s...]
    ppermute x5, waiting for transfers between devices: 9.55 us -> 6.72 us  [swap_tensor(): return lax.ppermute(value, 'tensor', [(0, 1), (1, 0)])]
  transfers between devices with their start and end apart: 30 -> 31, of which waited for: 15 -> 14; matrix products, arithmetic and copies ran while one was open for 8% -> 8% of each run, Pallas kernels for 11% -> 16%
where the time goes in v3:
time: 248 us; the launch traced here: 247 us
  waiting for transfers between devices  59 us (24%)
  starting transfers between devices  57.3 us (23%)
  Pallas kernels  55.5 us (22%)
  matrix products  23.1 us (9%)
  blocking collectives  17.2 us (7%)
  between operations  15 us (6%)
  other arithmetic  10.8 us (4%)
  local copies, waits for them, and re-layouts  9.33 us (4%)
    pallas_call x13, Pallas kernels, kernel_call(): pl.pallas_call(body, out_shape=out_shape, in_specs=[pl.BlockSpec(memory_s...  42.4 us
    all_to_all x1, blocking collectives, exchange(): return lax.all_to_all(value, 'seq', 0, 0, tiled=True)  17.2 us
    all_to_all x3, waiting for transfers between devices, exchange(): return lax.all_to_all(value, 'seq', 0, 0, tiled=True)  16.5 us
    ppermute x3, waiting for transfers between devices, per_device(): lax.ppermute(blocks[4 + s], 'seq', along_z(s))  15.8 us
    all_to_all x3, starting transfers between devices, exchange(): return lax.all_to_all(value, 'seq', 0, 0, tiled=True)  15.3 us
    dot_general x10, matrix products, dot(): return jnp.dot(a, b, preferred_element_type=f32)  13.5 us
    pallas_call x5, Pallas kernels, placed_call(): pl.pallas_call(body, out_shape=[kind(shape, bf16) for shape in outs], in_...  13.1 us
    ppermute x5, starting transfers between devices, swap_core(): return lax.ppermute(value, 'dp', [(0, 1), (1, 0), (2, 3), (3, 2)])  11.6 us
  transfers between devices with their start and end apart: 31, of which 14 were waited for; matrix products, arithmetic and copies ran while one was open for 8% of the time, Pallas kernels for 16%

profile of v3, /device:TPU:1, one launch (start us, length us, event | category | flops | bytes accessed | tf_op | source)
XLA Modules:
  0.0 247.2 jit_solution(13524675444718439497)
XLA Ops:
  14.1 3.9 %collective-permute-start = (bf16[16,2048]{1,0:T(8,128)(2,1)S(1)}, bf16[16,2048]{1,0:T(8,128)(2,1)S(1)}, u32[]{:S(2)}, u32[]{:S(2)}) collective-permute-start(bf16[16,2048]{1,0:T(8,128)(2,1)S(1)} %slice.45), channel_id=1, source_target_pairs={{0,1},{1,2},{2,3},{3,4},{4,5},{5,6},{6,7},{7,8},{8,9},{9,10},{10,1... | collective-permute-start | bytes 196616 | tf_op jit(solution)/shard_map/ppermute | solution.py:728
  20.4 6.4 %shard_map.347 = (bf16[144,3584]{1,0:T(8,128)(2,1)}, f32[136,2048]{1,0:T(8,128)}, f32[128,1536]{1,0:T(8,128)S(1)}, bf16[16,192,128]{2,1,0:T(8,128)(2,1)}) custom-call(bf16[128,2048]{1,0:T(8,128)(2,1)S(1)} %copy-done.13, bf16[16,2048]{1,0:T(8,128)(2,1)S(1)} %collective-permute-done.halo, f32[8,2048]{1,0:T(8,128)S(1)} %pad_convert_fusion.filt, ...), custom_call_target="tpu_custom_call" | custom-call | bytes 4505600 | tf_op jit(solution)/shard_map/pallas_call | solution.py:36
  27.7 8.2 %all-to-all-start = ((bf16[16,192,128]{2,1,0:T(8,128)(2,1)}), bf16[16,192,128]{2,1,0:T(8,128)(2,1)}, u32[]{:S(2)}, u32[]{:S(2)}) async-start(bf16[16,192,128]{2,1,0:T(8,128)(2,1)} %get-tuple-element.100), calls=%async_computation | async-start | bytes 1572864 | tf_op jit(solution)/shard_map/all_to_all | solution.py:732
  36.6 11.8 %all-to-all-done.maps = bf16[16,192,128]{2,1,0:T(8,128)(2,1)} async-done(((bf16[16,192,128]{2,1,0:T(8,128)(2,1)}), bf16[16,192,128]{2,1,0:T(8,128)(2,1)}, u32[]{:S(2)}, u32[]{:S(2)}) %all-to-all-start) | async-done | bytes 786464 | tf_op jit(solution)/shard_map/all_to_all | solution.py:732
  48.4 3.7 %shard_map.348 = bf16[16,64,128]{2,1,0:T(8,128)(2,1)} custom-call(bf16[16,192,128]{2,1,0:T(8,128)(2,1)} %all-to-all-done.maps), custom_call_target="tpu_custom_call" | custom-call | bytes 1048576 | tf_op jit(solution)/shard_map/pallas_call | solution.py:36
  52.1 3.5 %all-to-all-start.1 = ((bf16[16,64,128]{2,1,0:T(8,128)(2,1)}), bf16[16,64,128]{2,1,0:T(8,128)(2,1)S(1)}, u32[]{:S(2)}, u32[]{:S(2)}) async-start(bf16[16,64,128]{2,1,0:T(8,128)(2,1)} %shard_map.348), calls=%async_computation.1 | async-start | bytes 524288 | tf_op jit(solution)/shard_map/all_to_all | solution.py:732
  55.6 2.8 %fusion.28.gate_hbm.gate_pre = f32[128,1024]{1,0:T(8,128)} fusion(bf16[128,1024]{1,0:T(8,128)(2,1)S(1)} %fusion.12.refs_0_.normed, bf16[1024,1024]{1,0:T(8,128)(2,1)} %param.26), kind=kOutput, calls=%fused_computation.76 | convolution fusion | flops 268435456 | bytes 2883584 | tf_op jit(solution)/shard_map/dot_general | solution.py:736
  58.5 4.7 %all-to-all-done.1.st.st_hbm = bf16[16,64,128]{2,1,0:T(8,128)(2,1)S(1)} async-done(((bf16[16,64,128]{2,1,0:T(8,128)(2,1)}), bf16[16,64,128]{2,1,0:T(8,128)(2,1)S(1)}, u32[]{:S(2)}, u32[]{:S(2)}) %all-to-all-start.1) | async-done | bytes 262176 | tf_op jit(solution)/shard_map/all_to_all | solution.py:732
  66.7 2.8 %convolution_convert_fusion.1 = bf16[128,1024]{1,0:T(8,128)(2,1)} fusion(bf16[128,1024]{1,0:T(8,128)(2,1)S(1)} %get-tuple-element.101, bf16[1024,1024]{1,0:T(8,128)(2,1)} %param.35), kind=kOutput, calls=%fused_computation.9 | convolution fusion | flops 268566528 | bytes 2621440 | tf_op jit(solution)/shard_map/dot_general | solution.py:736
  76.5 2.6 %fusion.29 = f32[128,1408]{1,0:T(8,128)S(1)} fusion(bf16[128,1024]{1,0:T(8,128)(2,1)S(1)} %multiply_convert_fusion.3.refs_0_, bf16[1024,1408]{1,0:T(8,128)(2,1)} %param.38), kind=kOutput, calls=%fused_computation.77 | convolution fusion | flops 369098752 | bytes 3866624 | tf_op jit(solution)/shard_map/dot_general | solution.py:736
  80.9 4.7 %shard_map.350 = bf16[16,1088,128]{2,1,0:T(8,128)(2,1)} custom-call(bf16[128,1024]{1,0:T(8,128)(2,1)S(1)} %multiply_convert_fusion.3.refs_0_, bf16[128,1408]{1,0:T(8,128)(2,1)S(1)} %broadcast_select_fusion.1.refs_1_, bf16[128,1408]{1,0:T(8,128)(2,1)S(1)} %multiply_convert_fusion.refs_2_, bf16[128,512]{1,0:T(8,128)(2,1)S(1)} %get-tuple-element.188.refs_3_), custom_call_target="tpu_custom_call" | custom-call | flops 570425344 | bytes 5570560 | tf_op jit(solution)/shard_map/pallas_call | solution.py:36
  85.6 5.3 %collective-permute-start.3 = (bf16[16,1088,128]{2,1,0:T(8,128)(2,1)}, bf16[16,1088,128]{2,1,0:T(8,128)(2,1)}, u32[]{:S(2)}, u32[]{:S(2)}) collective-permute-start(bf16[16,1088,128]{2,1,0:T(8,128)(2,1)} %shard_map.350), channel_id=1, source_target_pairs={{0,16},{16,0},{32,48},{48,32},{1,17},{17,1},{33,49},{49,33},{2,18}... | collective-permute-start | bytes 13369352 | tf_op jit(solution)/shard_map/ppermute | solution.py:714
  94.8 5.6 %collective-permute-done.2 = bf16[128,1024]{1,0:T(8,128)(2,1)S(1)} collective-permute-done((bf16[128,1024]{1,0:T(8,128)(2,1)S(1)}, bf16[128,1024]{1,0:T(8,128)(2,1)S(1)}, u32[]{:S(2)}, u32[]{:S(2)}) %collective-permute-start.2) | collective-permute-done | bytes 262176 | tf_op jit(solution)/shard_map/ppermute | solution.py:710
  104.3 2.7 %shard_map.352 = bf16[16,512,128]{2,1,0:T(8,128)(2,1)} custom-call(bf16[128,1024]{1,0:T(8,128)(2,1)S(1)} %get-tuple-element.185.refs_0_, bf16[128,1024]{1,0:T(8,128)(2,1)S(1)} %get-tuple-element.181.refs_1_), custom_call_target="tpu_custom_call" | custom-call | flops 268435456 | bytes 2621440 | tf_op jit(solution)/shard_map/pallas_call | solution.py:36
  108.6 3.5 %all-to-all-start.2 = ((bf16[16,64,128]{2,1,0:T(8,128)(2,1)}), bf16[16,64,128]{2,1,0:T(8,128)(2,1)S(1)}, u32[]{:S(2)}, u32[]{:S(2)}) async-start(bf16[16,64,128]{2,1,0:T(8,128)(2,1)} %get-tuple-element.106), calls=%async_computation.2 | async-start | bytes 524288 | tf_op jit(solution)/shard_map/all_to_all | solution.py:732
  112.8 9.6 %shard_map.353 = bf16[16,1600,128]{2,1,0:T(8,128)(2,1)} custom-call(bf16[128,1024]{1,0:T(8,128)(2,1)S(1)} %copy-done.8, bf16[128,1408]{1,0:T(8,128)(2,1)S(1)} %copy-done.25, bf16[128,1408]{1,0:T(8,128)(2,1)S(1)} %copy-done.4, bf16[128,512]{1,0:T(8,128)(2,1)S(1)} %copy-done.22, bf16[128,1024]{1,0:T(8,128)(2,1)S(1)} %get-tuple-element.186.refs_4_, ...), custom_call_target="tpu_custom_call" | custom-call | flops 838860800 | bytes 14745600 | tf_op jit(solution)/shard_map/pallas_call | solution.py:36
  122.4 3.8 %shard_map.354 = bf16[16,64,128]{2,1,0:T(8,128)(2,1)} custom-call(bf16[16,64,128]{2,1,0:T(8,128)(2,1)S(1)} %all-to-all-done.2.grads, bf16[16,192,128]{2,1,0:T(8,128)(2,1)} %all-to-all-done.maps), custom_call_target="tpu_custom_call" | custom-call | bytes 1310720 | tf_op jit(solution)/shard_map/pallas_call | solution.py:36
  126.2 17.2 %all_to_all.20.gt_i = bf16[16,64,128]{2,1,0:T(8,128)(2,1)S(1)} all-to-all(bf16[16,64,128]{2,1,0:T(8,128)(2,1)} %shard_map.354), channel_id=1, replica_groups=mesh['tensor'=2,'dp'=4,'seq'=16] {'seq'}, dimensions={0} | all-to-all | bytes 524288 | tf_op jit(solution)/shard_map/all_to_all | solution.py:732
  143.4 4.9 %shard_map.355 = (f32[128,2048]{1,0:T(8,128)S(1)}, bf16[16,2048]{1,0:T(8,128)(2,1)}, f32[8,2048]{1,0:T(8,128)S(1)}, bf16[128,128]{1,0:T(8,128)(2,1)S(1)}, f32[8,128]{1,0:T(8,128)S(1)}) custom-call(bf16[144,3584]{1,0:T(8,128)(2,1)S(1)} %copy-done.21, f32[136,2048]{1,0:T(8,128)S(1)} %copy-done.16, bf16[128,1024]{1,0:T(8,128)(2,1)S(1)} %copy-done.27, ...), custom_call_target="tpu_custom_call" | custom-call | bytes 4149248 | tf_op jit(solution)/shard_map/pallas_call | solution.py:36
  149.7 5.3 %collective-permute-done.5.after = bf16[16,2048]{1,0:T(8,128)(2,1)S(1)} collective-permute-done((bf16[16,2048]{1,0:T(8,128)(2,1)}, bf16[16,2048]{1,0:T(8,128)(2,1)S(1)}, u32[]{:S(2)}, u32[]{:S(2)}) %collective-permute-start.5) | collective-permute-done | bytes 65568 | tf_op jit(solution)/shard_map/ppermute | solution.py:728
  155.8 2.6 %shard_map.357 = bf16[16,512,128]{2,1,0:T(8,128)(2,1)} custom-call(bf16[128,1024]{1,0:T(8,128)(2,1)S(1)} %fusion.12.refs_0_.normed, bf16[128,1024]{1,0:T(8,128)(2,1)S(1)} %get-tuple-element.183.refs_1_), custom_call_target="tpu_custom_call" | custom-call | flops 268435456 | bytes 2621440 | tf_op jit(solution)/shard_map/pallas_call | solution.py:36
  160.0 2.5 %fusion.31 = f32[128,1024]{1,0:T(8,128)S(1)} fusion(bf16[128,1024]{1,0:T(8,128)(2,1)S(1)} %copy-done.20, bf16[1024,1024]{1,0:T(8,128)(2,1)} %param.26), kind=kOutput, calls=%fused_computation.79 | convolution fusion | flops 268435456 | bytes 2883584 | tf_op jit(solution)/shard_map/dot_general | solution.py:740
  165.9 4.2 %shard_map.359 = (bf16[4,272,128]{2,1,0:T(8,128)(2,1)}, bf16[4,272,128]{2,1,0:T(8,128)(2,1)}, bf16[4,272,128]{2,1,0:T(8,128)(2,1)}, bf16[4,272,128]{2,1,0:T(8,12...) custom-call(s32[3]{0:T(128)S(1)} %pad_add_fusion.place, ...), custom_call_target="tpu_custom_call" | custom-call | tf_op jit(solution)/shard_map/pallas_call | solution.py:684
  176.1 7.0 %collective-permute-done.10.refs_5_ = bf16[4,256,128]{2,1,0:T(8,128)(2,1)S(1)} collective-permute-done((bf16[4,256,128]{2,1,0:T(8,128)(2,1)}, bf16[4,256,128]{2,1,0:T(8,128)(2,1)S(1)}, u32[]{:S(2)}, u32[]{:S(2)}) %collective-permute-start.10) | collective-permute-done | bytes 262176 | tf_op jit(solution)/shard_map/ppermute | solution.py:985
  188.4 5.6 %collective-permute-done.11.refs_6_ = bf16[4,256,128]{2,1,0:T(8,128)(2,1)S(1)} collective-permute-done((bf16[4,256,128]{2,1,0:T(8,128)(2,1)S(1)}, bf16[4,256,128]{2,1,0:T(8,128)(2,1)S(1)}, u32[]{:S(2)}, u32[]{:S(2)}) %collective-permute-start.11) | collective-permute-done | bytes 262176 | tf_op jit(solution)/shard_map/ppermute | solution.py:985
  194.0 3.2 %collective-permute-done.12.refs_7_ = bf16[4,256,128]{2,1,0:T(8,128)(2,1)S(1)} collective-permute-done((bf16[4,256,128]{2,1,0:T(8,128)(2,1)S(1)}, bf16[4,256,128]{2,1,0:T(8,128)(2,1)S(1)}, u32[]{:S(2)}, u32[]{:S(2)}) %collective-permute-start.12) | collective-permute-done | bytes 262176 | tf_op jit(solution)/shard_map/ppermute | solution.py:985
  198.6 3.5 %shard_map.361 = (bf16[272,128]{1,0:T(8,128)(2,1)}, bf16[272,128]{1,0:T(8,128)(2,1)}, bf16[272,128]{1,0:T(8,128)(2,1)}, bf16[272,128]{1,0:T(8,128)(2,1)}, bf16[2...) custom-call(s32[3]{0:T(128)} %copy-done.28, ...), custom_call_target="tpu_custom_call" | custom-call | tf_op jit(solution)/shard_map/pallas_call | solution.py:684
  210.0 3.7 %reduce-scatter.4.cloned.1.call-done = bf16[1,1600,128]{2,1,0:T(8,128)(2,1)} async-done(((bf16[16,1600,128]{2,1,0:T(8,128)(2,1)}), bf16[1,1600,128]{2,1,0:T(8,128)(2,1)}) %reduce-scatter.4.cloned.1.call-update) | async-done | bytes 409616
  213.8 2.9 %collective-permute-start.22 = (bf16[1600,128]{1,0:T(8,128)(2,1)}, bf16[1600,128]{1,0:T(8,128)(2,1)S(1)}, u32[]{:S(2)}, u32[]{:S(2)}) collective-permute-start(bf16[1600,128]{1,0:T(8,128)(2,1)} %bitcast.75), channel_id=1, source_target_pairs={{0,32},{32,0},{16,48},{48,16},{1,33},{33,1},{17,49},{49,17},{2,34}... | collective-permute-start | bytes 1228808 | tf_op jit(solution)/shard_map/ppermute | solution.py:723
  216.8 2.5 %shard_map.362 = bf16[528,128]{1,0:T(8,128)(2,1)} custom-call(s32[3]{0:T(128)} %copy-done.28, bf16[272,128]{1,0:T(8,128)(2,1)} %get-tuple-element.144.refs_0_, bf16[272,128]{1,0:T(8,128)(2,1)} %copy-done.49, bf16[272,128]{1,0:T(8,128)(2,1)} %copy-done.50, bf16[272,128]{1,0:T(8,128)(2,1)} %copy-done.51, bf16[256,128]{1,0:T(8,128)(2,1)} %get-tuple-element.148.refs_4_, ...), custom_call_target="tpu_custom_call" | custom-call | tf_op jit(solution)/shard_map/pallas_call | solution.py:684
  219.9 7.4 %collective-permute-done.21 = bf16[528,128]{1,0:T(8,128)(2,1)S(1)} collective-permute-done((bf16[528,128]{1,0:T(8,128)(2,1)}, bf16[528,128]{1,0:T(8,128)(2,1)S(1)}, u32[]{:S(2)}, u32[]{:S(2)}) %collective-permute-start.21) | collective-permute-done | bytes 135200 | tf_op jit(solution)/shard_map/ppermute | solution.py:723
  228.4 3.1 %collective-permute-start.26 = (bf16[1600,128]{1,0:T(8,128)(2,1)S(1)}, bf16[1600,128]{1,0:T(8,128)(2,1)S(1)}, u32[]{:S(2)}, u32[]{:S(2)}) collective-permute-start(bf16[1600,128]{1,0:T(8,128)(2,1)S(1)} %add_convert_fusion.mine), channel_id=1, source_target_pairs={{0,16},{16,0},{32,48},{48,32},{1,17},{17,1},{33,49},{49,33},{2,18}... | collective-permute-start | bytes 1228808 | tf_op jit(solution)/shard_map/ppermute | solution.py:714
  (242 shorter events, 70.7 us)
Async XLA Ops:
  7.2 71.9 %copy-start = (bf16[1024,1408]{1,0:T(8,128)(2,1)S(1)}, bf16[1024,1408]{1,0:T(8,128)(2,1)}, u32[]{:S(2)}) copy-start(bf16[1024,1408]{1,0:T(8,128)(2,1)} %param.37) | copy-start | bytes 8650756
  14.1 5.3 %collective-permute-start = (bf16[16,2048]{1,0:T(8,128)(2,1)S(1)}, bf16[16,2048]{1,0:T(8,128)(2,1)S(1)}, u32[]{:S(2)}, u32[]{:S(2)}) collective-permute-start(bf16[16,2048]{1,0:T(8,128)(2,1)S(1)} %slice.45), channel_id=1, source_target_pairs={{0,1},{1,2},{2,3},{3,4},{4,5},{5,6},{6,7},{7,8},{8,9},{9,10},{10,1... | collective-permute-start | bytes 196616 | tf_op jit(solution)/shard_map/ppermute | solution.py:728
  27.7 20.7 %all-to-all-start = ((bf16[16,192,128]{2,1,0:T(8,128)(2,1)}), bf16[16,192,128]{2,1,0:T(8,128)(2,1)}, u32[]{:S(2)}, u32[]{:S(2)}) async-start(bf16[16,192,128]{2,1,0:T(8,128)(2,1)} %get-tuple-element.100), calls=%async_computation | async-start | bytes 1572864 | tf_op jit(solution)/shard_map/all_to_all | solution.py:732
  52.1 11.0 %all-to-all-start.1 = ((bf16[16,64,128]{2,1,0:T(8,128)(2,1)}), bf16[16,64,128]{2,1,0:T(8,128)(2,1)S(1)}, u32[]{:S(2)}, u32[]{:S(2)}) async-start(bf16[16,64,128]{2,1,0:T(8,128)(2,1)} %shard_map.348), calls=%async_computation.1 | async-start | bytes 524288 | tf_op jit(solution)/shard_map/all_to_all | solution.py:732
  69.6 5.5 %collective-permute-start.1 = (bf16[128,1024]{1,0:T(8,128)(2,1)}, bf16[128,1024]{1,0:T(8,128)(2,1)}, u32[]{:S(2)}, u32[]{:S(2)}) collective-permute-start(bf16[128,1024]{1,0:T(8,128)(2,1)} %convolution_convert_fusion.1), channel_id=1, source_target_pairs={{0,64},{64,0},{1,65},{65,1},{2,66},{66,2},{3,67},{67,3},{4,68},{68... | collective-permute-start | bytes 786440 | tf_op jit(solution)/shard_map/ppermute | solution.py:710
  85.6 27.2 %collective-permute-start.3 = (bf16[16,1088,128]{2,1,0:T(8,128)(2,1)}, bf16[16,1088,128]{2,1,0:T(8,128)(2,1)}, u32[]{:S(2)}, u32[]{:S(2)}) collective-permute-start(bf16[16,1088,128]{2,1,0:T(8,128)(2,1)} %shard_map.350), channel_id=1, source_target_pairs={{0,16},{16,0},{32,48},{48,32},{1,17},{17,1},{33,49},{49,33},{2,18}... | collective-permute-start | bytes 13369352 | tf_op jit(solution)/shard_map/ppermute | solution.py:714
  93.0 7.4 %collective-permute-start.2 = (bf16[128,1024]{1,0:T(8,128)(2,1)S(1)}, bf16[128,1024]{1,0:T(8,128)(2,1)S(1)}, u32[]{:S(2)}, u32[]{:S(2)}) collective-permute-start(bf16[128,1024]{1,0:T(8,128)(2,1)S(1)} %fusion.5), channel_id=1, source_target_pairs={{0,64},{64,0},{1,65},{65,1},{2,66},{66,2},{3,67},{67,3},{4,68},{68... | collective-permute-start | bytes 786440 | tf_op jit(solution)/shard_map/ppermute | solution.py:710
  107.0 5.7 %collective-permute-start.4 = (bf16[16,512,128]{2,1,0:T(8,128)(2,1)}, bf16[16,512,128]{2,1,0:T(8,128)(2,1)}, u32[]{:S(2)}, u32[]{:S(2)}) collective-permute-start(bf16[16,512,128]{2,1,0:T(8,128)(2,1)} %shard_map.352), channel_id=1, source_target_pairs={{0,16},{16,0},{32,48},{48,32},{1,17},{17,1},{33,49},{49,33},{2,18}... | collective-permute-start | bytes 6291464 | tf_op jit(solution)/shard_map/ppermute | solution.py:714
  108.6 13.7 %all-to-all-start.2 = ((bf16[16,64,128]{2,1,0:T(8,128)(2,1)}), bf16[16,64,128]{2,1,0:T(8,128)(2,1)S(1)}, u32[]{:S(2)}, u32[]{:S(2)}) async-start(bf16[16,64,128]{2,1,0:T(8,128)(2,1)} %get-tuple-element.106), calls=%async_computation.2 | async-start | bytes 524288 | tf_op jit(solution)/shard_map/all_to_all | solution.py:732
  112.2 101.5 %reduce-scatter.4.cloned.1.call-start = ((), (), s32[]{:S(2)}) async-start(), calls=%async_computation.5 | async-start | bytes 6963200
  148.4 6.6 %collective-permute-start.5 = (bf16[16,2048]{1,0:T(8,128)(2,1)}, bf16[16,2048]{1,0:T(8,128)(2,1)S(1)}, u32[]{:S(2)}, u32[]{:S(2)}) collective-permute-start(bf16[16,2048]{1,0:T(8,128)(2,1)} %get-tuple-element.110), channel_id=1, source_target_pairs={{1,0},{2,1},{3,2},{4,3},{5,4},{6,5},{7,6},{8,7},{9,8},{10,9},{11,1... | collective-permute-start | bytes 196616 | tf_op jit(solution)/shard_map/ppermute | solution.py:728
  158.5 7.5 %collective-permute-start.6 = (bf16[16,512,128]{2,1,0:T(8,128)(2,1)}, bf16[16,512,128]{2,1,0:T(8,128)(2,1)}, u32[]{:S(2)}, u32[]{:S(2)}) collective-permute-start(bf16[16,512,128]{2,1,0:T(8,128)(2,1)} %shard_map.357), channel_id=1, source_target_pairs={{0,16},{16,0},{32,48},{48,32},{1,17},{17,1},{33,49},{49,33},{2,18}... | collective-permute-start | bytes 6291464 | tf_op jit(solution)/shard_map/ppermute | solution.py:714
  170.2 13.0 %collective-permute-start.10 = (bf16[4,256,128]{2,1,0:T(8,128)(2,1)}, bf16[4,256,128]{2,1,0:T(8,128)(2,1)S(1)}, u32[]{:S(2)}, u32[]{:S(2)}) collective-permute-start(bf16[4,256,128]{2,1,0:T(8,128)(2,1)} %get-tuple-element.120), channel_id=1, source_target_pairs={{0,4},{1,5},{2,6},{3,7},{4,8},{5,9},{6,10},{7,11},{8,12},{9,13},{1... | collective-permute-start | bytes 786440 | tf_op jit(solution)/shard_map/ppermute | solution.py:985
  170.3 15.1 %collective-permute-start.13 = (bf16[128,1024]{1,0:T(8,128)(2,1)S(1)}, bf16[128,1024]{1,0:T(8,128)(2,1)S(1)}, u32[]{:S(2)}, u32[]{:S(2)}) collective-permute-start(bf16[128,1024]{1,0:T(8,128)(2,1)S(1)} %fusion.4.part), channel_id=1, source_target_pairs={{0,64},{64,0},{1,65},{65,1},{2,66},{66,2},{3,67},{67,3},{4,68},{68... | collective-permute-start | bytes 786440 | tf_op jit(solution)/shard_map/ppermute | solution.py:710
  172.2 13.7 %collective-permute-start.14 = (bf16[128,1024]{1,0:T(8,128)(2,1)S(1)}, bf16[128,1024]{1,0:T(8,128)(2,1)S(1)}, u32[]{:S(2)}, u32[]{:S(2)}) collective-permute-start(bf16[128,1024]{1,0:T(8,128)(2,1)S(1)} %convolution_convert_fusion), channel_id=1, source_target_pairs={{0,64},{64,0},{1,65},{65,1},{2,66},{66,2},{3,67},{67,3},{4,68},{68... | collective-permute-start | bytes 786440 | tf_op jit(solution)/shard_map/ppermute | solution.py:710
  172.5 24.7 %collective-permute-start.7 = (bf16[4,272,128]{2,1,0:T(8,128)(2,1)S(1)}, bf16[4,272,128]{2,1,0:T(8,128)(2,1)S(1)}, u32[]{:S(2)}, u32[]{:S(2)}) collective-permute-start(bf16[4,272,128]{2,1,0:T(8,128)(2,1)S(1)} %copy-done.64), channel_id=1, source_target_pairs={{0,1},{1,2},{2,3},{3,0},{4,5},{5,6},{6,7},{7,4},{8,9},{9,10},{10,1... | collective-permute-start | bytes 835592 | tf_op jit(solution)/shard_map/ppermute | solution.py:984
  173.7 23.5 %collective-permute-start.8 = (bf16[4,272,128]{2,1,0:T(8,128)(2,1)S(1)}, bf16[4,272,128]{2,1,0:T(8,128)(2,1)S(1)}, u32[]{:S(2)}, u32[]{:S(2)}) collective-permute-start(bf16[4,272,128]{2,1,0:T(8,128)(2,1)S(1)} %copy-done.63), channel_id=1, source_target_pairs={{0,2},{1,3},{2,0},{3,1},{4,6},{5,7},{6,4},{7,5},{8,10},{9,11},{10,... | collective-permute-start | bytes 835592 | tf_op jit(solution)/shard_map/ppermute | solution.py:984
  183.1 14.8 %collective-permute-start.9 = (bf16[4,272,128]{2,1,0:T(8,128)(2,1)S(1)}, bf16[4,272,128]{2,1,0:T(8,128)(2,1)}, u32[]{:S(2)}, u32[]{:S(2)}) collective-permute-start(bf16[4,272,128]{2,1,0:T(8,128)(2,1)S(1)} %copy-done.62), channel_id=1, source_target_pairs={{0,3},{1,0},{2,1},{3,2},{4,7},{5,4},{6,5},{7,6},{8,11},{9,8},{10,9... | collective-permute-start | bytes 835592 | tf_op jit(solution)/shard_map/ppermute | solution.py:984
  185.4 8.6 %collective-permute-start.11 = (bf16[4,256,128]{2,1,0:T(8,128)(2,1)S(1)}, bf16[4,256,128]{2,1,0:T(8,128)(2,1)S(1)}, u32[]{:S(2)}, u32[]{:S(2)}) collective-permute-start(bf16[4,256,128]{2,1,0:T(8,128)(2,1)S(1)} %copy-done.66), channel_id=1, source_target_pairs={{0,8},{1,9},{2,10},{3,11},{4,12},{5,13},{6,14},{7,15},{8,0},{9,1},... | collective-permute-start | bytes 786440 | tf_op jit(solution)/shard_map/ppermute | solution.py:985
  185.9 11.3 %collective-permute-start.12 = (bf16[4,256,128]{2,1,0:T(8,128)(2,1)S(1)}, bf16[4,256,128]{2,1,0:T(8,128)(2,1)S(1)}, u32[]{:S(2)}, u32[]{:S(2)}) collective-permute-start(bf16[4,256,128]{2,1,0:T(8,128)(2,1)S(1)} %copy-done.65), channel_id=1, source_target_pairs={{0,12},{1,13},{2,14},{3,15},{4,0},{5,1},{6,2},{7,3},{8,4},{9,5},{1... | collective-permute-start | bytes 786440 | tf_op jit(solution)/shard_map/ppermute | solution.py:985
  202.2 6.6 %collective-permute-start.18 = (bf16[256,128]{1,0:T(8,128)(2,1)}, bf16[256,128]{1,0:T(8,128)(2,1)S(1)}, u32[]{:S(2)}, u32[]{:S(2)}) collective-permute-start(bf16[256,128]{1,0:T(8,128)(2,1)} %get-tuple-element.140), channel_id=1, source_target_pairs={{0,1},{1,2},{2,3},{3,0},{4,5},{5,6},{6,7},{7,4},{8,9},{9,10},{10,1... | collective-permute-start | bytes 196616 | tf_op jit(solution)/shard_map/ppermute | solution.py:1014
  202.3 11.5 %collective-permute-start.15 = (bf16[272,128]{1,0:T(8,128)(2,1)}, bf16[272,128]{1,0:T(8,128)(2,1)S(1)}, u32[]{:S(2)}, u32[]{:S(2)}) collective-permute-start(bf16[272,128]{1,0:T(8,128)(2,1)} %get-tuple-element.136), channel_id=1, source_target_pairs={{0,4},{1,5},{2,6},{3,7},{4,8},{5,9},{6,10},{7,11},{8,12},{9,13},{1... | collective-permute-start | bytes 208904 | tf_op jit(solution)/shard_map/ppermute | solution.py:1013
  204.7 9.1 %collective-permute-start.16 = (bf16[272,128]{1,0:T(8,128)(2,1)}, bf16[272,128]{1,0:T(8,128)(2,1)S(1)}, u32[]{:S(2)}, u32[]{:S(2)}) collective-permute-start(bf16[272,128]{1,0:T(8,128)(2,1)} %get-tuple-element.137), channel_id=1, source_target_pairs={{0,8},{1,9},{2,10},{3,11},{4,12},{5,13},{6,14},{7,15},{8,0},{9,1},... | collective-permute-start | bytes 208904 | tf_op jit(solution)/shard_map/ppermute | solution.py:1013
  206.8 7.0 %collective-permute-start.17 = (bf16[272,128]{1,0:T(8,128)(2,1)}, bf16[272,128]{1,0:T(8,128)(2,1)S(1)}, u32[]{:S(2)}, u32[]{:S(2)}) collective-permute-start(bf16[272,128]{1,0:T(8,128)(2,1)} %get-tuple-element.138), channel_id=1, source_target_pairs={{0,12},{1,13},{2,14},{3,15},{4,0},{5,1},{6,2},{7,3},{8,4},{9,5},{1... | collective-permute-start | bytes 208904 | tf_op jit(solution)/shard_map/ppermute | solution.py:1013
  207.1 6.6 %collective-permute-start.19 = (bf16[256,128]{1,0:T(8,128)(2,1)}, bf16[256,128]{1,0:T(8,128)(2,1)S(1)}, u32[]{:S(2)}, u32[]{:S(2)}) collective-permute-start(bf16[256,128]{1,0:T(8,128)(2,1)} %get-tuple-element.141), channel_id=1, source_target_pairs={{0,2},{1,3},{2,0},{3,1},{4,6},{5,7},{6,4},{7,5},{8,10},{9,11},{10,... | collective-permute-start | bytes 196616 | tf_op jit(solution)/shard_map/ppermute | solution.py:1014
  208.8 4.9 %collective-permute-start.20 = (bf16[256,128]{1,0:T(8,128)(2,1)}, bf16[256,128]{1,0:T(8,128)(2,1)S(1)}, u32[]{:S(2)}, u32[]{:S(2)}) collective-permute-start(bf16[256,128]{1,0:T(8,128)(2,1)} %get-tuple-element.142), channel_id=1, source_target_pairs={{0,3},{1,0},{2,1},{3,2},{4,7},{5,4},{6,5},{7,6},{8,11},{9,8},{10,9... | collective-permute-start | bytes 196616 | tf_op jit(solution)/shard_map/ppermute | solution.py:1014
  213.8 13.5 %collective-permute-start.22 = (bf16[1600,128]{1,0:T(8,128)(2,1)}, bf16[1600,128]{1,0:T(8,128)(2,1)S(1)}, u32[]{:S(2)}, u32[]{:S(2)}) collective-permute-start(bf16[1600,128]{1,0:T(8,128)(2,1)} %bitcast.75), channel_id=1, source_target_pairs={{0,32},{32,0},{16,48},{48,16},{1,33},{33,1},{17,49},{49,17},{2,34}... | collective-permute-start | bytes 1228808 | tf_op jit(solution)/shard_map/ppermute | solution.py:723
  219.3 8.0 %collective-permute-start.21 = (bf16[528,128]{1,0:T(8,128)(2,1)}, bf16[528,128]{1,0:T(8,128)(2,1)S(1)}, u32[]{:S(2)}, u32[]{:S(2)}) collective-permute-start(bf16[528,128]{1,0:T(8,128)(2,1)} %shard_map.362), channel_id=1, source_target_pairs={{0,32},{32,0},{16,48},{48,16},{1,33},{33,1},{17,49},{49,17},{2,34}... | collective-permute-start | bytes 405512 | tf_op jit(solution)/shard_map/ppermute | solution.py:723
  228.4 10.5 %collective-permute-start.26 = (bf16[1600,128]{1,0:T(8,128)(2,1)S(1)}, bf16[1600,128]{1,0:T(8,128)(2,1)S(1)}, u32[]{:S(2)}, u32[]{:S(2)}) collective-permute-start(bf16[1600,128]{1,0:T(8,128)(2,1)S(1)} %add_convert_fusion.mine), channel_id=1, source_target_pairs={{0,16},{16,0},{32,48},{48,32},{1,17},{17,1},{33,49},{49,33},{2,18}... | collective-permute-start | bytes 1228808 | tf_op jit(solution)/shard_map/ppermute | solution.py:714
  232.5 5.0 %collective-permute-start.23 = (bf16[528,128]{1,0:T(8,128)(2,1)S(1)}, bf16[528,128]{1,0:T(8,128)(2,1)S(1)}, u32[]{:S(2)}, u32[]{:S(2)}) collective-permute-start(bf16[528,128]{1,0:T(8,128)(2,1)S(1)} %add_convert_fusion.2.mine), channel_id=1, source_target_pairs={{0,16},{16,0},{32,48},{48,32},{1,17},{17,1},{33,49},{49,33},{2,18}... | collective-permute-start | bytes 405512 | tf_op jit(solution)/shard_map/ppermute | solution.py:714
  232.6 2.5 %collective-permute-start.24 = (bf16[16,128]{1,0:T(8,128)(2,1)S(1)}, bf16[16,128]{1,0:T(8,128)(2,1)S(1)}, u32[]{:S(2)}, u32[]{:S(2)}) collective-permute-start(bf16[16,128]{1,0:T(8,128)(2,1)S(1)} %slice.52), channel_id=1, source_target_pairs={{0,64},{64,0},{1,65},{65,1},{2,66},{66,2},{3,67},{67,3},{4,68},{68... | collective-permute-start | bytes 12296 | tf_op jit(solution)/shard_map/ppermute | solution.py:710
  234.2 3.4 %collective-permute-start.25 = (bf16[16,128]{1,0:T(8,128)(2,1)S(1)}, bf16[16,128]{1,0:T(8,128)(2,1)S(1)}, u32[]{:S(2)}, u32[]{:S(2)}) collective-permute-start(bf16[16,128]{1,0:T(8,128)(2,1)S(1)} %slice.52), channel_id=1, source_target_pairs={{0,80},{16,64},{32,112},{48,96},{64,16},{80,0},{96,48},{112,32},{1... | collective-permute-start | bytes 12296 | tf_op jit(solution)/shard_map/ppermute | solution.py:719
  (68 other events, 494.0 us)
Sparse Core Ops, SparseCore 0:
  122.5 91.1 reduce-scatter.3

commit v4 on v3

--- a/solution.py
+++ b/solution.py
@@ -638,11 +638,16 @@
         out[:, column : column + 128] = block.astype(bf16)[0:rows]
 
 
-def unpack_early_body(place, mine, other, gate_o, up_o, down_o, outgate_o, wout_o):
+def unpack_body(place, mine, other, over_tensor, over_both, *outs):
+    unpack_early(place, mine, other, VW // 2 + 16, *outs[:5])
+    unpack_late(place, mine, other, over_tensor, over_both, *outs[5:])
+
+
+def unpack_early(place, mine, other, at, gate_o, up_o, down_o, outgate_o, wout_o):
     put = functools.partial(fill, place[2] == 0, mine, other)
-    put(gate_o, 0, 0)
-    put(up_o, 1, 0)
-    at = gate_o.shape[1] // 128 * 64
+    put(gate_o, 0, at)
+    put(up_o, 1, at)
+    at += gate_o.shape[1] // 128 * 64
     tiles = down_o.shape[1] // 256
     put(down_o, 0, at, 88, 96, tiles)
     put(down_o, 1, at, 88, 96, tiles, tiles)
@@ -651,7 +656,7 @@
     put(wout_o, 1, at)
 
 
-def unpack_late_body(
+def unpack_late(
     place, mine, other, over_tensor, over_both, query_o, key_o, value_o, mix_o, ffn_o, gain_o,
     log_o, bias_o, beta_o, decay_o, taps_q_o, taps_k_o, taps_v_o,
 ):
@@ -928,11 +933,14 @@
         far=(0, 1, 2, 3),
         main=(1,),
     )
+    dz_after, gate_part = lax.optimization_barrier(
+        (shift(dz_first, -1), dot_t(gate_pre_low, w_outgate))
+    )
     (pre_low,) = kernel_call(
         conv_back_kernel,
         [((TOK, PRE), bf16)],
         dz,
-        shift(dz_first, -1),
+        dz_after,
         filt,
         scratch=[pltpu.VMEM((TOK + HALO, PRE), f32)],
     )
@@ -940,7 +948,7 @@
         dot_t(pre_low[:, :QK], w_query)
         + dot_t(pre_low[:, QK : 2 * QK], w_key)
         + dot_t(pre_low[:, 2 * QK :], w_value)
-        + dot_t(gate_pre_low, w_outgate)
+        + gate_part
         + dot_t(logit_low[:, :HEADS], w_beta)
         + dot_t(logit_low[:, HEADS : 2 * HEADS], w_decay)
     ).astype(bf16)
@@ -1027,19 +1035,18 @@
     )
     late_far, early, early_far = lax.optimization_barrier((swap_far(late), early, early_far))
     columns = w_gate.shape[1]
-    early = (early.astype(f32) + early_far.astype(f32)).astype(bf16)
-    grad_gate, grad_up, grad_down, grad_outgate, grad_wout = placed_call(
-        unpack_early_body,
-        [(64, columns), (64, columns), (88, width), (64, VW), (64, width)],
-        place,
-        early,
-        swap_core(early),
-    )
-    late = (late.astype(f32) + late_far.astype(f32)).astype(bf16)
-    small = late[half_rows:small_rows]
+    mine = jnp.concatenate(
+        [late.astype(f32) + late_far.astype(f32), early.astype(f32) + early_far.astype(f32)], axis=0
+    ).astype(bf16)
+    small = mine[half_rows:small_rows]
     shares = placed_call(
-        unpack_late_body,
+        unpack_body,
         [
+            (64, columns),
+            (64, columns),
+            (88, width),
+            (64, VW),
+            (64, width),
             (64, QK),
             (64, QK),
             (64, VW),
@@ -1055,11 +1062,13 @@
             (4, 64),
         ],
         place,
-        late,
-        swap_core(late),
+        mine,
+        swap_core(mine),
         swap_tensor(small),
         swap_both(small),
     )
+    grad_gate, grad_up, grad_down, grad_outgate, grad_wout = shares[:5]
+    shares = shares[5:]
     grad_query, grad_key, grad_value = shares[:3]
     mix, ffn, gain, log, bias, beta, decay, taps_q, taps_k, taps_v = shares[3:]
     return (

time: 248 us -> 248 us (level)
  waiting for transfers between devices: 59 us -> 56.3 us
    unnamed x2, waiting for transfers between devices: 3.73 us -> 0.02 us
    ppermute x3, waiting for transfers between devices: 0.02 us -> 3.39 us  [per_device(): lax.ppermute(blocks[4 + s], 'seq', along_x(s))]
    unnamed x138 -> x142, local copies, waits for them, and re-layouts: 9.1 us -> 10.9 us
    pallas_call x5 -> x4, Pallas kernels: 13.1 us -> 11.9 us  [placed_call(): pl.pallas_call(body, out_shape=[kind(shape, bf16) for shape in outs], in_...]
    ppermute x5 -> x4, starting transfers between devices: 11.6 us -> 12.7 us  [swap_core(): return lax.ppermute(value, 'dp', [(0, 1), (1, 0), (2, 3), (3, 2)])]
  transfers between devices with their start and end apart: 31 -> 30, of which waited for: 14 -> 16; matrix products, arithmetic and copies ran while one was open for 8% -> 7% of each run, Pallas kernels for 16% -> 15%
where the time goes in v4:
time: 248 us; the launch traced here: 246 us
  starting transfers between devices  57.7 us (23%)
  waiting for transfers between devices  56.3 us (23%)
  Pallas kernels  54.4 us (22%)
  matrix products  23.6 us (10%)
  blocking collectives  17.2 us (7%)
  between operations  15.1 us (6%)
  local copies, waits for them, and re-layouts  11.1 us (4%)
  other arithmetic  10.9 us (4%)
    pallas_call x13, Pallas kernels, kernel_call(): pl.pallas_call(body, out_shape=out_shape, in_specs=[pl.BlockSpec(memory_s...  42.4 us
    all_to_all x1, blocking collectives, exchange(): return lax.all_to_all(value, 'seq', 0, 0, tiled=True)  17.2 us
    all_to_all x3, waiting for transfers between devices, exchange(): return lax.all_to_all(value, 'seq', 0, 0, tiled=True)  16.5 us
    ppermute x3, waiting for transfers between devices, per_device(): lax.ppermute(blocks[4 + s], 'seq', along_z(s))  15.4 us
    all_to_all x3, starting transfers between devices, exchange(): return lax.all_to_all(value, 'seq', 0, 0, tiled=True)  15.3 us
    dot_general x10, matrix products, dot(): return jnp.dot(a, b, preferred_element_type=f32)  13.5 us
    ppermute x4, starting transfers between devices, swap_core(): return lax.ppermute(value, 'dp', [(0, 1), (1, 0), (2, 3), (3, 2)])  12.7 us
    pallas_call x4, Pallas kernels, placed_call(): pl.pallas_call(body, out_shape=[kind(shape, bf16) for shape in outs], in_...  11.9 us
  transfers between devices with their start and end apart: 30, of which 16 were waited for; matrix products, arithmetic and copies ran while one was open for 7% of the time, Pallas kernels for 15%

profile of v4, /device:TPU:1, one launch (start us, length us, event | category | flops | bytes accessed | tf_op | source)
XLA Modules:
  0.0 246.4 jit_solution(118924634234803918)
XLA Ops:
  14.1 3.9 %collective-permute-start = (bf16[16,2048]{1,0:T(8,128)(2,1)S(1)}, bf16[16,2048]{1,0:T(8,128)(2,1)S(1)}, u32[]{:S(2)}, u32[]{:S(2)}) collective-permute-start(bf16[16,2048]{1,0:T(8,128)(2,1)S(1)} %slice.46), channel_id=1, source_target_pairs={{0,1},{1,2},{2,3},{3,4},{4,5},{5,6},{6,7},{7,8},{8,9},{9,10},{10,1... | collective-permute-start | bytes 196616 | tf_op jit(solution)/shard_map/ppermute | solution.py:733
  20.4 6.4 %shard_map.347 = (bf16[144,3584]{1,0:T(8,128)(2,1)}, f32[136,2048]{1,0:T(8,128)}, f32[128,1536]{1,0:T(8,128)S(1)}, bf16[16,192,128]{2,1,0:T(8,128)(2,1)}) custom-call(bf16[128,2048]{1,0:T(8,128)(2,1)S(1)} %copy-done.13, bf16[16,2048]{1,0:T(8,128)(2,1)S(1)} %collective-permute-done.halo, f32[8,2048]{1,0:T(8,128)S(1)} %pad_convert_fusion.filt, ...), custom_call_target="tpu_custom_call" | custom-call | bytes 4505600 | tf_op jit(solution)/shard_map/pallas_call | solution.py:36
  27.7 8.2 %all-to-all-start = ((bf16[16,192,128]{2,1,0:T(8,128)(2,1)}), bf16[16,192,128]{2,1,0:T(8,128)(2,1)}, u32[]{:S(2)}, u32[]{:S(2)}) async-start(bf16[16,192,128]{2,1,0:T(8,128)(2,1)} %get-tuple-element.102), calls=%async_computation | async-start | bytes 1572864 | tf_op jit(solution)/shard_map/all_to_all | solution.py:737
  36.6 11.8 %all-to-all-done.maps = bf16[16,192,128]{2,1,0:T(8,128)(2,1)} async-done(((bf16[16,192,128]{2,1,0:T(8,128)(2,1)}), bf16[16,192,128]{2,1,0:T(8,128)(2,1)}, u32[]{:S(2)}, u32[]{:S(2)}) %all-to-all-start) | async-done | bytes 786464 | tf_op jit(solution)/shard_map/all_to_all | solution.py:737
  48.4 3.7 %shard_map.348 = bf16[16,64,128]{2,1,0:T(8,128)(2,1)} custom-call(bf16[16,192,128]{2,1,0:T(8,128)(2,1)} %all-to-all-done.maps), custom_call_target="tpu_custom_call" | custom-call | bytes 1048576 | tf_op jit(solution)/shard_map/pallas_call | solution.py:36
  52.1 3.5 %all-to-all-start.1 = ((bf16[16,64,128]{2,1,0:T(8,128)(2,1)}), bf16[16,64,128]{2,1,0:T(8,128)(2,1)S(1)}, u32[]{:S(2)}, u32[]{:S(2)}) async-start(bf16[16,64,128]{2,1,0:T(8,128)(2,1)} %shard_map.348), calls=%async_computation.1 | async-start | bytes 524288 | tf_op jit(solution)/shard_map/all_to_all | solution.py:737
  55.7 2.8 %fusion.26.gate_hbm.gate_pre = f32[128,1024]{1,0:T(8,128)} fusion(bf16[128,1024]{1,0:T(8,128)(2,1)S(1)} %fusion.8.refs_0_.normed, bf16[1024,1024]{1,0:T(8,128)(2,1)} %param.26), kind=kOutput, calls=%fused_computation.74 | convolution fusion | flops 268435456 | bytes 2883584 | tf_op jit(solution)/shard_map/dot_general | solution.py:741
  58.5 4.7 %all-to-all-done.1.st.st_hbm = bf16[16,64,128]{2,1,0:T(8,128)(2,1)S(1)} async-done(((bf16[16,64,128]{2,1,0:T(8,128)(2,1)}), bf16[16,64,128]{2,1,0:T(8,128)(2,1)S(1)}, u32[]{:S(2)}, u32[]{:S(2)}) %all-to-all-start.1) | async-done | bytes 262176 | tf_op jit(solution)/shard_map/all_to_all | solution.py:737
  66.8 2.9 %convolution_convert_fusion.1 = bf16[128,1024]{1,0:T(8,128)(2,1)} fusion(bf16[128,1024]{1,0:T(8,128)(2,1)S(1)} %get-tuple-element.103, bf16[1024,1024]{1,0:T(8,128)(2,1)} %param.35), kind=kOutput, calls=%fused_computation.5 | convolution fusion | flops 268566528 | bytes 2621440 | tf_op jit(solution)/shard_map/dot_general | solution.py:741
  76.6 2.6 %fusion.27 = f32[128,1408]{1,0:T(8,128)S(1)} fusion(bf16[128,1024]{1,0:T(8,128)(2,1)S(1)} %multiply_convert_fusion.3.refs_0_, bf16[1024,1408]{1,0:T(8,128)(2,1)} %param.38), kind=kOutput, calls=%fused_computation.75 | convolution fusion | flops 369098752 | bytes 3866624 | tf_op jit(solution)/shard_map/dot_general | solution.py:741
  80.9 4.7 %shard_map.350 = bf16[16,1088,128]{2,1,0:T(8,128)(2,1)} custom-call(bf16[128,1024]{1,0:T(8,128)(2,1)S(1)} %multiply_convert_fusion.3.refs_0_, bf16[128,1408]{1,0:T(8,128)(2,1)S(1)} %broadcast_select_fusion.1.refs_1_, bf16[128,1408]{1,0:T(8,128)(2,1)S(1)} %multiply_convert_fusion.refs_2_, bf16[128,512]{1,0:T(8,128)(2,1)S(1)} %get-tuple-element.192.refs_3_), custom_call_target="tpu_custom_call" | custom-call | flops 570425344 | bytes 5570560 | tf_op jit(solution)/shard_map/pallas_call | solution.py:36
  85.6 5.2 %collective-permute-start.3 = (bf16[16,1088,128]{2,1,0:T(8,128)(2,1)}, bf16[16,1088,128]{2,1,0:T(8,128)(2,1)}, u32[]{:S(2)}, u32[]{:S(2)}) collective-permute-start(bf16[16,1088,128]{2,1,0:T(8,128)(2,1)} %shard_map.350), channel_id=1, source_target_pairs={{0,16},{16,0},{32,48},{48,32},{1,17},{17,1},{33,49},{49,33},{2,18}... | collective-permute-start | bytes 13369352 | tf_op jit(solution)/shard_map/ppermute | solution.py:719
  94.7 5.6 %collective-permute-done.2 = bf16[128,1024]{1,0:T(8,128)(2,1)S(1)} collective-permute-done((bf16[128,1024]{1,0:T(8,128)(2,1)S(1)}, bf16[128,1024]{1,0:T(8,128)(2,1)S(1)}, u32[]{:S(2)}, u32[]{:S(2)}) %collective-permute-start.2) | collective-permute-done | bytes 262176 | tf_op jit(solution)/shard_map/ppermute | solution.py:715
  104.3 2.7 %shard_map.352 = bf16[16,512,128]{2,1,0:T(8,128)(2,1)} custom-call(bf16[128,1024]{1,0:T(8,128)(2,1)S(1)} %get-tuple-element.189.refs_0_, bf16[128,1024]{1,0:T(8,128)(2,1)S(1)} %get-tuple-element.185.refs_1_), custom_call_target="tpu_custom_call" | custom-call | flops 268435456 | bytes 2621440 | tf_op jit(solution)/shard_map/pallas_call | solution.py:36
  108.6 3.5 %all-to-all-start.2 = ((bf16[16,64,128]{2,1,0:T(8,128)(2,1)}), bf16[16,64,128]{2,1,0:T(8,128)(2,1)S(1)}, u32[]{:S(2)}, u32[]{:S(2)}) async-start(bf16[16,64,128]{2,1,0:T(8,128)(2,1)} %get-tuple-element.108), calls=%async_computation.2 | async-start | bytes 524288 | tf_op jit(solution)/shard_map/all_to_all | solution.py:737
  112.8 9.6 %shard_map.353 = bf16[16,1600,128]{2,1,0:T(8,128)(2,1)} custom-call(bf16[128,1024]{1,0:T(8,128)(2,1)S(1)} %copy-done.8, bf16[128,1408]{1,0:T(8,128)(2,1)S(1)} %copy-done.25, bf16[128,1408]{1,0:T(8,128)(2,1)S(1)} %copy-done.4, bf16[128,512]{1,0:T(8,128)(2,1)S(1)} %copy-done.22, bf16[128,1024]{1,0:T(8,128)(2,1)S(1)} %get-tuple-element.190.refs_4_, ...), custom_call_target="tpu_custom_call" | custom-call | flops 838860800 | bytes 14745600 | tf_op jit(solution)/shard_map/pallas_call | solution.py:36
  122.4 3.8 %shard_map.354 = bf16[16,64,128]{2,1,0:T(8,128)(2,1)} custom-call(bf16[16,64,128]{2,1,0:T(8,128)(2,1)S(1)} %all-to-all-done.2.grads, bf16[16,192,128]{2,1,0:T(8,128)(2,1)} %all-to-all-done.maps), custom_call_target="tpu_custom_call" | custom-call | bytes 1310720 | tf_op jit(solution)/shard_map/pallas_call | solution.py:36
  126.2 17.2 %all_to_all.20.gt_i = bf16[16,64,128]{2,1,0:T(8,128)(2,1)S(1)} all-to-all(bf16[16,64,128]{2,1,0:T(8,128)(2,1)} %shard_map.354), channel_id=1, replica_groups=mesh['tensor'=2,'dp'=4,'seq'=16] {'seq'}, dimensions={0} | all-to-all | bytes 524288 | tf_op jit(solution)/shard_map/all_to_all | solution.py:737
  145.6 4.9 %shard_map.355 = (f32[128,2048]{1,0:T(8,128)S(1)}, bf16[16,2048]{1,0:T(8,128)(2,1)}, f32[8,2048]{1,0:T(8,128)S(1)}, bf16[128,128]{1,0:T(8,128)(2,1)S(1)}, f32[8,128]{1,0:T(8,128)S(1)}) custom-call(bf16[144,3584]{1,0:T(8,128)(2,1)S(1)} %copy-done.21, f32[136,2048]{1,0:T(8,128)S(1)} %copy-done.16, bf16[128,1024]{1,0:T(8,128)(2,1)S(1)} %copy-done.27, ...), custom_call_target="tpu_custom_call" | custom-call | bytes 4149248 | tf_op jit(solution)/shard_map/pallas_call | solution.py:36
  153.5 3.9 %collective-permute-done.5.after = bf16[16,2048]{1,0:T(8,128)(2,1)S(1)} collective-permute-done((bf16[16,2048]{1,0:T(8,128)(2,1)}, bf16[16,2048]{1,0:T(8,128)(2,1)S(1)}, u32[]{:S(2)}, u32[]{:S(2)}) %collective-permute-start.5) | collective-permute-done | bytes 65568 | tf_op jit(solution)/shard_map/ppermute | solution.py:733
  158.2 2.6 %shard_map.357 = bf16[16,512,128]{2,1,0:T(8,128)(2,1)} custom-call(bf16[128,1024]{1,0:T(8,128)(2,1)S(1)} %fusion.8.refs_0_.normed, bf16[128,1024]{1,0:T(8,128)(2,1)S(1)} %get-tuple-element.187.refs_1_), custom_call_target="tpu_custom_call" | custom-call | flops 268435456 | bytes 2621440 | tf_op jit(solution)/shard_map/pallas_call | solution.py:36
  166.9 4.2 %shard_map.359 = (bf16[4,272,128]{2,1,0:T(8,128)(2,1)}, bf16[4,272,128]{2,1,0:T(8,128)(2,1)}, bf16[4,272,128]{2,1,0:T(8,128)(2,1)}, bf16[4,272,128]{2,1,0:T(8,12...) custom-call(s32[3]{0:T(128)S(1)} %pad_add_fusion.place, ...), custom_call_target="tpu_custom_call" | custom-call | tf_op jit(solution)/shard_map/pallas_call | solution.py:689
  173.9 2.8 %collective-permute-start.8 = (bf16[4,272,128]{2,1,0:T(8,128)(2,1)S(1)}, bf16[4,272,128]{2,1,0:T(8,128)(2,1)S(1)}, u32[]{:S(2)}, u32[]{:S(2)}) collective-permute-start(bf16[4,272,128]{2,1,0:T(8,128)(2,1)S(1)} %copy-done.65), channel_id=1, source_target_pairs={{0,2},{1,3},{2,0},{3,1},{4,6},{5,7},{6,4},{7,5},{8,10},{9,11},{10,... | collective-permute-start | bytes 835592 | tf_op jit(solution)/shard_map/ppermute | solution.py:992
  176.6 6.4 %collective-permute-done.10.refs_5_ = bf16[4,256,128]{2,1,0:T(8,128)(2,1)S(1)} collective-permute-done((bf16[4,256,128]{2,1,0:T(8,128)(2,1)}, bf16[4,256,128]{2,1,0:T(8,128)(2,1)S(1)}, u32[]{:S(2)}, u32[]{:S(2)}) %collective-permute-start.10) | collective-permute-done | bytes 262176 | tf_op jit(solution)/shard_map/ppermute | solution.py:993
  189.0 4.1 %collective-permute-done.11.refs_6_ = bf16[4,256,128]{2,1,0:T(8,128)(2,1)S(1)} collective-permute-done((bf16[4,256,128]{2,1,0:T(8,128)(2,1)S(1)}, bf16[4,256,128]{2,1,0:T(8,128)(2,1)S(1)}, u32[]{:S(2)}, u32[]{:S(2)}) %collective-permute-start.11) | collective-permute-done | bytes 262176 | tf_op jit(solution)/shard_map/ppermute | solution.py:993
  193.2 5.0 %collective-permute-done.12.refs_7_ = bf16[4,256,128]{2,1,0:T(8,128)(2,1)S(1)} collective-permute-done((bf16[4,256,128]{2,1,0:T(8,128)(2,1)S(1)}, bf16[4,256,128]{2,1,0:T(8,128)(2,1)S(1)}, u32[]{:S(2)}, u32[]{:S(2)}) %collective-permute-start.12) | collective-permute-done | bytes 262176 | tf_op jit(solution)/shard_map/ppermute | solution.py:993
  199.8 3.3 %shard_map.361 = (bf16[272,128]{1,0:T(8,128)(2,1)}, bf16[272,128]{1,0:T(8,128)(2,1)}, bf16[272,128]{1,0:T(8,128)(2,1)}, bf16[272,128]{1,0:T(8,128)(2,1)}, bf16[2...) custom-call(s32[3]{0:T(128)} %copy-done.28, ...), custom_call_target="tpu_custom_call" | custom-call | tf_op jit(solution)/shard_map/pallas_call | solution.py:689
  204.5 3.5 %collective-permute-start.16 = (bf16[272,128]{1,0:T(8,128)(2,1)}, bf16[272,128]{1,0:T(8,128)(2,1)S(1)}, u32[]{:S(2)}, u32[]{:S(2)}) collective-permute-start(bf16[272,128]{1,0:T(8,128)(2,1)} %get-tuple-element.141), channel_id=1, source_target_pairs={{0,8},{1,9},{2,10},{3,11},{4,12},{5,13},{6,14},{7,15},{8,0},{9,1},... | collective-permute-start | bytes 208904 | tf_op jit(solution)/shard_map/ppermute | solution.py:1021
  213.8 2.5 %collective-permute-start.22 = (bf16[1600,128]{1,0:T(8,128)(2,1)}, bf16[1600,128]{1,0:T(8,128)(2,1)S(1)}, u32[]{:S(2)}, u32[]{:S(2)}) collective-permute-start(bf16[1600,128]{1,0:T(8,128)(2,1)} %bitcast.75), channel_id=1, source_target_pairs={{0,32},{32,0},{16,48},{48,16},{1,33},{33,1},{17,49},{49,17},{2,34}... | collective-permute-start | bytes 1228808 | tf_op jit(solution)/shard_map/ppermute | solution.py:728
  216.4 2.7 %shard_map.362 = bf16[528,128]{1,0:T(8,128)(2,1)} custom-call(s32[3]{0:T(128)} %copy-done.28, bf16[272,128]{1,0:T(8,128)(2,1)} %get-tuple-element.148.refs_0_, bf16[272,128]{1,0:T(8,128)(2,1)} %copy-done.51, bf16[272,128]{1,0:T(8,128)(2,1)} %copy-done.52, bf16[272,128]{1,0:T(8,128)(2,1)} %copy-done.53, bf16[256,128]{1,0:T(8,128)(2,1)} %get-tuple-element.152.refs_4_, ...), custom_call_target="tpu_custom_call" | custom-call | tf_op jit(solution)/shard_map/pallas_call | solution.py:689
  219.7 6.8 %collective-permute-done.21 = bf16[528,128]{1,0:T(8,128)(2,1)S(1)} collective-permute-done((bf16[528,128]{1,0:T(8,128)(2,1)}, bf16[528,128]{1,0:T(8,128)(2,1)S(1)}, u32[]{:S(2)}, u32[]{:S(2)}) %collective-permute-start.21) | collective-permute-done | bytes 135200 | tf_op jit(solution)/shard_map/ppermute | solution.py:728
  228.7 3.9 %collective-permute-start.23 = (bf16[2128,128]{1,0:T(8,128)(2,1)S(1)}, bf16[2128,128]{1,0:T(8,128)(2,1)S(1)}, u32[]{:S(2)}, u32[]{:S(2)}) collective-permute-start(bf16[2128,128]{1,0:T(8,128)(2,1)S(1)} %pad_maximum_fusion.mine), channel_id=1, source_target_pairs={{0,16},{16,0},{32,48},{48,32},{1,17},{17,1},{33,49},{49,33},{2,18}... | collective-permute-start | bytes 1634312 | tf_op jit(solution)/shard_map/ppermute | solution.py:719
  (244 shorter events, 71.9 us)
Async XLA Ops:
  7.2 72.0 %copy-start = (bf16[1024,1408]{1,0:T(8,128)(2,1)S(1)}, bf16[1024,1408]{1,0:T(8,128)(2,1)}, u32[]{:S(2)}) copy-start(bf16[1024,1408]{1,0:T(8,128)(2,1)} %param.37) | copy-start | bytes 8650756
  14.1 5.3 %collective-permute-start = (bf16[16,2048]{1,0:T(8,128)(2,1)S(1)}, bf16[16,2048]{1,0:T(8,128)(2,1)S(1)}, u32[]{:S(2)}, u32[]{:S(2)}) collective-permute-start(bf16[16,2048]{1,0:T(8,128)(2,1)S(1)} %slice.46), channel_id=1, source_target_pairs={{0,1},{1,2},{2,3},{3,4},{4,5},{5,6},{6,7},{7,8},{8,9},{9,10},{10,1... | collective-permute-start | bytes 196616 | tf_op jit(solution)/shard_map/ppermute | solution.py:733
  27.7 20.7 %all-to-all-start = ((bf16[16,192,128]{2,1,0:T(8,128)(2,1)}), bf16[16,192,128]{2,1,0:T(8,128)(2,1)}, u32[]{:S(2)}, u32[]{:S(2)}) async-start(bf16[16,192,128]{2,1,0:T(8,128)(2,1)} %get-tuple-element.102), calls=%async_computation | async-start | bytes 1572864 | tf_op jit(solution)/shard_map/all_to_all | solution.py:737
  52.1 11.0 %all-to-all-start.1 = ((bf16[16,64,128]{2,1,0:T(8,128)(2,1)}), bf16[16,64,128]{2,1,0:T(8,128)(2,1)S(1)}, u32[]{:S(2)}, u32[]{:S(2)}) async-start(bf16[16,64,128]{2,1,0:T(8,128)(2,1)} %shard_map.348), calls=%async_computation.1 | async-start | bytes 524288 | tf_op jit(solution)/shard_map/all_to_all | solution.py:737
  69.6 5.5 %collective-permute-start.1 = (bf16[128,1024]{1,0:T(8,128)(2,1)}, bf16[128,1024]{1,0:T(8,128)(2,1)}, u32[]{:S(2)}, u32[]{:S(2)}) collective-permute-start(bf16[128,1024]{1,0:T(8,128)(2,1)} %convolution_convert_fusion.1), channel_id=1, source_target_pairs={{0,64},{64,0},{1,65},{65,1},{2,66},{66,2},{3,67},{67,3},{4,68},{68... | collective-permute-start | bytes 786440 | tf_op jit(solution)/shard_map/ppermute | solution.py:715
  85.6 27.1 %collective-permute-start.3 = (bf16[16,1088,128]{2,1,0:T(8,128)(2,1)}, bf16[16,1088,128]{2,1,0:T(8,128)(2,1)}, u32[]{:S(2)}, u32[]{:S(2)}) collective-permute-start(bf16[16,1088,128]{2,1,0:T(8,128)(2,1)} %shard_map.350), channel_id=1, source_target_pairs={{0,16},{16,0},{32,48},{48,32},{1,17},{17,1},{33,49},{49,33},{2,18}... | collective-permute-start | bytes 13369352 | tf_op jit(solution)/shard_map/ppermute | solution.py:719
  93.0 7.4 %collective-permute-start.2 = (bf16[128,1024]{1,0:T(8,128)(2,1)S(1)}, bf16[128,1024]{1,0:T(8,128)(2,1)S(1)}, u32[]{:S(2)}, u32[]{:S(2)}) collective-permute-start(bf16[128,1024]{1,0:T(8,128)(2,1)S(1)} %fusion.1), channel_id=1, source_target_pairs={{0,64},{64,0},{1,65},{65,1},{2,66},{66,2},{3,67},{67,3},{4,68},{68... | collective-permute-start | bytes 786440 | tf_op jit(solution)/shard_map/ppermute | solution.py:715
  107.0 5.8 %collective-permute-start.4 = (bf16[16,512,128]{2,1,0:T(8,128)(2,1)}, bf16[16,512,128]{2,1,0:T(8,128)(2,1)}, u32[]{:S(2)}, u32[]{:S(2)}) collective-permute-start(bf16[16,512,128]{2,1,0:T(8,128)(2,1)} %shard_map.352), channel_id=1, source_target_pairs={{0,16},{16,0},{32,48},{48,32},{1,17},{17,1},{33,49},{49,33},{2,18}... | collective-permute-start | bytes 6291464 | tf_op jit(solution)/shard_map/ppermute | solution.py:719
  108.6 13.7 %all-to-all-start.2 = ((bf16[16,64,128]{2,1,0:T(8,128)(2,1)}), bf16[16,64,128]{2,1,0:T(8,128)(2,1)S(1)}, u32[]{:S(2)}, u32[]{:S(2)}) async-start(bf16[16,64,128]{2,1,0:T(8,128)(2,1)} %get-tuple-element.108), calls=%async_computation.2 | async-start | bytes 524288 | tf_op jit(solution)/shard_map/all_to_all | solution.py:737
  112.1 98.5 %reduce-scatter.4.cloned.1.call-start = ((), (), s32[]{:S(2)}) async-start(), calls=%async_computation.5 | async-start | bytes 6963200
  150.5 6.8 %collective-permute-start.5 = (bf16[16,2048]{1,0:T(8,128)(2,1)}, bf16[16,2048]{1,0:T(8,128)(2,1)S(1)}, u32[]{:S(2)}, u32[]{:S(2)}) collective-permute-start(bf16[16,2048]{1,0:T(8,128)(2,1)} %get-tuple-element.112), channel_id=1, source_target_pairs={{1,0},{2,1},{3,2},{4,3},{5,4},{6,5},{7,6},{8,7},{9,8},{10,9},{11,1... | collective-permute-start | bytes 196616 | tf_op jit(solution)/shard_map/ppermute | solution.py:733
  160.8 6.1 %collective-permute-start.6 = (bf16[16,512,128]{2,1,0:T(8,128)(2,1)}, bf16[16,512,128]{2,1,0:T(8,128)(2,1)}, u32[]{:S(2)}, u32[]{:S(2)}) collective-permute-start(bf16[16,512,128]{2,1,0:T(8,128)(2,1)} %shard_map.357), channel_id=1, source_target_pairs={{0,16},{16,0},{32,48},{48,32},{1,17},{17,1},{33,49},{49,33},{2,18}... | collective-permute-start | bytes 6291464 | tf_op jit(solution)/shard_map/ppermute | solution.py:719
  171.2 11.8 %collective-permute-start.10 = (bf16[4,256,128]{2,1,0:T(8,128)(2,1)}, bf16[4,256,128]{2,1,0:T(8,128)(2,1)S(1)}, u32[]{:S(2)}, u32[]{:S(2)}) collective-permute-start(bf16[4,256,128]{2,1,0:T(8,128)(2,1)} %get-tuple-element.124), channel_id=1, source_target_pairs={{0,4},{1,5},{2,6},{3,7},{4,8},{5,9},{6,10},{7,11},{8,12},{9,13},{1... | collective-permute-start | bytes 786440 | tf_op jit(solution)/shard_map/ppermute | solution.py:993
  171.3 13.4 %collective-permute-start.13 = (bf16[128,1024]{1,0:T(8,128)(2,1)S(1)}, bf16[128,1024]{1,0:T(8,128)(2,1)S(1)}, u32[]{:S(2)}, u32[]{:S(2)}) collective-permute-start(bf16[128,1024]{1,0:T(8,128)(2,1)S(1)} %add_convert_fusion.2.part), channel_id=1, source_target_pairs={{0,64},{64,0},{1,65},{65,1},{2,66},{66,2},{3,67},{67,3},{4,68},{68... | collective-permute-start | bytes 786440 | tf_op jit(solution)/shard_map/ppermute | solution.py:715
  173.3 12.0 %collective-permute-start.14 = (bf16[128,1024]{1,0:T(8,128)(2,1)S(1)}, bf16[128,1024]{1,0:T(8,128)(2,1)S(1)}, u32[]{:S(2)}, u32[]{:S(2)}) collective-permute-start(bf16[128,1024]{1,0:T(8,128)(2,1)S(1)} %convolution_convert_fusion), channel_id=1, source_target_pairs={{0,64},{64,0},{1,65},{65,1},{2,66},{66,2},{3,67},{67,3},{4,68},{68... | collective-permute-start | bytes 786440 | tf_op jit(solution)/shard_map/ppermute | solution.py:715
  173.6 24.6 %collective-permute-start.7 = (bf16[4,272,128]{2,1,0:T(8,128)(2,1)S(1)}, bf16[4,272,128]{2,1,0:T(8,128)(2,1)S(1)}, u32[]{:S(2)}, u32[]{:S(2)}) collective-permute-start(bf16[4,272,128]{2,1,0:T(8,128)(2,1)S(1)} %copy-done.66), channel_id=1, source_target_pairs={{0,1},{1,2},{2,3},{3,0},{4,5},{5,6},{6,7},{7,4},{8,9},{9,10},{10,1... | collective-permute-start | bytes 835592 | tf_op jit(solution)/shard_map/ppermute | solution.py:992
  173.9 24.3 %collective-permute-start.8 = (bf16[4,272,128]{2,1,0:T(8,128)(2,1)S(1)}, bf16[4,272,128]{2,1,0:T(8,128)(2,1)S(1)}, u32[]{:S(2)}, u32[]{:S(2)}) collective-permute-start(bf16[4,272,128]{2,1,0:T(8,128)(2,1)S(1)} %copy-done.65), channel_id=1, source_target_pairs={{0,2},{1,3},{2,0},{3,1},{4,6},{5,7},{6,4},{7,5},{8,10},{9,11},{10,... | collective-permute-start | bytes 835592 | tf_op jit(solution)/shard_map/ppermute | solution.py:992
  183.0 15.2 %collective-permute-start.9 = (bf16[4,272,128]{2,1,0:T(8,128)(2,1)S(1)}, bf16[4,272,128]{2,1,0:T(8,128)(2,1)S(1)}, u32[]{:S(2)}, u32[]{:S(2)}) collective-permute-start(bf16[4,272,128]{2,1,0:T(8,128)(2,1)S(1)} %copy-done.64), channel_id=1, source_target_pairs={{0,3},{1,0},{2,1},{3,2},{4,7},{5,4},{6,5},{7,6},{8,11},{9,8},{10,9... | collective-permute-start | bytes 835592 | tf_op jit(solution)/shard_map/ppermute | solution.py:992
  184.7 8.4 %collective-permute-start.11 = (bf16[4,256,128]{2,1,0:T(8,128)(2,1)S(1)}, bf16[4,256,128]{2,1,0:T(8,128)(2,1)S(1)}, u32[]{:S(2)}, u32[]{:S(2)}) collective-permute-start(bf16[4,256,128]{2,1,0:T(8,128)(2,1)S(1)} %copy-done.68), channel_id=1, source_target_pairs={{0,8},{1,9},{2,10},{3,11},{4,12},{5,13},{6,14},{7,15},{8,0},{9,1},... | collective-permute-start | bytes 786440 | tf_op jit(solution)/shard_map/ppermute | solution.py:993
  185.3 12.8 %collective-permute-start.12 = (bf16[4,256,128]{2,1,0:T(8,128)(2,1)S(1)}, bf16[4,256,128]{2,1,0:T(8,128)(2,1)S(1)}, u32[]{:S(2)}, u32[]{:S(2)}) collective-permute-start(bf16[4,256,128]{2,1,0:T(8,128)(2,1)S(1)} %copy-done.67), channel_id=1, source_target_pairs={{0,12},{1,13},{2,14},{3,15},{4,0},{5,1},{6,2},{7,3},{8,4},{9,5},{1... | collective-permute-start | bytes 786440 | tf_op jit(solution)/shard_map/ppermute | solution.py:993
  203.1 34.8 %copy-start.29 = (s32[3]{0:T(128)S(1)}, s32[3]{0:T(128)}, u32[]{:S(2)}) copy-start(s32[3]{0:T(128)} %copy-done.28) | copy-start | bytes 40
  203.1 6.2 %collective-permute-start.18 = (bf16[256,128]{1,0:T(8,128)(2,1)}, bf16[256,128]{1,0:T(8,128)(2,1)S(1)}, u32[]{:S(2)}, u32[]{:S(2)}) collective-permute-start(bf16[256,128]{1,0:T(8,128)(2,1)} %get-tuple-element.144), channel_id=1, source_target_pairs={{0,1},{1,2},{2,3},{3,0},{4,5},{5,6},{6,7},{7,4},{8,9},{9,10},{10,1... | collective-permute-start | bytes 196616 | tf_op jit(solution)/shard_map/ppermute | solution.py:1022
  203.2 10.5 %collective-permute-start.15 = (bf16[272,128]{1,0:T(8,128)(2,1)}, bf16[272,128]{1,0:T(8,128)(2,1)S(1)}, u32[]{:S(2)}, u32[]{:S(2)}) collective-permute-start(bf16[272,128]{1,0:T(8,128)(2,1)} %get-tuple-element.140), channel_id=1, source_target_pairs={{0,4},{1,5},{2,6},{3,7},{4,8},{5,9},{6,10},{7,11},{8,12},{9,13},{1... | collective-permute-start | bytes 208904 | tf_op jit(solution)/shard_map/ppermute | solution.py:1021
  204.5 9.2 %collective-permute-start.16 = (bf16[272,128]{1,0:T(8,128)(2,1)}, bf16[272,128]{1,0:T(8,128)(2,1)S(1)}, u32[]{:S(2)}, u32[]{:S(2)}) collective-permute-start(bf16[272,128]{1,0:T(8,128)(2,1)} %get-tuple-element.141), channel_id=1, source_target_pairs={{0,8},{1,9},{2,10},{3,11},{4,12},{5,13},{6,14},{7,15},{8,0},{9,1},... | collective-permute-start | bytes 208904 | tf_op jit(solution)/shard_map/ppermute | solution.py:1021
  208.0 5.8 %collective-permute-start.17 = (bf16[272,128]{1,0:T(8,128)(2,1)}, bf16[272,128]{1,0:T(8,128)(2,1)S(1)}, u32[]{:S(2)}, u32[]{:S(2)}) collective-permute-start(bf16[272,128]{1,0:T(8,128)(2,1)} %get-tuple-element.142), channel_id=1, source_target_pairs={{0,12},{1,13},{2,14},{3,15},{4,0},{5,1},{6,2},{7,3},{8,4},{9,5},{1... | collective-permute-start | bytes 208904 | tf_op jit(solution)/shard_map/ppermute | solution.py:1021
  208.0 5.0 %collective-permute-start.19 = (bf16[256,128]{1,0:T(8,128)(2,1)}, bf16[256,128]{1,0:T(8,128)(2,1)S(1)}, u32[]{:S(2)}, u32[]{:S(2)}) collective-permute-start(bf16[256,128]{1,0:T(8,128)(2,1)} %get-tuple-element.145), channel_id=1, source_target_pairs={{0,2},{1,3},{2,0},{3,1},{4,6},{5,7},{6,4},{7,5},{8,10},{9,11},{10,... | collective-permute-start | bytes 196616 | tf_op jit(solution)/shard_map/ppermute | solution.py:1022
  209.3 4.4 %collective-permute-start.20 = (bf16[256,128]{1,0:T(8,128)(2,1)}, bf16[256,128]{1,0:T(8,128)(2,1)S(1)}, u32[]{:S(2)}, u32[]{:S(2)}) collective-permute-start(bf16[256,128]{1,0:T(8,128)(2,1)} %get-tuple-element.146), channel_id=1, source_target_pairs={{0,3},{1,0},{2,1},{3,2},{4,7},{5,4},{6,5},{7,6},{8,11},{9,8},{10,9... | collective-permute-start | bytes 196616 | tf_op jit(solution)/shard_map/ppermute | solution.py:1022
  213.8 12.7 %collective-permute-start.22 = (bf16[1600,128]{1,0:T(8,128)(2,1)}, bf16[1600,128]{1,0:T(8,128)(2,1)S(1)}, u32[]{:S(2)}, u32[]{:S(2)}) collective-permute-start(bf16[1600,128]{1,0:T(8,128)(2,1)} %bitcast.75), channel_id=1, source_target_pairs={{0,32},{32,0},{16,48},{48,16},{1,33},{33,1},{17,49},{49,17},{2,34}... | collective-permute-start | bytes 1228808 | tf_op jit(solution)/shard_map/ppermute | solution.py:728
  219.1 7.4 %collective-permute-start.21 = (bf16[528,128]{1,0:T(8,128)(2,1)}, bf16[528,128]{1,0:T(8,128)(2,1)S(1)}, u32[]{:S(2)}, u32[]{:S(2)}) collective-permute-start(bf16[528,128]{1,0:T(8,128)(2,1)} %shard_map.362), channel_id=1, source_target_pairs={{0,32},{32,0},{16,48},{48,16},{1,33},{33,1},{17,49},{49,17},{2,34}... | collective-permute-start | bytes 405512 | tf_op jit(solution)/shard_map/ppermute | solution.py:728
  228.7 9.2 %collective-permute-start.23 = (bf16[2128,128]{1,0:T(8,128)(2,1)S(1)}, bf16[2128,128]{1,0:T(8,128)(2,1)S(1)}, u32[]{:S(2)}, u32[]{:S(2)}) collective-permute-start(bf16[2128,128]{1,0:T(8,128)(2,1)S(1)} %pad_maximum_fusion.mine), channel_id=1, source_target_pairs={{0,16},{16,0},{32,48},{48,32},{1,17},{17,1},{33,49},{49,33},{2,18}... | collective-permute-start | bytes 1634312 | tf_op jit(solution)/shard_map/ppermute | solution.py:719
  232.6 3.2 %collective-permute-start.24 = (bf16[16,128]{1,0:T(8,128)(2,1)S(1)}, bf16[16,128]{1,0:T(8,128)(2,1)S(1)}, u32[]{:S(2)}, u32[]{:S(2)}) collective-permute-start(bf16[16,128]{1,0:T(8,128)(2,1)S(1)} %slice.53), channel_id=1, source_target_pairs={{0,64},{64,0},{1,65},{65,1},{2,66},{66,2},{3,67},{67,3},{4,68},{68... | collective-permute-start | bytes 12296 | tf_op jit(solution)/shard_map/ppermute | solution.py:715
  234.8 3.0 %collective-permute-start.25 = (bf16[16,128]{1,0:T(8,128)(2,1)S(1)}, bf16[16,128]{1,0:T(8,128)(2,1)S(1)}, u32[]{:S(2)}, u32[]{:S(2)}) collective-permute-start(bf16[16,128]{1,0:T(8,128)(2,1)S(1)} %slice.53), channel_id=1, source_target_pairs={{0,80},{16,64},{32,112},{48,96},{64,16},{80,0},{96,48},{112,32},{1... | collective-permute-start | bytes 12296 | tf_op jit(solution)/shard_map/ppermute | solution.py:724
  (69 other events, 413.5 us)
Sparse Core Ops, SparseCore 0:
  122.5 87.6 reduce-scatter.3
